TPU v7x, 256 devices: a whole 4x4x8 slice. The times are simulated.
256 devices in a mesh: tm: 128 (over z, x_lo, y, core), head: 2 (over x_hi).
Axes of the slice: x: 4 (x_hi: 2, x_lo: 2; x = x_hi * 2 + x_lo), y: 4, z: 8, core: 2. Of those that a mesh axis runs over, the one named last changes fastest.
Arguments:
- inputs: bfloat16 [32768, 1024], P('tm', 'head'), may hold values from -8 to 8
- w_query: bfloat16 [1024, 1024], P(None, 'head'), may hold values from -1 to 1
- w_key: bfloat16 [1024, 1024], P(None, 'head'), may hold values from -1 to 1
- w_value: bfloat16 [1024, 1024], P(None, 'head'), may hold values from -0.1875 to 0.1875
- w_out: bfloat16 [1024, 1024], P('head'), may hold values from -0.1875 to 0.1875
- kernel: float32 [9, 1024], P(None, 'head'), may hold values from -1.2 to 1.6
- cotangent: bfloat16 [32768, 1024], P('tm', 'head'), may hold values from -9 to 9
Outputs:
- output: bfloat16 [32768, 1024], P('tm', 'head')
- grad_inputs: bfloat16 [32768, 1024], P('tm', 'head')
- grad_kernel: float32 [9, 1024], P(None, 'head')
All inputs are finite; a program needn't handle non-finite values.
Results may differ from a plain program's by a relative error of at most 0.008.
Values may be sent and summed in bfloat16 or wider, within the bound.
No kernel may reach another device: no remote copies, remote signals or barrier semaphores. Data moves between devices by JAX's collectives and lax.ppermute only.
A program may use at most 64 MiB of HBM per device.

v0:
```python
import jax
import jax.numpy as jnp
from jax import lax
from jax.sharding import PartitionSpec as P

D = 1024
HEAD_DIM = 128
BLOCK = 128
CONTEXT = 2
KW = 9


EPSILON = 1e-05
MASKED = -1e30


def extended_2(shard, sides, width):
    for axis, dim in sides:
        size, length = (lax.axis_size(axis), shard.shape[dim])
        up = [(i, (i + 1) % size) for i in range(size - 1)]
        down = [(j, i) for i, j in up]
        last = lax.slice_in_dim(shard, length - width, length, axis=dim)
        first = lax.slice_in_dim(shard, 0, width, axis=dim)
        before = lax.ppermute(last, axis, up)
        after = lax.ppermute(first, axis, down)
        shard = jnp.concatenate([before, shard, after], axis=dim)
    return shard


def passed_along(value, axis, steps):
    count = lax.axis_size(axis)
    first, last = (max(0, -steps), min(count, count - steps))
    return lax.ppermute(value, axis, [(source, source + steps) for source in range(first, last)])


def normalize(values):
    center = jnp.mean(values, axis=1)
    spread = jnp.mean(values * values, axis=1) - center * center
    rstd = lax.rsqrt(spread + EPSILON)
    return ((values - center[:, None]) * rstd[:, None], rstd)


def windows(extended, blocks, axis):
    span = (2 * CONTEXT + 1) * BLOCK
    return jnp.stack(
        [
            lax.slice_in_dim(extended, index * BLOCK, index * BLOCK + span, axis=axis)
            for index in range(blocks)
        ]
    )


def blockify(matrix, blocks):
    return matrix.reshape(blocks, -1, matrix.shape[1] // HEAD_DIM, HEAD_DIM)


def local(inputs, w_query, w_key, w_value, w_out, kernel, cotangent):
    rows = inputs.shape[0]
    share = inputs.shape[1]
    blocks = rows // BLOCK
    margin = CONTEXT * BLOCK
    span = (2 * CONTEXT + 1) * BLOCK
    scale = HEAD_DIM ** (-0.5)
    half = KW // 2
    whole = lax.all_gather(inputs, "head", axis=1, tiled=True)
    normed, rstd_one = normalize(whole.astype(jnp.float32))
    normed_b = normed.astype(jnp.bfloat16)
    query = jnp.dot(normed_b, w_query, preferred_element_type=jnp.float32).astype(jnp.bfloat16)
    keys = jnp.dot(normed_b, w_key, preferred_element_type=jnp.float32).astype(jnp.bfloat16)
    values = jnp.dot(normed_b, w_value, preferred_element_type=jnp.float32).astype(jnp.bfloat16)
    pair_ext = extended_2(jnp.stack((keys, values)), (("tm", 1),), margin)
    first = lax.axis_index("tm") * rows - margin
    positions = first + jnp.arange(rows + 2 * margin, dtype=jnp.int32)
    valid = (positions >= 0) & (positions < rows * lax.axis_size("tm"))
    valid_win = windows(valid, blocks, 0)
    key_win = windows(pair_ext[0], blocks, 0).reshape(blocks, span, -1, HEAD_DIM)
    value_win = windows(pair_ext[1], blocks, 0).reshape(blocks, span, -1, HEAD_DIM)
    query_blk = blockify(query, blocks)
    scores = (
        jnp.einsum("bqhe,bkhe->bhqk", query_blk, key_win, preferred_element_type=jnp.float32)
        * scale
    )
    scores = jnp.where(valid_win[:, None, None, :], scores, MASKED)
    top = jnp.max(scores, axis=-1, keepdims=True)
    logsum = top[..., 0] + jnp.log(jnp.sum(jnp.exp(scores - top), axis=-1))
    probs = jnp.exp(scores - logsum[..., None])
    probs_b = probs.astype(jnp.bfloat16)
    attended = (
        jnp.einsum("bhqk,bkhe->bqhe", probs_b, value_win, preferred_element_type=jnp.float32)
        .reshape(rows, share)
        .astype(jnp.bfloat16)
    )
    partial_out = jnp.dot(attended, w_out, preferred_element_type=jnp.float32)
    hidden = inputs.astype(jnp.float32) + lax.psum_scatter(
        partial_out, "head", scatter_dimension=1, tiled=True
    )
    totals = lax.psum((jnp.sum(hidden, axis=1), jnp.sum(hidden * hidden, axis=1)), "head")
    center = totals[0] / D
    rstd_two = lax.rsqrt(totals[1] / D - center * center + EPSILON)
    normed_two = (hidden - center[:, None]) * rstd_two[:, None]
    conv_ext = extended_2(normed_two, (("tm", 0),), half)
    mixed = jnp.zeros_like(hidden)
    for tap in range(KW):
        mixed = mixed + kernel[tap][None, :] * conv_ext[tap : tap + rows]
    gate = jax.nn.sigmoid(mixed)
    output = (hidden + mixed * gate).astype(jnp.bfloat16)
    upstream = cotangent.astype(jnp.float32)
    grad_mixed = upstream * gate * (1.0 + mixed * (1.0 - gate))
    grad_ext = extended_2(grad_mixed, (("tm", 0),), half)
    grad_normed = jnp.zeros_like(hidden)
    for tap in range(KW):
        grad_normed = (
            grad_normed + kernel[tap][None, :] * grad_ext[2 * half - tap : 2 * half - tap + rows]
        )
    kernel_local = jnp.stack(
        [jnp.sum(grad_mixed * conv_ext[tap : tap + rows], axis=0) for tap in range(KW)]
    )
    grad_kernel = lax.psum(kernel_local, "tm")
    sums_two = lax.psum(
        (jnp.sum(grad_normed, axis=1), jnp.sum(grad_normed * normed_two, axis=1)), "head"
    )
    grad_hidden = upstream + rstd_two[:, None] * (
        grad_normed - sums_two[0][:, None] / D - normed_two * sums_two[1][:, None] / D
    )
    grad_whole = lax.all_gather(grad_hidden.astype(jnp.bfloat16), "head", axis=1, tiled=True)
    grad_att = jnp.einsum(
        "rd,fd->rf", grad_whole, w_out, preferred_element_type=jnp.float32
    ).astype(jnp.bfloat16)
    grad_blk = blockify(grad_att, blocks)
    dots = jnp.einsum("bqhe,bkhe->bhqk", grad_blk, value_win, preferred_element_type=jnp.float32)
    delta = jnp.sum(probs * dots, axis=-1)
    dscore = (probs * (dots - delta[..., None]) * scale).astype(jnp.bfloat16)
    grad_query = (
        jnp.einsum("bhqk,bkhe->bqhe", dscore, key_win, preferred_element_type=jnp.float32)
        .reshape(rows, share)
        .astype(jnp.bfloat16)
    )
    grad_k_win = jnp.einsum(
        "bhqk,bqhe->bkhe", dscore, query_blk, preferred_element_type=jnp.float32
    ).reshape(blocks, span, share)
    grad_v_win = jnp.einsum(
        "bhqk,bqhe->bkhe", probs_b, grad_blk, preferred_element_type=jnp.float32
    ).reshape(blocks, span, share)
    extended = jnp.zeros((2, rows + 2 * margin, share), jnp.float32)
    for index in range(blocks):
        extended = extended.at[:, index * BLOCK : index * BLOCK + span].add(
            jnp.stack((grad_k_win[index], grad_v_win[index]))
        )
    owned = extended[:, margin : margin + rows]
    from_right = passed_along(extended[:, :margin], "tm", -1)
    from_left = passed_along(extended[:, rows + margin :], "tm", 1)
    owned = owned.at[:, rows - margin :].add(from_right)
    owned = owned.at[:, :margin].add(from_left)
    grad_key = owned[0].astype(jnp.bfloat16)
    grad_value = owned[1].astype(jnp.bfloat16)
    partial_in = jnp.einsum("rf,df->rd", grad_query, w_query, preferred_element_type=jnp.float32)
    partial_in = partial_in + jnp.einsum(
        "rf,df->rd", grad_key, w_key, preferred_element_type=jnp.float32
    )
    partial_in = partial_in + jnp.einsum(
        "rf,df->rd", grad_value, w_value, preferred_element_type=jnp.float32
    )
    grad_n1 = lax.psum_scatter(partial_in, "head", scatter_dimension=1, tiled=True)
    normed_local = lax.dynamic_slice_in_dim(normed, lax.axis_index("head") * share, share, 1)
    sums_one = lax.psum((jnp.sum(grad_n1, axis=1), jnp.sum(grad_n1 * normed_local, axis=1)), "head")
    grad_inputs = grad_hidden + rstd_one[:, None] * (
        grad_n1 - sums_one[0][:, None] / D - normed_local * sums_one[1][:, None] / D
    )
    return (output, grad_inputs.astype(jnp.bfloat16), grad_kernel)


def solution(mesh):
    placed = (
        P("tm", "head"),
        P(None, "head"),
        P(None, "head"),
        P(None, "head"),
        P("head", None),
        P(None, "head"),
        P("tm", "head"),
    )
    return jax.shard_map(
        local,
        mesh=mesh,
        in_specs=placed,
        out_specs=(P("tm", "head"), P("tm", "head"), P(None, "head")),
        check_vma=False,
    )
```

profile of v0, /device:TPU:128, one launch (start us, length us, event | category | flops | bytes accessed | tf_op | source)
XLA Modules:
  0.0 764.1 jit_solution(1728886588096192742)
XLA Ops:
  7.2 10.6 %all_gather.6 = bf16[256,1024]{1,0:T(8,128)(2,1)S(1)} all-gather(bf16[256,512]{1,0:T(8,128)(2,1)} %param.19), channel_id=1, replica_groups=mesh['tm'=128,'head'=2] {'head'}, dimensions={1}, use_global_device_ids=true | all-gather | bytes 786432 | tf_op jit(solution)/shard_map/all_gather | solution.py:65
  17.8 0.2 convert_reduce_fusion
  18.1 1.8 fusion.20
  19.9 0.5 fusion.21
  20.4 0.8 pad_maximum_fusion.8
  21.2 4.0 collective-permute-start.1
  25.2 1.9 collective-permute-start
  27.2 0.5 convolution_convert_fusion.2
  28.0 4.2 collective-permute-done.1
  32.2 8.0 %collective-permute-done = bf16[2,256,512]{2,1,0:T(8,128)(2,1)} collective-permute-done((bf16[2,256,512]{2,1,0:T(8,128)(2,1)}, bf16[2,256,512]{2,1,0:T(8,128)(2,1)}, u32[]{:S(2)}, u32[]{:S(2)}) %collective-permute-start) | collective-permute-done | bytes 524320 | tf_op jit(solution)/shard_map/ppermute | solution.py:24
  40.2 1.3 pad_maximum_fusion
  41.5 1.4 slice_bitcast_fusion
  43.0 2.2 copy.35
  45.1 2.2 copy.34
  47.6 0.7 fusion.4
  48.4 0.7 exponential_reduce_fusion
  49.1 0.7 copy-done.1
  49.8 0.9 fusion.19
  51.0 1.4 fusion.63
  52.5 25.6 %reduce-scatter.3.cloned.1.call-done = f32[256,512]{1,0:T(8,128)} async-done(((f32[256,1024]{1,0:T(8,128)}), f32[256,512]{1,0:T(8,128)}) %reduce-scatter.3.cloned.1.call-update) | async-done | bytes 524304 | tf_op jit(solution)/shard_map/reduce_scatter | solution.py:94
  78.1 1.2 fusion.66
  79.3 6.4 all-reduce.3
  85.8 1.2 subtract_multiply_fusion
  87.0 1.9 collective-permute-start.2
  88.9 7.9 %collective-permute-start.3 = (f32[4,512]{1,0:T(4,128)S(1)}, f32[4,512]{1,0:T(4,128)S(1)}, u32[]{:S(2)}, u32[]{:S(2)}) collective-permute-start(f32[4,512]{1,0:T(4,128)S(1)} %get-tuple-element.112), channel_id=1, source_target_pairs={{2,0},{4,2},{6,4},{8,6},{10,8},{12,10},{14,12},{16,14},{18,16},{20... | collective-permute-start | bytes 24584 | tf_op jit(solution)/shard_map/ppermute | solution.py:25
  96.8 1.3 collective-permute-done.3
  98.1 1.5 fusion.31
  99.6 7.8 %collective-permute-start.4 = (f32[4,512]{1,0:T(4,128)S(1)}, f32[4,512]{1,0:T(4,128)S(1)}, u32[]{:S(2)}, u32[]{:S(2)}) collective-permute-start(f32[4,512]{1,0:T(4,128)S(1)} %get-tuple-element.109), channel_id=1, source_target_pairs={{2,0},{4,2},{6,4},{8,6},{10,8},{12,10},{14,12},{16,14},{18,16},{20... | collective-permute-start | bytes 24584 | tf_op jit(solution)/shard_map/ppermute | solution.py:25
  107.5 1.9 collective-permute-start.5
  109.4 7.2 collective-permute-done.5
  116.7 1.3 fusion.96
  117.9 1.3 multiply_reduce_fusion.1
  119.2 7.1 all-reduce.2
  126.3 0.7 broadcast_multiply_fusion.1
  127.0 2.0 fusion.95
  128.9 8.9 %all_gather.7 = bf16[256,1024]{1,0:T(8,128)(2,1)S(1)} all-gather(bf16[256,512]{1,0:T(8,128)(2,1)S(1)} %get-tuple-element.95), channel_id=1, replica_groups=mesh['tm'=128,'head'=2] {'head'}, dimensions={1}, use_global_device_ids=true | all-gather | bytes 786432 | tf_op jit(solution)/shard_map/all_gather | solution.py:125
  137.8 0.5 convolution_convert_fusion
  138.3 0.8 reshape.192
  139.0 1.1 copy.31
  140.2 2.0 fusion.29
  142.2 0.2 copy-done.2
  142.4 2.4 convolution_bitcast_fusion
  144.8 11.4 %fusion.11 = f32[2,640,4,128]{1,3,2,0:T(8,128)} fusion(bf16[2,128,4,128]{1,3,2,0:T(8,128)(2,1)S(1)} %copy-done.15, f32[2,4,128,640]{3,2,1,0:T(8,128)} %fusion.29, f32[2,4,128,640]{3,2,1,0:T(8,128)} %copy-done.1, f32[2,4,128]{2,1,0:T(4,128)S(1)} %bitcast.109, pred[2,640]{1,0:T(4,128)(4,1)S(1)} %pad_add_fusion), kind=kOutput, calls=%fused_computation.13 | convolution fusion | flops 174982784 | bytes 8131840 | tf_op jit(solution)/shard_map/bhqk,bqhe->bkhe/dot_general | solution.py:138
  156.2 2.0 fusion.99
  158.3 0.5 copy-done.8
  158.9 0.2 select_maximum_fusion
  159.2 0.9 constant_dynamic-update-slice_fusion
  160.1 1.1 slice.361
  161.2 0.7 copy-done.3
  162.0 1.1 slice.362
  163.1 1.9 collective-permute-start.7
  165.0 7.9 %collective-permute-start.6 = (f32[2,256,512]{1,2,0:T(8,128)}, f32[2,256,512]{1,2,0:T(8,128)}, u32[]{:S(2)}, u32[]{:S(2)}) collective-permute-start(f32[2,256,512]{1,2,0:T(8,128)} %slice.361), channel_id=1, source_target_pairs={{2,0},{4,2},{6,4},{8,6},{10,8},{12,10},{14,12},{16,14},{18,16},{20... | collective-permute-start | bytes 3145736 | tf_op jit(solution)/shard_map/ppermute | solution.py:33
  172.9 11.0 %fusion.22 = bf16[2,128,4,128]{1,3,2,0:T(8,128)(2,1)S(1)} fusion(bf16[2,640,4,128]{3,1,2,0:T(8,128)(2,1)} %copy-done.7, f32[2,4,128,640]{3,2,1,0:T(8,128)} %fusion.29, f32[2,4,128,640]{3,2,1,0:T(8,128)} %copy-done.1, f32[2,4,128]{2,1,0:T(4,128)S(1)} %bitcast.110, pred[2,640]{1,0:T(4,128)(4,1)S(1)} %pad_add_fusion), kind=kOutput, calls=%fused_computation.33 | convolution fusion | flops 175113856 | bytes 6821120 | tf_op jit(solution)/shard_map/bhqk,bkhe->bqhe/dot_general | solution.py:134
  184.1 1.8 fusion.60
  186.0 1.0 copy-done.13
  186.9 2.0 fusion.28
  189.0 0.5 convolution_add_fusion.1
  189.5 1.5 convolution_add_fusion
  191.1 1.2 fusion.25
  192.3 0.9 add_convert_fusion.1
  193.3 554.0 %psum.55 = f32[9,512]{1,0:T(8,128)} all-reduce(f32[9,512]{1,0:T(8,128)S(1)} %stack.95), channel_id=1, replica_groups=mesh['tm'=128,'head'=2] {'tm'}, use_global_device_ids=true, to_apply=%region_28.29 | all-reduce | flops 4608 | bytes 36864 | tf_op jit(solution)/shard_map/psum | solution.py:118
  747.3 1.4 fusion.94
  748.7 6.4 all-reduce.1
  755.1 2.1 add_convert_fusion
  (90 shorter events, 1.5 us)
Async XLA Ops:
  7.2 43.8 %copy-start = (bf16[512,1024]{1,0:T(8,128)(2,1)S(1)}, bf16[512,1024]{1,0:T(8,128)(2,1)}, u32[]{:S(2)}) copy-start(bf16[512,1024]{1,0:T(8,128)(2,1)} %param.23) | copy-start | bytes 3145732
  7.2 70.9 %reduce-scatter.3.cloned.1.call-start = ((), (), s32[]{:S(2)}) async-start(), calls=%async_computation.2 | async-start | bytes 1572864 | tf_op jit(solution)/shard_map/reduce_scatter | solution.py:94
  7.2 12.7 %copy-start.18 = (bf16[1024,512]{1,0:T(8,128)(2,1)S(1)}, bf16[1024,512]{1,0:T(8,128)(2,1)}, u32[]{:S(2)}) copy-start(bf16[1024,512]{1,0:T(8,128)(2,1)} %param.22) | copy-start | bytes 3145732
  18.1 9.1 %copy-start.31 = (f32[256]{0:T(256)}, f32[256]{0:T(256)S(1)}, u32[]{:S(2)}) copy-start(f32[256]{0:T(256)S(1)} %get-tuple-element.126) | copy-start | bytes 3076
  18.1 9.1 %copy-start.16 = (bf16[1024,512]{1,0:T(8,128)(2,1)S(1)}, bf16[1024,512]{1,0:T(8,128)(2,1)}, u32[]{:S(2)}) copy-start(bf16[1024,512]{1,0:T(8,128)(2,1)} %param.20) | copy-start | bytes 3145732
  21.2 11.0 %collective-permute-start.1 = (bf16[2,256,512]{2,1,0:T(8,128)(2,1)}, bf16[2,256,512]{2,1,0:T(8,128)(2,1)}, u32[]{:S(2)}, u32[]{:S(2)}) collective-permute-start(bf16[2,256,512]{2,1,0:T(8,128)(2,1)} %pad_maximum_fusion.8), channel_id=1, source_target_pairs={{2,0},{4,2},{6,4},{8,6},{10,8},{12,10},{14,12},{16,14},{18,16},{20... | collective-permute-start | bytes 1572872 | tf_op jit(solution)/shard_map/ppermute | solution.py:25
  25.2 15.0 %collective-permute-start = (bf16[2,256,512]{2,1,0:T(8,128)(2,1)}, bf16[2,256,512]{2,1,0:T(8,128)(2,1)}, u32[]{:S(2)}, u32[]{:S(2)}) collective-permute-start(bf16[2,256,512]{2,1,0:T(8,128)(2,1)} %pad_maximum_fusion.8), channel_id=1, source_target_pairs={{0,2},{2,4},{4,6},{6,8},{8,10},{10,12},{12,14},{14,16},{16,18},{18... | collective-permute-start | bytes 1572872 | tf_op jit(solution)/shard_map/ppermute | solution.py:24
  28.0 19.6 %copy-start.14 = (bf16[2,128,4,128]{1,3,2,0:T(8,128)(2,1)}, bf16[2,128,4,128]{1,3,2,0:T(8,128)(2,1)S(1)}, u32[]{:S(2)}) copy-start(bf16[2,128,4,128]{1,3,2,0:T(8,128)(2,1)S(1)} %copy.30) | copy-start | bytes 786436
  47.6 1.5 copy-start.7
  47.6 2.2 copy-start.9
  47.6 2.2 copy-start.10
  48.4 1.5 copy-start.1
  50.8 27.3 %copy-start.5 = (bf16[256,512]{1,0:T(8,128)(2,1)S(1)}, bf16[256,512]{1,0:T(8,128)(2,1)}, u32[]{:S(2)}) copy-start(bf16[256,512]{1,0:T(8,128)(2,1)} %param.19) | copy-start | bytes 786436
  51.0 45.8 %copy-start.21 = (f32[9,512]{1,0:T(8,128)S(1)}, f32[9,512]{1,0:T(8,128)}, u32[]{:S(2)}) copy-start(f32[9,512]{1,0:T(8,128)} %param.24) | copy-start | bytes 55300
  51.0 47.1 %copy-start.20 = (bf16[256,512]{1,0:T(8,128)(2,1)S(1)}, bf16[256,512]{1,0:T(8,128)(2,1)}, u32[]{:S(2)}) copy-start(bf16[256,512]{1,0:T(8,128)(2,1)} %param.25) | copy-start | bytes 786436
  52.4 694.9 %reduce-scatter.5.cloned.1.call-start = ((), (), s32[]{:S(2)}) async-start(), calls=%async_computation.3 | async-start | bytes 1572864 | tf_op jit(solution)/shard_map/reduce_scatter | solution.py:163
  87.0 9.8 %collective-permute-start.2 = (f32[4,512]{1,0:T(4,128)S(1)}, f32[4,512]{1,0:T(4,128)S(1)}, u32[]{:S(2)}, u32[]{:S(2)}) collective-permute-start(f32[4,512]{1,0:T(4,128)S(1)} %get-tuple-element.111), channel_id=1, source_target_pairs={{0,2},{2,4},{4,6},{6,8},{8,10},{10,12},{12,14},{14,16},{16,18},{18... | collective-permute-start | bytes 24584 | tf_op jit(solution)/shard_map/ppermute | solution.py:24
  88.9 9.2 %collective-permute-start.3 = (f32[4,512]{1,0:T(4,128)S(1)}, f32[4,512]{1,0:T(4,128)S(1)}, u32[]{:S(2)}, u32[]{:S(2)}) collective-permute-start(f32[4,512]{1,0:T(4,128)S(1)} %get-tuple-element.112), channel_id=1, source_target_pairs={{2,0},{4,2},{6,4},{8,6},{10,8},{12,10},{14,12},{16,14},{18,16},{20... | collective-permute-start | bytes 24584 | tf_op jit(solution)/shard_map/ppermute | solution.py:25
  99.6 9.8 %collective-permute-start.4 = (f32[4,512]{1,0:T(4,128)S(1)}, f32[4,512]{1,0:T(4,128)S(1)}, u32[]{:S(2)}, u32[]{:S(2)}) collective-permute-start(f32[4,512]{1,0:T(4,128)S(1)} %get-tuple-element.109), channel_id=1, source_target_pairs={{2,0},{4,2},{6,4},{8,6},{10,8},{12,10},{14,12},{16,14},{18,16},{20... | collective-permute-start | bytes 24584 | tf_op jit(solution)/shard_map/ppermute | solution.py:25
  107.5 9.2 %collective-permute-start.5 = (f32[4,512]{1,0:T(4,128)S(1)}, f32[4,512]{1,0:T(4,128)S(1)}, u32[]{:S(2)}, u32[]{:S(2)}) collective-permute-start(f32[4,512]{1,0:T(4,128)S(1)} %get-tuple-element.110), channel_id=1, source_target_pairs={{0,2},{2,4},{4,6},{6,8},{8,10},{10,12},{12,14},{14,16},{16,18},{18... | collective-permute-start | bytes 24584 | tf_op jit(solution)/shard_map/ppermute | solution.py:24
  128.9 11.2 %copy-start.11 = (bf16[1,640,512]{1,2,0:T(8,128)(2,1)S(1)}, bf16[1,640,512]{1,2,0:T(8,128)(2,1)}, u32[]{:S(2)}) copy-start(bf16[1,640,512]{1,2,0:T(8,128)(2,1)} %copy.34) | copy-start | bytes 1966084
  140.2 2.3 copy-start.2
  142.4 2.4 copy-start.15
  156.2 2.5 copy-start.8
  160.1 1.9 copy-start.3
  163.1 22.8 %collective-permute-start.7 = (f32[2,256,512]{1,2,0:T(8,128)}, f32[2,256,512]{1,2,0:T(8,128)S(1)}, u32[]{:S(2)}, u32[]{:S(2)}) collective-permute-start(f32[2,256,512]{1,2,0:T(8,128)} %slice.362), channel_id=1, source_target_pairs={{0,2},{2,4},{4,6},{6,8},{8,10},{10,12},{12,14},{14,16},{16,18},{18... | collective-permute-start | bytes 3145736 | tf_op jit(solution)/shard_map/ppermute | solution.py:33
  165.0 21.9 %collective-permute-start.6 = (f32[2,256,512]{1,2,0:T(8,128)}, f32[2,256,512]{1,2,0:T(8,128)}, u32[]{:S(2)}, u32[]{:S(2)}) collective-permute-start(f32[2,256,512]{1,2,0:T(8,128)} %slice.361), channel_id=1, source_target_pairs={{2,0},{4,2},{6,4},{8,6},{10,8},{12,10},{14,12},{16,14},{18,16},{20... | collective-permute-start | bytes 3145736 | tf_op jit(solution)/shard_map/ppermute | solution.py:33
  184.1 4.8 copy-start.17
  185.9 3.5 copy-start.19
  185.9 1.0 copy-start.13
  189.5 1.6 copy-start.32
  189.5 2.9 copy-start.4
  189.5 2.8 copy-start.12
  191.0 2.2 copy-start.22
  191.0 2.2 copy-start.23
  191.0 2.2 copy-start.24
  191.0 2.2 copy-start.25
  191.0 2.2 copy-start.26
  191.0 2.2 copy-start.27
  191.0 2.2 copy-start.28
  191.0 2.2 copy-start.29
  191.0 2.2 copy-start.30
  192.3 562.8 %copy-start.6 = (f32[256,1024]{1,0:T(8,128)S(1)}, f32[256,1024]{1,0:T(8,128)}, u32[]{:S(2)}) copy-start(f32[256,1024]{1,0:T(8,128)} %fusion.25) | copy-start | bytes 3145732
Sparse Core Ops, SparseCore 0:
  52.6 25.4 reduce-scatter.2
  191.2 25.5 reduce-scatter.4
where the time goes:
time: 765 us; the launch traced here: 764 us
  blocking collectives  593 us (78%)
  waiting for transfers between devices  46.4 us (6%)
  matrix products  36.9 us (5%)
  starting transfers between devices  35.2 us (5%)
  other arithmetic  20.9 us (3%)
  local copies, waits for them, and re-layouts  16.4 us (2%)
  between operations  14.7 us (2%)
    psum x1, blocking collectives, local(): grad_kernel = lax.psum(kernel_local, 'tm')  554 us
    reduce_scatter x1, waiting for transfers between devices, local(): lax.psum_scatter(partial_out, 'head', scatter_dimension=1, tiled=True)  25.6 us
    ppermute x3, starting transfers between devices, extended_2(): after = lax.ppermute(first, axis, down)  19.6 us
  transfers between devices with their start and end apart: 10, of which 5 were waited for; matrix products, arithmetic and copies ran while one was open for 2% of the time, Pallas kernels for 0%

commit v1 on v0

v1 whole, which is shorter than its diff:
```python
import functools
import jax
import jax.numpy as jnp
from jax import lax
from jax.experimental import pallas as pl
from jax.experimental.pallas import tpu as pltpu
from jax.sharding import PartitionSpec as P

D = 1024
HEAD_DIM = 128
BLOCK = 128
CONTEXT = 2
KW = 9
EPSILON = 1e-05
MASKED = -1e30

ROWS = CONTEXT * BLOCK
SHARE = 512
HEADS = SHARE // HEAD_DIM
LANES = 128
EDGE = 16
PACK = ROWS + 2 * EDGE
CHUNKS = D // LANES
HALF_CHUNKS = SHARE // LANES
PAD = 16
EXT = ROWS + 2 * PAD
HALF = KW // 2
SCALE = HEAD_DIM ** (-0.5)
F32 = jnp.float32
BF16 = jnp.bfloat16


def nn(a, b):
    return lax.dot_general(a, b, (((1,), (0,)), ((), ())), preferred_element_type=F32)


def nt(a, b):
    return lax.dot_general(a, b, (((1,), (1,)), ((), ())), preferred_element_type=F32)


def tn(a, b):
    return lax.dot_general(a, b, (((0,), (0,)), ((), ())), preferred_element_type=F32)


def row_sum(a):
    return jnp.sum(a, axis=1, keepdims=True)


def moments(a, b):
    center = (row_sum(a) + row_sum(b)) * (1.0 / D)
    spread = (row_sum(a * a) + row_sum(b * b)) * (1.0 / D) - center * center
    return center, lax.rsqrt(spread + EPSILON)


def norm_pair(a, b):
    a = a.astype(F32)
    b = b.astype(F32)
    center, rstd = moments(a, b)
    return (a - center) * rstd, (b - center) * rstd, rstd


def own_other(h):
    own = pl.ds(pl.multiple_of(h * SHARE, SHARE), SHARE)
    other = pl.ds(pl.multiple_of((1 - h) * SHARE, SHARE), SHARE)
    return own, other


def lanes_of(head):
    return slice(head * HEAD_DIM, (head + 1) * HEAD_DIM)


def band_bias(right, valid):
    row = (lax.broadcasted_iota(jnp.int32, (ROWS, ROWS), 0) >= BLOCK).astype(jnp.int32)
    col = (lax.broadcasted_iota(jnp.int32, (ROWS, ROWS), 1) >= BLOCK).astype(jnp.int32)
    hidden = ((row - col) == 1 - 2 * right) | (valid == 0)
    return jnp.where(hidden, MASKED, 0.0).astype(F32)


def own_kernel(info, xo, mp, wq, wk, wv, q, k, v):
    own, other = own_other(info[0])
    no, np_, _ = norm_pair(xo[...], mp[:ROWS, :])
    no = no.astype(BF16)
    np_ = np_.astype(BF16)
    for w, out in ((wq, q), (wk, k), (wv, v)):
        out[...] = (nn(no, w[own, :]) + nn(np_, w[other, :])).astype(BF16)


def halo_kv(info, mo, mp, wk, wv, k, v):
    own, other = own_other(info[0])
    no, np_, _ = norm_pair(mo[:ROWS, :], mp[:ROWS, :])
    no = no.astype(BF16)
    np_ = np_.astype(BF16)
    for w, out in ((wk, k), (wv, v)):
        out[...] = (nn(no, w[own, :]) + nn(np_, w[other, :])).astype(BF16)


def first_kernel(info, mo, mp, wk, wv, q, k, v, ka, va, e, acc, top, total):
    halo_kv(info, mo, mp, wk, wv, ka, va)
    bias = band_bias(1 - info[1], 1)
    for head in range(HEADS):
        f = lanes_of(head)
        qh = q[:, f]
        s_own = nt(qh, k[:, f]) * SCALE
        s_a = nt(qh, ka[:, f]) * SCALE + bias
        m = jnp.maximum(jnp.max(s_own, axis=1, keepdims=True), jnp.max(s_a, axis=1, keepdims=True))
        e_own = jnp.exp(s_own - m)
        e_a = jnp.exp(s_a - m)
        total[head] = jnp.broadcast_to(row_sum(e_own) + row_sum(e_a), (ROWS, LANES))
        top[head] = jnp.broadcast_to(m, (ROWS, LANES))
        e_own = e_own.astype(BF16)
        e_a = e_a.astype(BF16)
        e[head, :, :ROWS] = e_own
        e[head, :, ROWS:] = e_a
        acc[:, f] = nn(e_own, v[:, f]) + nn(e_a, va[:, f])


def second_kernel(
    info, mo, mp, wk, wv, wo, q, acc, top, total, kb, vb, e, weight, att, part, edge_a, edge_b
):
    halo_kv(info, mo, mp, wk, wv, kb, vb)
    bias = band_bias(info[1], info[2])
    for head in range(HEADS):
        f = lanes_of(head)
        s = nt(q[:, f], kb[:, f]) * SCALE + bias
        m1 = top[head][:, :1]
        m = jnp.maximum(m1, jnp.max(s, axis=1, keepdims=True))
        shrink = jnp.exp(m1 - m)
        eb = jnp.exp(s - m)
        inverse = 1.0 / (total[head][:, :1] * shrink + row_sum(eb))
        eb = eb.astype(BF16)
        e[head] = eb
        o = (acc[:, f] * shrink + nn(eb, vb[:, f])) * inverse
        att[:, f] = o.astype(BF16)
        weight[0, head] = jnp.broadcast_to(shrink * inverse, (ROWS, LANES))
        weight[1, head] = jnp.broadcast_to(inverse, (ROWS, LANES))
    own, other = own_other(info[0])
    part[:, :SHARE] = nn(att[...], wo[:, own]).astype(BF16)
    part[:, SHARE:] = nn(att[...], wo[:, other]).astype(BF16)
    odd = info[1]
    last = ROWS - EDGE
    edge_a[...] = part[pl.ds(pl.multiple_of((1 - odd) * last, EDGE), EDGE), :]
    edge_b[...] = part[pl.ds(pl.multiple_of(odd * last, EDGE), EDGE), :]


def conv_kernel(
    info, xo, mp, a0, a1, b0, b1, part, part_p, ea, eb, e2, co, cp, to, tp, wo,
    output, dh, datt, gk,
    n2s, cs, dzs, dns, hs, taps, rs2, sum0, sum1, dhb,
):
    odd = info[1]
    own, other = own_other(info[0])
    is_odd = odd == 1
    step = 32
    for c in range(HALF_CHUNKS):
        f = slice(c * LANES, (c + 1) * LANES)
        taps[c, :KW, :] = to[:, f]
        taps[HALF_CHUNKS + c, :KW, :] = tp[:, f]

    def rows_in(index, carry):
        r = pl.multiple_of(index * step, step)
        rows = pl.ds(r, step)
        held = pl.ds(pl.multiple_of(PAD + r, PAD), step)
        p = part[rows, :].astype(F32)
        pp = part_p[rows, :].astype(F32)
        ho = xo[rows, :].astype(F32) + p[:, :SHARE] + pp[:, SHARE:]
        hp = mp[rows, :].astype(F32) + p[:, SHARE:] + pp[:, :SHARE]
        center, rstd = moments(ho, hp)
        hs[rows, :] = ho
        rs2[rows, :] = jnp.broadcast_to(rstd, (step, LANES))
        ctan = co[rows, :].astype(F32)
        ctan_p = cp[rows, :].astype(F32)
        for c in range(HALF_CHUNKS):
            f = slice(c * LANES, (c + 1) * LANES)
            n2s[c, held, :] = (ho[:, f] - center) * rstd
            n2s[HALF_CHUNKS + c, held, :] = (hp[:, f] - center) * rstd
            cs[c, held, :] = ctan[:, f]
            cs[HALF_CHUNKS + c, held, :] = ctan_p[:, f]
        return carry

    lax.fori_loop(0, ROWS // step, rows_in, 0)

    pa = ea[...].astype(F32)
    pb = eb[...].astype(F32)
    qb = e2[:EDGE, :].astype(F32)
    qa = e2[EDGE:, :].astype(F32)
    sides = (
        (slice(ROWS - EDGE, ROWS), slice(ROWS + EDGE, PACK), is_odd, 0, info[3]),
        (slice(0, EDGE), slice(ROWS, ROWS + EDGE), jnp.logical_not(is_odd), PAD + ROWS, info[4]),
    )
    for x_rows, c_rows, from_a, at, valid in sides:
        def pick(one, two):
            return jnp.where(from_a, one.astype(F32), two.astype(F32))

        pe = pick(pa, pb)
        pe_p = pick(qa, qb)
        ho = pick(a0[x_rows, :], b0[x_rows, :]) + pe[:, :SHARE] + pe_p[:, SHARE:]
        hp = pick(a1[x_rows, :], b1[x_rows, :]) + pe[:, SHARE:] + pe_p[:, :SHARE]
        center, rstd = moments(ho, hp)
        ctan = pick(a0[c_rows, :], b0[c_rows, :])
        ctan_p = pick(a1[c_rows, :], b1[c_rows, :])
        inside = valid == 1
        for c in range(HALF_CHUNKS):
            f = slice(c * LANES, (c + 1) * LANES)
            for d, hh, cc in ((c, ho, ctan), (HALF_CHUNKS + c, hp, ctan_p)):
                n2s[d, at:at + EDGE, :] = jnp.where(inside, (hh[:, f] - center) * rstd, 0.0)
                cs[d, at:at + EDGE, :] = jnp.where(inside, cc[:, f], 0.0)

    piece = 136

    def forward(c, carry, mine):
        w = taps[c]
        for r0 in (8, 8 + piece):
            z = w[0:1, :] * n2s[c, r0 - HALF:r0 - HALF + piece, :]
            for tap in range(1, KW):
                at = r0 + tap - HALF
                z = z + w[tap:tap + 1, :] * n2s[c, at:at + piece, :]
            gate = jax.nn.sigmoid(z)
            dzs[c, r0:r0 + piece, :] = cs[c, r0:r0 + piece, :] * gate * (1.0 + z * (1.0 - gate))
            if mine:
                lo = max(r0, PAD)
                hi = min(r0 + piece, PAD + ROWS)
                lane = pl.ds(pl.multiple_of(c * LANES, LANES), LANES)
                mix = (z * gate)[lo - r0:hi - r0, :]
                hs[lo - PAD:hi - PAD, lane] = hs[lo - PAD:hi - PAD, lane] + mix
        if mine:
            lane = pl.ds(pl.multiple_of(c * LANES, LANES), LANES)
            dz = dzs[c, PAD:PAD + ROWS, :]
            for tap in range(KW):
                at = PAD + tap - HALF
                gk[tap:tap + 1, lane] = jnp.sum(
                    dz * n2s[c, at:at + ROWS, :], axis=0, keepdims=True
                )
        return carry

    lax.fori_loop(0, HALF_CHUNKS, functools.partial(forward, mine=True), 0)
    lax.fori_loop(HALF_CHUNKS, CHUNKS, functools.partial(forward, mine=False), 0)
    output[...] = hs[...].astype(BF16)

    sum0[...] = jnp.zeros_like(sum0)
    sum1[...] = jnp.zeros_like(sum1)

    def backward(c, carry):
        w = taps[c]
        for r0 in (0, ROWS // 2):
            at = PAD + r0 + HALF
            g = w[0:1, :] * dzs[c, at:at + ROWS // 2, :]
            for tap in range(1, KW):
                at = PAD + r0 + HALF - tap
                g = g + w[tap:tap + 1, :] * dzs[c, at:at + ROWS // 2, :]
            dns[c, r0:r0 + ROWS // 2, :] = g
            half = slice(r0, r0 + ROWS // 2)
            sum0[half, :] = sum0[half, :] + g
            sum1[half, :] = sum1[half, :] + g * n2s[c, PAD + r0:PAD + r0 + ROWS // 2, :]
        return carry

    lax.fori_loop(0, CHUNKS, backward, 0)
    sum0[...] = jnp.broadcast_to(row_sum(sum0[...]) * (1.0 / D), (ROWS, LANES))
    sum1[...] = jnp.broadcast_to(row_sum(sum1[...]) * (1.0 / D), (ROWS, LANES))

    def finish(c, carry, mine):
        lane = pl.ds(pl.multiple_of(c * LANES, LANES), LANES)
        value = cs[c, PAD:PAD + ROWS, :] + rs2[...] * (
            dns[c] - sum0[...] - n2s[c, PAD:PAD + ROWS, :] * sum1[...]
        )
        if mine:
            dh[:, lane] = value
        dhb[:, lane] = value.astype(BF16)
        return carry

    lax.fori_loop(0, HALF_CHUNKS, functools.partial(finish, mine=True), 0)
    lax.fori_loop(HALF_CHUNKS, CHUNKS, functools.partial(finish, mine=False), 0)
    datt[...] = (nt(dhb[:, :SHARE], wo[:, own]) + nt(dhb[:, SHARE:], wo[:, other])).astype(BF16)


def pair_grad(qh, kh, vh, gh, eh, wh, delta):
    dots = nt(gh, vh)
    p = eh.astype(F32) * wh
    ds = (p * (dots - delta) * SCALE).astype(BF16)
    return nn(ds, kh), tn(ds, qh), tn(p.astype(BF16), gh)


def back_b_kernel(q, kb, vb, datt, att, e, weight, dq, dkv):
    for head in range(HEADS):
        f = lanes_of(head)
        gh = datt[:, f]
        delta = row_sum(gh.astype(F32) * att[:, f].astype(F32))
        d_q, d_k, d_v = pair_grad(
            q[:, f], kb[:, f], vb[:, f], gh, e[head], weight[1, head][:, :1], delta
        )
        dq[:, f] = d_q
        dkv[0, :, f] = d_k.astype(BF16)
        dkv[1, :, f] = d_v.astype(BF16)


def back_own_kernel(info, q, k, v, ka, va, datt, att, e, weight, dq_b, wq, dkv_a, dkv, pin):
    dq = []
    for head in range(HEADS):
        f = lanes_of(head)
        gh = datt[:, f]
        delta = row_sum(gh.astype(F32) * att[:, f].astype(F32))
        wh = weight[0, head][:, :1]
        q_a, k_a, v_a = pair_grad(q[:, f], ka[:, f], va[:, f], gh, e[head, :, ROWS:], wh, delta)
        dkv_a[0, :, f] = k_a.astype(BF16)
        dkv_a[1, :, f] = v_a.astype(BF16)
        q_o, k_o, v_o = pair_grad(q[:, f], k[:, f], v[:, f], gh, e[head, :, :ROWS], wh, delta)
        dkv[0, :, f] = k_o
        dkv[1, :, f] = v_o
        dq.append((dq_b[:, f] + q_a + q_o).astype(BF16))
    own, other = own_other(info[0])
    dq = jnp.concatenate(dq, axis=1)
    pin[:, :SHARE] = nt(dq, wq[own, :])
    pin[:, SHARE:] = nt(dq, wq[other, :])


def project_kernel(info, xo, mp, dkv, got_a, got_b, pin, wk, wv, send, keep, stat):
    own, other = own_other(info[0])
    dk = (dkv[0] + got_a[0].astype(F32) + got_b[0].astype(F32)).astype(BF16)
    dv = (dkv[1] + got_a[1].astype(F32) + got_b[1].astype(F32)).astype(BF16)
    p_own = pin[:, :SHARE] + nt(dk, wk[own, :]) + nt(dv, wv[own, :])
    p_other = pin[:, SHARE:] + nt(dk, wk[other, :]) + nt(dv, wv[other, :])
    no, np_, _ = norm_pair(xo[...], mp[:ROWS, :])
    s0 = row_sum(p_own) + row_sum(p_other)
    s1 = row_sum(p_own * no) + row_sum(p_other * np_)
    keep[...] = p_own
    send[:, :SHARE] = p_other.astype(BF16)
    lane = lax.broadcasted_iota(jnp.int32, (ROWS, LANES), 1)
    s0_hi = s0.astype(BF16).astype(F32)
    s1_hi = s1.astype(BF16).astype(F32)
    packed = jnp.where(lane == 0, s0_hi, 0.0)
    packed = jnp.where(lane == 1, s0 - s0_hi, packed)
    packed = jnp.where(lane == 2, s1_hi, packed)
    packed = jnp.where(lane == 3, s1 - s1_hi, packed)
    send[:, SHARE:] = packed.astype(BF16)
    stat[...] = jnp.where(lane == 0, s0, jnp.where(lane == 2, s1, 0.0))


def final_kernel(xo, mp, keep, stat, got, dh, grad):
    no, _, rstd = norm_pair(xo[...], mp[:ROWS, :])
    dn1 = keep[...] + got[:, :SHARE].astype(F32)
    lane = lax.broadcasted_iota(jnp.int32, (ROWS, LANES), 1)
    sums = stat[...] + got[:, SHARE:].astype(F32)
    s0 = row_sum(jnp.where(lane < 2, sums, 0.0)) * (1.0 / D)
    s1 = row_sum(jnp.where(lane < 2, 0.0, sums)) * (1.0 / D)
    grad[...] = (dh[...] + rstd * (dn1 - s0 - no * s1)).astype(BF16)


def call(kernel, args, outs, scratch=(), smem=True, us=1.0):
    whole = pl.BlockSpec(memory_space=pltpu.VMEM)
    specs = [whole] * len(args)
    if smem:
        specs[0] = pl.BlockSpec(memory_space=pltpu.SMEM)
    return pl.pallas_call(
        kernel,
        out_shape=[jax.ShapeDtypeStruct(shape, dtype) for shape, dtype in outs],
        in_specs=specs,
        out_specs=[whole] * len(outs),
        scratch_shapes=[pltpu.VMEM(shape, dtype) for shape, dtype in scratch],
        compiler_params=pltpu.CompilerParams(vmem_limit_bytes=40 * 1024 * 1024),
        cost_estimate=pl.CostEstimate(
            flops=int(us * 1e9), bytes_accessed=int(us * 1e6), transcendentals=0
        ),
    )(*args)


def local(inputs, w_query, w_key, w_value, w_out, kernel, cotangent):
    count = lax.axis_size("tm")
    assert inputs.shape == (ROWS, SHARE) and count % 2 == 0
    place = lax.axis_index("tm")
    odd = place % 2
    not_first = (place > 0).astype(jnp.int32)
    not_last = (place < count - 1).astype(jnp.int32)
    info = jnp.stack(
        [lax.axis_index("head"), odd, jnp.where(odd == 1, not_last, not_first), not_first, not_last]
    ).astype(jnp.int32)

    def over_head(value):
        return lax.ppermute(value, "head", [(0, 1), (1, 0)])

    def over_a(value):
        return lax.ppermute(value, "tm", [(i, i ^ 1) for i in range(count)])

    def over_b(value):
        pairs = [(i, i + 1) for i in range(1, count - 1, 2)]
        return lax.ppermute(value, "tm", pairs + [(j, i) for i, j in pairs])

    big = ((ROWS, SHARE), BF16)
    state = ((HEADS, ROWS, LANES), F32)
    mine = jnp.concatenate([inputs, cotangent[:EDGE], cotangent[ROWS - EDGE:]], axis=0)
    mp = over_head(mine)
    b0 = over_b(mine)
    a0 = over_a(mine)
    b1 = over_b(mp)
    a1 = over_a(mp)
    cot_p = over_head(cotangent)
    taps_p = over_head(kernel)
    q, k, v = call(
        own_kernel, (info, inputs, mp, w_query, w_key, w_value), (big, big, big), us=2.0
    )
    ka, va, e_one, acc, top, total = call(
        first_kernel,
        (info, a0, a1, w_key, w_value, q, k, v),
        (big, big, ((HEADS, ROWS, 2 * ROWS), BF16), ((ROWS, SHARE), F32), state, state),
        us=4.0,
    )
    kb, vb, e_two, weight, att, part, edge_a, edge_b = call(
        second_kernel,
        (info, b0, b1, w_key, w_value, w_out, q, acc, top, total),
        (
            big,
            big,
            ((HEADS, ROWS, ROWS), BF16),
            ((2, HEADS, ROWS, LANES), F32),
            big,
            ((ROWS, D), BF16),
            ((EDGE, D), BF16),
            ((EDGE, D), BF16),
        ),
        us=4.0,
    )
    part_p = over_head(part)
    eb = over_b(edge_b)
    ea = over_a(edge_a)
    e2 = over_head(jnp.concatenate([eb, ea], axis=0))
    chunked = ((CHUNKS, EXT, LANES), F32)
    tall = ((ROWS, LANES), F32)
    output, dh, datt, gk = call(
        conv_kernel,
        (
            info, inputs, mp, a0, a1, b0, b1, part, part_p, ea, eb, e2, cotangent, cot_p,
            kernel, taps_p, w_out,
        ),
        (big, ((ROWS, SHARE), F32), big, ((KW, SHARE), F32)),
        scratch=(
            chunked, chunked, chunked, ((CHUNKS, ROWS, LANES), F32), ((ROWS, SHARE), F32),
            ((CHUNKS, 16, LANES), F32), tall, tall, tall, ((ROWS, D), BF16),
        ),
        us=6.0,
    )
    pair = ((2, ROWS, SHARE), BF16)
    dq_b, dkv_b = call(
        back_b_kernel,
        (q, kb, vb, datt, att, e_two, weight),
        (((ROWS, SHARE), F32), pair),
        smem=False,
        us=3.0,
    )
    got_b = over_b(dkv_b)
    dkv_a, dkv, pin = call(
        back_own_kernel,
        (info, q, k, v, ka, va, datt, att, e_one, weight, dq_b, w_query),
        (pair, ((2, ROWS, SHARE), F32), ((ROWS, D), F32)),
        us=6.0,
    )
    got_a = over_a(dkv_a)
    send, keep, stat = call(
        project_kernel,
        (info, inputs, mp, dkv, got_a, got_b, pin, w_key, w_value),
        (((ROWS, SHARE + LANES), BF16), ((ROWS, SHARE), F32), tall),
        us=2.0,
    )
    got = over_head(send)
    (grad,) = call(
        final_kernel, (inputs, mp, keep, stat, got, dh), (big,), smem=False, us=1.0
    )
    step = 1
    while step < count:
        gk = gk + lax.ppermute(gk, "tm", [(i, i ^ step) for i in range(count)])
        step *= 2
    return output, grad, gk


def solution(mesh):
    placed = (
        P("tm", "head"),
        P(None, "head"),
        P(None, "head"),
        P(None, "head"),
        P("head", None),
        P(None, "head"),
        P("tm", "head"),
    )
    return jax.shard_map(
        local,
        mesh=mesh,
        in_specs=placed,
        out_specs=(P("tm", "head"), P("tm", "head"), P(None, "head")),
        check_vma=False,
    )
```

time: 765 us -> 126 us (0.16)
  the two profiles are of different devices: /device:TPU:128 before, /device:TPU:2 now
where the time goes in v1:
time: 126 us; the launch traced here: 125 us
  waiting for transfers between devices  57.2 us (45%)
  starting transfers between devices  39.2 us (31%)
  Pallas kernels  21.6 us (17%)
  local copies, waits for them, and re-layouts  4.52 us (4%)
  other arithmetic  1.7 us (1%)
    ppermute x4, waiting for transfers between devices, over_b(): return lax.ppermute(value, 'tm', pairs + [(j, i) for i, j in pairs])  26.3 us
    pallas_call x8, Pallas kernels, call(): pl.pallas_call(kernel, out_shape=[jax.ShapeDtypeStruct(shape, dtype) for...  21.6 us
    ppermute x7, waiting for transfers between devices, local(): gk = gk + lax.ppermute(gk, 'tm', [(i, i ^ step) for i in range(count)])  20.2 us
    ppermute x4, starting transfers between devices, over_b(): return lax.ppermute(value, 'tm', pairs + [(j, i) for i, j in pairs])  14.1 us
    ppermute x7, starting transfers between devices, local(): gk = gk + lax.ppermute(gk, 'tm', [(i, i ^ step) for i in range(count)])  12.7 us
    ppermute x6, starting transfers between devices, over_head(): return lax.ppermute(value, 'head', [(0, 1), (1, 0)])  12.3 us
    ppermute x6, waiting for transfers between devices, over_head(): return lax.ppermute(value, 'head', [(0, 1), (1, 0)])  10.7 us
    unnamed x20, local copies, waits for them, and re-layouts  3.7 us
  transfers between devices with their start and end apart: 21, of which 11 were waited for; matrix products, arithmetic and copies ran while one was open for 1% of the time, Pallas kernels for 4%

profile of v1, /device:TPU:2, one launch (start us, length us, event | category | flops | bytes accessed | tf_op | source)
XLA Modules:
  0.0 125.2 jit_solution(4040725791741153827)
XLA Ops:
  0.6 0.7 fusion
  1.4 1.0 pad_maximum_fusion
  2.4 2.2 %collective-permute-start = (bf16[288,512]{1,0:T(8,128)(2,1)S(1)}, bf16[288,512]{1,0:T(8,128)(2,1)S(1)}, u32[]{:S(2)}, u32[]{:S(2)}) collective-permute-start(bf16[288,512]{1,0:T(8,128)(2,1)S(1)} %pad_maximum_fusion), channel_id=1, source_target_pairs={{0,1},{1,0},{2,3},{3,2},{4,5},{5,4},{6,7},{7,6},{8,9},{9,8},{10,11... | collective-permute-start | bytes 884744 | tf_op jit(solution)/shard_map/ppermute | solution.py:377
  4.6 0.0 collective-permute-start.1
  4.6 8.1 %collective-permute-done.mp = bf16[288,512]{1,0:T(8,128)(2,1)S(1)} collective-permute-done((bf16[288,512]{1,0:T(8,128)(2,1)S(1)}, bf16[288,512]{1,0:T(8,128)(2,1)S(1)}, u32[]{:S(2)}, u32[]{:S(2)}) %collective-permute-start) | collective-permute-done | bytes 294944 | tf_op jit(solution)/shard_map/ppermute | solution.py:377
  12.8 0.0 collective-permute-start.2
  12.8 5.0 %collective-permute-start.3 = (bf16[288,512]{1,0:T(8,128)(2,1)S(1)}, bf16[288,512]{1,0:T(8,128)(2,1)S(1)}, u32[]{:S(2)}, u32[]{:S(2)}) collective-permute-start(bf16[288,512]{1,0:T(8,128)(2,1)S(1)} %pad_maximum_fusion), channel_id=1, source_target_pairs={{2,4},{6,8},{10,12},{14,16},{18,20},{22,24},{26,28},{30,32},{34,36... | collective-permute-start | bytes 884744 | tf_op jit(solution)/shard_map/ppermute | solution.py:384
  17.8 0.1 stack.23.info
  17.9 2.7 %collective-permute-start.4 = (bf16[288,512]{1,0:T(8,128)(2,1)S(1)}, bf16[288,512]{1,0:T(8,128)(2,1)S(1)}, u32[]{:S(2)}, u32[]{:S(2)}) collective-permute-start(bf16[288,512]{1,0:T(8,128)(2,1)S(1)} %collective-permute-done.mp), channel_id=1, source_target_pairs={{2,4},{6,8},{10,12},{14,16},{18,20},{22,24},{26,28},{30,32},{34,36... | collective-permute-start | bytes 884744 | tf_op jit(solution)/shard_map/ppermute | solution.py:384
  20.5 0.0 copy-done
  20.5 0.0 copy-start.3
  20.6 1.2 copy-done.3
  21.8 1.2 copy-done.5
  23.0 1.2 copy-done.7
  24.2 1.7 %shard_map.94 = (bf16[256,512]{1,0:T(8,128)(2,1)S(1)}, bf16[256,512]{1,0:T(8,128)(2,1)S(1)}, bf16[256,512]{1,0:T(8,128)(2,1)S(1)}) custom-call(s32[5]{0:T(128)S(1)} %stack.23.info, bf16[256,512]{1,0:T(8,128)(2,1)S(1)} %copy-done, bf16[288,512]{1,0:T(8,128)(2,1)S(1)} %collective-permute-done.mp, bf16[1024,512]{1,0:T(8,128)(2,1)S(1)} %copy-done.3, ...), custom_call_target="tpu_custom_call" | custom-call | flops 2000000000 | bytes 2000000 | tf_op jit(solution)/shard_map/pallas_call | solution.py:352
  25.9 0.0 collective-permute-done.1.mo.a0
  25.9 0.0 collective-permute-done.2.mp.a1
  26.0 0.0 copy-done.6
  26.0 0.0 copy-done.8
  26.0 0.0 copy-start.2
  26.0 2.7 %shard_map.95 = (bf16[256,512]{1,0:T(8,128)(2,1)S(1)}, bf16[256,512]{1,0:T(8,128)(2,1)S(1)}, bf16[4,256,512]{2,1,0:T(8,128)(2,1)S(1)}, f32[256,512]{1,0:T(8,128)...) custom-call(s32[5]{0:T(128)S(1)} %stack.23.info, bf16[288,512]{1,0:T(8,128)(2,1)S(1)} %collective-permute-done.1.mo.a0, ...), custom_call_target="tpu_custom_call" | custom-call | flops 4000000000 | bytes 4000000 | tf_op jit(solution)/shard_map/pallas_call | solution.py:352
  28.7 0.0 collective-permute-done.3.mo.b0
  28.7 0.0 collective-permute-done.4.mp.b1
  28.7 0.0 copy-start.1
  28.8 4.5 %shard_map.96 = (bf16[256,512]{1,0:T(8,128)(2,1)S(1)}, bf16[256,512]{1,0:T(8,128)(2,1)S(1)}, bf16[4,256,256]{2,1,0:T(8,128)(2,1)S(1)}, f32[2,4,256,128]{3,2,1,0:...) custom-call(s32[5]{0:T(128)S(1)} %stack.23.info, ...), custom_call_target="tpu_custom_call" | custom-call | flops 4000000000 | bytes 4000000 | tf_op jit(solution)/shard_map/pallas_call | solution.py:352
  33.3 2.2 %collective-permute-start.5 = (bf16[256,1024]{1,0:T(8,128)(2,1)S(1)}, bf16[256,1024]{1,0:T(8,128)(2,1)S(1)}, u32[]{:S(2)}, u32[]{:S(2)}) collective-permute-start(bf16[256,1024]{1,0:T(8,128)(2,1)S(1)} %get-tuple-element.38.part), channel_id=1, source_target_pairs={{0,1},{1,0},{2,3},{3,2},{4,5},{5,4},{6,7},{7,6},{8,9},{9,8},{10,11... | collective-permute-start | bytes 1572872 | tf_op jit(solution)/shard_map/ppermute | solution.py:377
  35.5 1.4 %collective-permute-start.9 = (bf16[256,512]{1,0:T(8,128)(2,1)S(1)}, bf16[256,512]{1,0:T(8,128)(2,1)S(1)}, u32[]{:S(2)}, u32[]{:S(2)}) collective-permute-start(bf16[256,512]{1,0:T(8,128)(2,1)S(1)} %copy-done.1), channel_id=1, source_target_pairs={{0,1},{1,0},{2,3},{3,2},{4,5},{5,4},{6,7},{7,6},{8,9},{9,8},{10,11... | collective-permute-start | bytes 786440 | tf_op jit(solution)/shard_map/ppermute | solution.py:377
  36.9 0.0 collective-permute-start.6
  36.9 4.6 %collective-permute-start.7 = (bf16[16,1024]{1,0:T(8,128)(2,1)S(1)}, bf16[16,1024]{1,0:T(8,128)(2,1)S(1)}, u32[]{:S(2)}, u32[]{:S(2)}) collective-permute-start(bf16[16,1024]{1,0:T(8,128)(2,1)S(1)} %get-tuple-element.40), channel_id=1, source_target_pairs={{2,4},{6,8},{10,12},{14,16},{18,20},{22,24},{26,28},{30,32},{34,36... | collective-permute-start | bytes 98312 | tf_op jit(solution)/shard_map/ppermute | solution.py:384
  41.5 0.0 collective-permute-done.6.ea
  41.5 15.6 %collective-permute-done.7.eb = bf16[16,1024]{1,0:T(8,128)(2,1)S(1)} collective-permute-done((bf16[16,1024]{1,0:T(8,128)(2,1)S(1)}, bf16[16,1024]{1,0:T(8,128)(2,1)S(1)}, u32[]{:S(2)}, u32[]{:S(2)}) %collective-permute-start.7) | collective-permute-done | bytes 32800 | tf_op jit(solution)/shard_map/ppermute | solution.py:384
  57.1 0.0 collective-permute-start.8
  57.1 0.0 copy-done.9
  57.1 3.5 %collective-permute-start.10 = (f32[9,512]{1,0:T(8,128)S(1)}, f32[9,512]{1,0:T(8,128)S(1)}, u32[]{:S(2)}, u32[]{:S(2)}) collective-permute-start(f32[9,512]{1,0:T(8,128)S(1)} %copy-done.9), channel_id=1, source_target_pairs={{0,1},{1,0},{2,3},{3,2},{4,5},{5,4},{6,7},{7,6},{8,9},{9,8},{10,11... | collective-permute-start | bytes 55304 | tf_op jit(solution)/shard_map/ppermute | solution.py:377
  60.6 2.6 %collective-permute-done.10.tp = f32[9,512]{1,0:T(8,128)S(1)} collective-permute-done((f32[9,512]{1,0:T(8,128)S(1)}, f32[9,512]{1,0:T(8,128)S(1)}, u32[]{:S(2)}, u32[]{:S(2)}) %collective-permute-start.10) | collective-permute-done | bytes 18464 | tf_op jit(solution)/shard_map/ppermute | solution.py:377
  63.2 0.0 collective-permute-done.9.cp
  63.2 0.0 collective-permute-done.8.e2
  63.2 0.0 collective-permute-done.5.part_p
  63.2 5.2 %shard_map.97 = (bf16[256,512]{1,0:T(8,128)(2,1)}, f32[256,512]{1,0:T(8,128)S(1)}, bf16[256,512]{1,0:T(8,128)(2,1)S(1)}, f32[9,512]{1,0:T(8,128)S(1)}) custom-call(s32[5]{0:T(128)S(1)} %stack.23.info, bf16[256,512]{1,0:T(8,128)(2,1)S(1)} %copy-done, bf16[288,512]{1,0:T(8,128)(2,1)S(1)} %collective-permute-done.mp, ...), custom_call_target="tpu_custom_call" | custom-call | flops 6000000000 | bytes 6000000 | tf_op jit(solution)/shard_map/pallas_call | solution.py:352
  68.4 1.4 %shard_map.98 = (f32[256,512]{1,0:T(8,128)S(1)}, bf16[2,256,512]{2,1,0:T(8,128)(2,1)S(1)}) custom-call(bf16[256,512]{1,0:T(8,128)(2,1)S(1)} %get-tuple-element.32.q, bf16[256,512]{1,0:T(8,128)(2,1)S(1)} %get-tuple-element.48.kb, bf16[256,512]{1,0:T(8,128)(2,1)S(1)} %get-tuple-element.49.vb, bf16[256,512]{1,0:T(8,128)(2,1)S(1)} %get-tuple-element.44.datt, ...), custom_call_target="tpu_custom_call" | custom-call | flops 3000000000 | bytes 3000000 | tf_op jit(solution)/shard_map/pallas_call | solution.py:352
  69.8 3.4 %shard_map.99 = (bf16[2,256,512]{2,1,0:T(8,128)(2,1)S(1)}, f32[2,256,512]{2,1,0:T(8,128)S(1)}, f32[256,1024]{1,0:T(8,128)S(1)}) custom-call(s32[5]{0:T(128)S(1)} %stack.23.info, bf16[256,512]{1,0:T(8,128)(2,1)S(1)} %get-tuple-element.32.q, bf16[256,512]{1,0:T(8,128)(2,1)S(1)} %get-tuple-element.33.k, bf16[256,512]{1,0:T(8,128)(2,1)S(1)} %get-tuple-element.34.v, ...), custom_call_target="tpu_custom_call" | custom-call | flops 6000000000 | bytes 6000000 | tf_op jit(solution)/shard_map/pallas_call | solution.py:352
  73.2 0.1 collective-permute-start.11
  73.3 1.9 %collective-permute-start.12 = (bf16[2,256,512]{2,1,0:T(8,128)(2,1)S(1)}, bf16[2,256,512]{2,1,0:T(8,128)(2,1)S(1)}, u32[]{:S(2)}, u32[]{:S(2)}) collective-permute-start(bf16[2,256,512]{2,1,0:T(8,128)(2,1)S(1)} %get-tuple-element.54), channel_id=1, source_target_pairs={{2,4},{6,8},{10,12},{14,16},{18,20},{22,24},{26,28},{30,32},{34,36... | collective-permute-start | bytes 1572872 | tf_op jit(solution)/shard_map/ppermute | solution.py:384
  75.3 0.0 collective-permute-done.11.got_a
  75.3 10.7 %collective-permute-done.12.got_b = bf16[2,256,512]{2,1,0:T(8,128)(2,1)S(1)} collective-permute-done((bf16[2,256,512]{2,1,0:T(8,128)(2,1)S(1)}, bf16[2,256,512]{2,1,0:T(8,128)(2,1)S(1)}, u32[]{:S(2)}, u32[]{:S(2)}) %collective-permute-start.12) | collective-permute-done | bytes 524320 | tf_op jit(solution)/shard_map/ppermute | solution.py:384
  85.9 1.6 %shard_map.100 = (bf16[256,640]{1,0:T(8,128)(2,1)S(1)}, f32[256,512]{1,0:T(8,128)S(1)}, f32[256,128]{1,0:T(8,128)S(1)}) custom-call(s32[5]{0:T(128)S(1)} %stack.23.info, bf16[256,512]{1,0:T(8,128)(2,1)S(1)} %copy-done, bf16[288,512]{1,0:T(8,128)(2,1)S(1)} %collective-permute-done.mp, f32[2,256,512]{2,1,0:T(8,128)S(1)} %get-tuple-element.52.dkv, ...), custom_call_target="tpu_custom_call" | custom-call | flops 2000000000 | bytes 2000000 | tf_op jit(solution)/shard_map/pallas_call | solution.py:352
  87.5 2.9 %collective-permute-start.13 = (bf16[256,640]{1,0:T(8,128)(2,1)S(1)}, bf16[256,640]{1,0:T(8,128)(2,1)S(1)}, u32[]{:S(2)}, u32[]{:S(2)}) collective-permute-start(bf16[256,640]{1,0:T(8,128)(2,1)S(1)} %get-tuple-element.58), channel_id=1, source_target_pairs={{0,1},{1,0},{2,3},{3,2},{4,5},{5,4},{6,7},{7,6},{8,9},{9,8},{10,11... | collective-permute-start | bytes 983048 | tf_op jit(solution)/shard_map/ppermute | solution.py:377
  90.4 0.0 collective-permute-start.14
  90.4 1.2 collective-permute-done.14
  91.6 0.0 collective-permute-start.15
  91.6 3.9 %collective-permute-done.15 = f32[9,512]{1,0:T(8,128)S(1)} collective-permute-done((f32[9,512]{1,0:T(8,128)S(1)}, f32[9,512]{1,0:T(8,128)S(1)}, u32[]{:S(2)}, u32[]{:S(2)}) %collective-permute-start.15) | collective-permute-done | bytes 18464 | tf_op jit(solution)/shard_map/ppermute | solution.py:467
  95.6 0.0 collective-permute-start.16
  95.6 5.4 %collective-permute-done.16 = f32[9,512]{1,0:T(8,128)S(1)} collective-permute-done((f32[9,512]{1,0:T(8,128)S(1)}, f32[9,512]{1,0:T(8,128)S(1)}, u32[]{:S(2)}, u32[]{:S(2)}) %collective-permute-start.16) | collective-permute-done | bytes 18464 | tf_op jit(solution)/shard_map/ppermute | solution.py:467
  101.0 0.0 collective-permute-start.17
  101.0 3.9 %collective-permute-done.17 = f32[9,512]{1,0:T(8,128)S(1)} collective-permute-done((f32[9,512]{1,0:T(8,128)S(1)}, f32[9,512]{1,0:T(8,128)S(1)}, u32[]{:S(2)}, u32[]{:S(2)}) %collective-permute-start.17) | collective-permute-done | bytes 18464 | tf_op jit(solution)/shard_map/ppermute | solution.py:467
  104.9 1.9 %collective-permute-start.18 = (f32[9,512]{1,0:T(8,128)S(1)}, f32[9,512]{1,0:T(8,128)S(1)}, u32[]{:S(2)}, u32[]{:S(2)}) collective-permute-start(f32[9,512]{1,0:T(8,128)S(1)} %add.29), channel_id=1, source_target_pairs={{0,32},{2,34},{4,36},{6,38},{8,40},{10,42},{12,44},{14,46},{16,48}... | collective-permute-start | bytes 55304 | tf_op jit(solution)/shard_map/ppermute | solution.py:467
  106.8 2.0 %collective-permute-done.18 = f32[9,512]{1,0:T(8,128)S(1)} collective-permute-done((f32[9,512]{1,0:T(8,128)S(1)}, f32[9,512]{1,0:T(8,128)S(1)}, u32[]{:S(2)}, u32[]{:S(2)}) %collective-permute-start.18) | collective-permute-done | bytes 18464 | tf_op jit(solution)/shard_map/ppermute | solution.py:467
  108.8 3.3 %collective-permute-start.19 = (f32[9,512]{1,0:T(8,128)S(1)}, f32[9,512]{1,0:T(8,128)S(1)}, u32[]{:S(2)}, u32[]{:S(2)}) collective-permute-start(f32[9,512]{1,0:T(8,128)S(1)} %add.30), channel_id=1, source_target_pairs={{0,64},{2,66},{4,68},{6,70},{8,72},{10,74},{12,76},{14,78},{16,80}... | collective-permute-start | bytes 55304 | tf_op jit(solution)/shard_map/ppermute | solution.py:467
  112.1 1.9 %collective-permute-done.19 = f32[9,512]{1,0:T(8,128)S(1)} collective-permute-done((f32[9,512]{1,0:T(8,128)S(1)}, f32[9,512]{1,0:T(8,128)S(1)}, u32[]{:S(2)}, u32[]{:S(2)}) %collective-permute-start.19) | collective-permute-done | bytes 18464 | tf_op jit(solution)/shard_map/ppermute | solution.py:467
  114.0 7.6 %collective-permute-start.20 = (f32[9,512]{1,0:T(8,128)S(1)}, f32[9,512]{1,0:T(8,128)S(1)}, u32[]{:S(2)}, u32[]{:S(2)}) collective-permute-start(f32[9,512]{1,0:T(8,128)S(1)} %add.31), channel_id=1, source_target_pairs={{0,128},{2,130},{4,132},{6,134},{8,136},{10,138},{12,140},{14,142}... | collective-permute-start | bytes 55304 | tf_op jit(solution)/shard_map/ppermute | solution.py:467
  121.6 1.9 %collective-permute-done.20 = f32[9,512]{1,0:T(8,128)S(1)} collective-permute-done((f32[9,512]{1,0:T(8,128)S(1)}, f32[9,512]{1,0:T(8,128)S(1)}, u32[]{:S(2)}, u32[]{:S(2)}) %collective-permute-start.20) | collective-permute-done | bytes 18464 | tf_op jit(solution)/shard_map/ppermute | solution.py:467
  123.5 0.6 add.32
  124.1 0.0 collective-permute-done.13.got
  124.1 1.1 shard_map.101
  (17 shorter events, 0.1 us)
Async XLA Ops:
  1.4 19.2 %copy-start = (bf16[256,512]{1,0:T(8,128)(2,1)S(1)}, bf16[256,512]{1,0:T(8,128)(2,1)}, u32[]{:S(2)}) copy-start(bf16[256,512]{1,0:T(8,128)(2,1)} %xo.7) | copy-start | bytes 786436
  2.4 10.3 %collective-permute-start = (bf16[288,512]{1,0:T(8,128)(2,1)S(1)}, bf16[288,512]{1,0:T(8,128)(2,1)S(1)}, u32[]{:S(2)}, u32[]{:S(2)}) collective-permute-start(bf16[288,512]{1,0:T(8,128)(2,1)S(1)} %pad_maximum_fusion), channel_id=1, source_target_pairs={{0,1},{1,0},{2,3},{3,2},{4,5},{5,4},{6,7},{7,6},{8,9},{9,8},{10,11... | collective-permute-start | bytes 884744 | tf_op jit(solution)/shard_map/ppermute | solution.py:377
  4.6 21.3 %collective-permute-start.1 = (bf16[288,512]{1,0:T(8,128)(2,1)S(1)}, bf16[288,512]{1,0:T(8,128)(2,1)S(1)}, u32[]{:S(2)}, u32[]{:S(2)}) collective-permute-start(bf16[288,512]{1,0:T(8,128)(2,1)S(1)} %pad_maximum_fusion), channel_id=1, source_target_pairs={{0,2},{2,0},{4,6},{6,4},{8,10},{10,8},{12,14},{14,12},{16,18},{18,... | collective-permute-start | bytes 884744 | tf_op jit(solution)/shard_map/ppermute | solution.py:380
  12.8 13.2 %collective-permute-start.2 = (bf16[288,512]{1,0:T(8,128)(2,1)S(1)}, bf16[288,512]{1,0:T(8,128)(2,1)S(1)}, u32[]{:S(2)}, u32[]{:S(2)}) collective-permute-start(bf16[288,512]{1,0:T(8,128)(2,1)S(1)} %collective-permute-done.mp), channel_id=1, source_target_pairs={{0,2},{2,0},{4,6},{6,4},{8,10},{10,8},{12,14},{14,12},{16,18},{18,... | collective-permute-start | bytes 884744 | tf_op jit(solution)/shard_map/ppermute | solution.py:380
  12.8 16.0 %collective-permute-start.3 = (bf16[288,512]{1,0:T(8,128)(2,1)S(1)}, bf16[288,512]{1,0:T(8,128)(2,1)S(1)}, u32[]{:S(2)}, u32[]{:S(2)}) collective-permute-start(bf16[288,512]{1,0:T(8,128)(2,1)S(1)} %pad_maximum_fusion), channel_id=1, source_target_pairs={{2,4},{6,8},{10,12},{14,16},{18,20},{22,24},{26,28},{30,32},{34,36... | collective-permute-start | bytes 884744 | tf_op jit(solution)/shard_map/ppermute | solution.py:384
  17.9 10.9 %collective-permute-start.4 = (bf16[288,512]{1,0:T(8,128)(2,1)S(1)}, bf16[288,512]{1,0:T(8,128)(2,1)S(1)}, u32[]{:S(2)}, u32[]{:S(2)}) collective-permute-start(bf16[288,512]{1,0:T(8,128)(2,1)S(1)} %collective-permute-done.mp), channel_id=1, source_target_pairs={{2,4},{6,8},{10,12},{14,16},{18,20},{22,24},{26,28},{30,32},{34,36... | collective-permute-start | bytes 884744 | tf_op jit(solution)/shard_map/ppermute | solution.py:384
  20.5 1.2 copy-start.3
  21.8 1.2 copy-start.5
  23.0 1.2 copy-start.7
  24.2 1.7 %copy-start.6 = (bf16[1024,512]{1,0:T(8,128)(2,1)S(1)}, bf16[1024,512]{1,0:T(8,128)(2,1)}, u32[]{:S(2)}) copy-start(bf16[1024,512]{1,0:T(8,128)(2,1)} %wk.7) | copy-start | bytes 3145732
  24.2 1.8 %copy-start.8 = (bf16[1024,512]{1,0:T(8,128)(2,1)S(1)}, bf16[1024,512]{1,0:T(8,128)(2,1)}, u32[]{:S(2)}) copy-start(bf16[1024,512]{1,0:T(8,128)(2,1)} %wv.7) | copy-start | bytes 3145732
  26.0 2.8 %copy-start.2 = (bf16[512,1024]{1,0:T(8,128)(2,1)S(1)}, bf16[512,1024]{1,0:T(8,128)(2,1)}, u32[]{:S(2)}) copy-start(bf16[512,1024]{1,0:T(8,128)(2,1)} %wo.3) | copy-start | bytes 3145732
  28.7 6.7 %copy-start.1 = (bf16[256,512]{1,0:T(8,128)(2,1)S(1)}, bf16[256,512]{1,0:T(8,128)(2,1)}, u32[]{:S(2)}) copy-start(bf16[256,512]{1,0:T(8,128)(2,1)} %co.1) | copy-start | bytes 786436
  33.3 29.9 %collective-permute-start.5 = (bf16[256,1024]{1,0:T(8,128)(2,1)S(1)}, bf16[256,1024]{1,0:T(8,128)(2,1)S(1)}, u32[]{:S(2)}, u32[]{:S(2)}) collective-permute-start(bf16[256,1024]{1,0:T(8,128)(2,1)S(1)} %get-tuple-element.38.part), channel_id=1, source_target_pairs={{0,1},{1,0},{2,3},{3,2},{4,5},{5,4},{6,7},{7,6},{8,9},{9,8},{10,11... | collective-permute-start | bytes 1572872 | tf_op jit(solution)/shard_map/ppermute | solution.py:377
  35.5 27.7 %collective-permute-start.9 = (bf16[256,512]{1,0:T(8,128)(2,1)S(1)}, bf16[256,512]{1,0:T(8,128)(2,1)S(1)}, u32[]{:S(2)}, u32[]{:S(2)}) collective-permute-start(bf16[256,512]{1,0:T(8,128)(2,1)S(1)} %copy-done.1), channel_id=1, source_target_pairs={{0,1},{1,0},{2,3},{3,2},{4,5},{5,4},{6,7},{7,6},{8,9},{9,8},{10,11... | collective-permute-start | bytes 786440 | tf_op jit(solution)/shard_map/ppermute | solution.py:377
  36.9 4.6 %collective-permute-start.6 = (bf16[16,1024]{1,0:T(8,128)(2,1)S(1)}, bf16[16,1024]{1,0:T(8,128)(2,1)S(1)}, u32[]{:S(2)}, u32[]{:S(2)}) collective-permute-start(bf16[16,1024]{1,0:T(8,128)(2,1)S(1)} %get-tuple-element.39), channel_id=1, source_target_pairs={{0,2},{2,0},{4,6},{6,4},{8,10},{10,8},{12,14},{14,12},{16,18},{18,... | collective-permute-start | bytes 98312 | tf_op jit(solution)/shard_map/ppermute | solution.py:380
  36.9 20.2 %copy-start.9 = (f32[9,512]{1,0:T(8,128)S(1)}, f32[9,512]{1,0:T(8,128)}, u32[]{:S(2)}) copy-start(f32[9,512]{1,0:T(8,128)} %to.1) | copy-start | bytes 55300
  36.9 20.2 %collective-permute-start.7 = (bf16[16,1024]{1,0:T(8,128)(2,1)S(1)}, bf16[16,1024]{1,0:T(8,128)(2,1)S(1)}, u32[]{:S(2)}, u32[]{:S(2)}) collective-permute-start(bf16[16,1024]{1,0:T(8,128)(2,1)S(1)} %get-tuple-element.40), channel_id=1, source_target_pairs={{2,4},{6,8},{10,12},{14,16},{18,20},{22,24},{26,28},{30,32},{34,36... | collective-permute-start | bytes 98312 | tf_op jit(solution)/shard_map/ppermute | solution.py:384
  57.1 6.1 %collective-permute-start.8 = (bf16[32,1024]{1,0:T(8,128)(2,1)S(1)}, bf16[32,1024]{1,0:T(8,128)(2,1)S(1)}, u32[]{:S(2)}, u32[]{:S(2)}) collective-permute-start(bf16[32,1024]{1,0:T(8,128)(2,1)S(1)} %pad_maximum_fusion.1), channel_id=1, source_target_pairs={{0,1},{1,0},{2,3},{3,2},{4,5},{5,4},{6,7},{7,6},{8,9},{9,8},{10,11... | collective-permute-start | bytes 196616 | tf_op jit(solution)/shard_map/ppermute | solution.py:377
  57.1 6.1 %collective-permute-start.10 = (f32[9,512]{1,0:T(8,128)S(1)}, f32[9,512]{1,0:T(8,128)S(1)}, u32[]{:S(2)}, u32[]{:S(2)}) collective-permute-start(f32[9,512]{1,0:T(8,128)S(1)} %copy-done.9), channel_id=1, source_target_pairs={{0,1},{1,0},{2,3},{3,2},{4,5},{5,4},{6,7},{7,6},{8,9},{9,8},{10,11... | collective-permute-start | bytes 55304 | tf_op jit(solution)/shard_map/ppermute | solution.py:377
  68.4 1.4 %copy-start.4 = (bf16[1024,512]{1,0:T(8,128)(2,1)S(1)}, bf16[1024,512]{1,0:T(8,128)(2,1)}, u32[]{:S(2)}) copy-start(bf16[1024,512]{1,0:T(8,128)(2,1)} %wq.3) | copy-start | bytes 3145732
  73.2 2.0 %collective-permute-start.11 = (bf16[2,256,512]{2,1,0:T(8,128)(2,1)S(1)}, bf16[2,256,512]{2,1,0:T(8,128)(2,1)S(1)}, u32[]{:S(2)}, u32[]{:S(2)}) collective-permute-start(bf16[2,256,512]{2,1,0:T(8,128)(2,1)S(1)} %get-tuple-element.53), channel_id=1, source_target_pairs={{0,2},{2,0},{4,6},{6,4},{8,10},{10,8},{12,14},{14,12},{16,18},{18,... | collective-permute-start | bytes 1572872 | tf_op jit(solution)/shard_map/ppermute | solution.py:380
  73.3 12.6 %collective-permute-start.12 = (bf16[2,256,512]{2,1,0:T(8,128)(2,1)S(1)}, bf16[2,256,512]{2,1,0:T(8,128)(2,1)S(1)}, u32[]{:S(2)}, u32[]{:S(2)}) collective-permute-start(bf16[2,256,512]{2,1,0:T(8,128)(2,1)S(1)} %get-tuple-element.54), channel_id=1, source_target_pairs={{2,4},{6,8},{10,12},{14,16},{18,20},{22,24},{26,28},{30,32},{34,36... | collective-permute-start | bytes 1572872 | tf_op jit(solution)/shard_map/ppermute | solution.py:384
  87.5 36.6 %collective-permute-start.13 = (bf16[256,640]{1,0:T(8,128)(2,1)S(1)}, bf16[256,640]{1,0:T(8,128)(2,1)S(1)}, u32[]{:S(2)}, u32[]{:S(2)}) collective-permute-start(bf16[256,640]{1,0:T(8,128)(2,1)S(1)} %get-tuple-element.58), channel_id=1, source_target_pairs={{0,1},{1,0},{2,3},{3,2},{4,5},{5,4},{6,7},{7,6},{8,9},{9,8},{10,11... | collective-permute-start | bytes 983048 | tf_op jit(solution)/shard_map/ppermute | solution.py:377
  90.4 1.2 collective-permute-start.14
  91.6 3.9 %collective-permute-start.15 = (f32[9,512]{1,0:T(8,128)S(1)}, f32[9,512]{1,0:T(8,128)S(1)}, u32[]{:S(2)}, u32[]{:S(2)}) collective-permute-start(f32[9,512]{1,0:T(8,128)S(1)} %add.26), channel_id=1, source_target_pairs={{0,4},{2,6},{4,0},{6,2},{8,12},{10,14},{12,8},{14,10},{16,20},{18,... | collective-permute-start | bytes 55304 | tf_op jit(solution)/shard_map/ppermute | solution.py:467
  95.6 5.4 %collective-permute-start.16 = (f32[9,512]{1,0:T(8,128)S(1)}, f32[9,512]{1,0:T(8,128)S(1)}, u32[]{:S(2)}, u32[]{:S(2)}) collective-permute-start(f32[9,512]{1,0:T(8,128)S(1)} %add.27), channel_id=1, source_target_pairs={{0,8},{2,10},{4,12},{6,14},{8,0},{10,2},{12,4},{14,6},{16,24},{18,... | collective-permute-start | bytes 55304 | tf_op jit(solution)/shard_map/ppermute | solution.py:467
  101.0 3.9 %collective-permute-start.17 = (f32[9,512]{1,0:T(8,128)S(1)}, f32[9,512]{1,0:T(8,128)S(1)}, u32[]{:S(2)}, u32[]{:S(2)}) collective-permute-start(f32[9,512]{1,0:T(8,128)S(1)} %add.28), channel_id=1, source_target_pairs={{0,16},{2,18},{4,20},{6,22},{8,24},{10,26},{12,28},{14,30},{16,0},... | collective-permute-start | bytes 55304 | tf_op jit(solution)/shard_map/ppermute | solution.py:467
  104.9 3.9 %collective-permute-start.18 = (f32[9,512]{1,0:T(8,128)S(1)}, f32[9,512]{1,0:T(8,128)S(1)}, u32[]{:S(2)}, u32[]{:S(2)}) collective-permute-start(f32[9,512]{1,0:T(8,128)S(1)} %add.29), channel_id=1, source_target_pairs={{0,32},{2,34},{4,36},{6,38},{8,40},{10,42},{12,44},{14,46},{16,48}... | collective-permute-start | bytes 55304 | tf_op jit(solution)/shard_map/ppermute | solution.py:467
  108.8 5.2 %collective-permute-start.19 = (f32[9,512]{1,0:T(8,128)S(1)}, f32[9,512]{1,0:T(8,128)S(1)}, u32[]{:S(2)}, u32[]{:S(2)}) collective-permute-start(f32[9,512]{1,0:T(8,128)S(1)} %add.30), channel_id=1, source_target_pairs={{0,64},{2,66},{4,68},{6,70},{8,72},{10,74},{12,76},{14,78},{16,80}... | collective-permute-start | bytes 55304 | tf_op jit(solution)/shard_map/ppermute | solution.py:467
  114.0 9.4 %collective-permute-start.20 = (f32[9,512]{1,0:T(8,128)S(1)}, f32[9,512]{1,0:T(8,128)S(1)}, u32[]{:S(2)}, u32[]{:S(2)}) collective-permute-start(f32[9,512]{1,0:T(8,128)S(1)} %add.31), channel_id=1, source_target_pairs={{0,128},{2,130},{4,132},{6,134},{8,136},{10,138},{12,140},{14,142}... | collective-permute-start | bytes 55304 | tf_op jit(solution)/shard_map/ppermute | solution.py:467

commit v2 on v1

--- a/solution.py
+++ b/solution.py
@@ -19,7 +19,6 @@
 HEADS = SHARE // HEAD_DIM
 LANES = 128
 EDGE = 16
-PACK = ROWS + 2 * EDGE
 CHUNKS = D // LANES
 HALF_CHUNKS = SHARE // LANES
 PAD = 16
@@ -59,7 +58,17 @@
     return (a - center) * rstd, (b - center) * rstd, rstd
 
 
-def own_other(h):
+def placement():
+    place = lax.axis_index("tm")
+    last = lax.axis_size("tm") - 1
+    odd = lax.rem(place, 2)
+    left = (place > 0).astype(jnp.int32)
+    right = (place < last).astype(jnp.int32)
+    return odd, left, right
+
+
+def own_other():
+    h = lax.axis_index("head")
     own = pl.ds(pl.multiple_of(h * SHARE, SHARE), SHARE)
     other = pl.ds(pl.multiple_of((1 - h) * SHARE, SHARE), SHARE)
     return own, other
@@ -76,27 +85,28 @@
     return jnp.where(hidden, MASKED, 0.0).astype(F32)
 
 
-def own_kernel(info, xo, mp, wq, wk, wv, q, k, v):
-    own, other = own_other(info[0])
-    no, np_, _ = norm_pair(xo[...], mp[:ROWS, :])
+def own_kernel(xo, xp, wq, wk, wv, q, k, v):
+    own, other = own_other()
+    no, np_, _ = norm_pair(xo[...], xp[...])
     no = no.astype(BF16)
     np_ = np_.astype(BF16)
     for w, out in ((wq, q), (wk, k), (wv, v)):
         out[...] = (nn(no, w[own, :]) + nn(np_, w[other, :])).astype(BF16)
 
 
-def halo_kv(info, mo, mp, wk, wv, k, v):
-    own, other = own_other(info[0])
-    no, np_, _ = norm_pair(mo[:ROWS, :], mp[:ROWS, :])
+def halo_kv(xo, xp, wk, wv, k, v):
+    own, other = own_other()
+    no, np_, _ = norm_pair(xo[...], xp[...])
     no = no.astype(BF16)
     np_ = np_.astype(BF16)
     for w, out in ((wk, k), (wv, v)):
         out[...] = (nn(no, w[own, :]) + nn(np_, w[other, :])).astype(BF16)
 
 
-def first_kernel(info, mo, mp, wk, wv, q, k, v, ka, va, e, acc, top, total):
-    halo_kv(info, mo, mp, wk, wv, ka, va)
-    bias = band_bias(1 - info[1], 1)
+def first_kernel(xo, xp, wk, wv, q, k, v, pack, ka, va, e, acc, top, total):
+    halo_kv(xo, xp, wk, wv, ka, va)
+    odd, _, _ = placement()
+    bias = band_bias(1 - odd, 1)
     for head in range(HEADS):
         f = lanes_of(head)
         qh = q[:, f]
@@ -115,10 +125,11 @@
 
 
 def second_kernel(
-    info, mo, mp, wk, wv, wo, q, acc, top, total, kb, vb, e, weight, att, part, edge_a, edge_b
+    xo, xp, wk, wv, wo, q, acc, top, total, kb, vb, e, weight, att, edges
 ):
-    halo_kv(info, mo, mp, wk, wv, kb, vb)
-    bias = band_bias(info[1], info[2])
+    halo_kv(xo, xp, wk, wv, kb, vb)
+    odd, left, right = placement()
+    bias = band_bias(odd, jnp.where(odd == 1, right, left))
     for head in range(HEADS):
         f = lanes_of(head)
         s = nt(q[:, f], kb[:, f]) * SCALE + bias
@@ -133,24 +144,47 @@
         att[:, f] = o.astype(BF16)
         weight[0, head] = jnp.broadcast_to(shrink * inverse, (ROWS, LANES))
         weight[1, head] = jnp.broadcast_to(inverse, (ROWS, LANES))
-    own, other = own_other(info[0])
+    own, other = own_other()
+    rim = jnp.concatenate([att[at, :] for at in edge_rows(placement()[0])], axis=0)
+    edges[:, :SHARE] = nn(rim, wo[:, own]).astype(BF16)
+    edges[:, SHARE:] = nn(rim, wo[:, other]).astype(BF16)
+
+
+def project_out_kernel(att, wo, part):
+    own, other = own_other()
     part[:, :SHARE] = nn(att[...], wo[:, own]).astype(BF16)
     part[:, SHARE:] = nn(att[...], wo[:, other]).astype(BF16)
-    odd = info[1]
+
+
+def edge_rows(odd):
     last = ROWS - EDGE
-    edge_a[...] = part[pl.ds(pl.multiple_of((1 - odd) * last, EDGE), EDGE), :]
-    edge_b[...] = part[pl.ds(pl.multiple_of(odd * last, EDGE), EDGE), :]
+    return (
+        pl.ds(pl.multiple_of((1 - odd) * last, EDGE), EDGE),
+        pl.ds(pl.multiple_of(odd * last, EDGE), EDGE),
+    )
+
+
+def merge_kernel(edges, edges_p, co, cp, to_a, to_b):
+    for n, (at, out) in enumerate(zip(edge_rows(placement()[0]), (to_a, to_b))):
+        rows = slice(n * EDGE, (n + 1) * EDGE)
+        mine = edges[rows, :].astype(F32)
+        theirs = edges_p[rows, :].astype(F32)
+        out[:EDGE, :SHARE] = (mine[:, :SHARE] + theirs[:, SHARE:]).astype(BF16)
+        out[:EDGE, SHARE:] = (mine[:, SHARE:] + theirs[:, :SHARE]).astype(BF16)
+        out[EDGE:, :SHARE] = co[at, :]
+        out[EDGE:, SHARE:] = cp[at, :]
 
 
 def conv_kernel(
-    info, xo, mp, a0, a1, b0, b1, part, part_p, ea, eb, e2, co, cp, to, tp, wo,
+    xo, xp, a0, a1, b0, b1, part, part_p, ea, eb, co, cp, to, wo,
     output, dh, datt, gk,
     n2s, cs, dzs, dns, hs, taps, rs2, sum0, sum1, dhb,
 ):
-    odd = info[1]
-    own, other = own_other(info[0])
+    odd, left, right = placement()
+    own, other = own_other()
     is_odd = odd == 1
     step = 32
+    tp = unpack_taps(cp)
     for c in range(HALF_CHUNKS):
         f = slice(c * LANES, (c + 1) * LANES)
         taps[c, :KW, :] = to[:, f]
@@ -163,7 +197,7 @@
         p = part[rows, :].astype(F32)
         pp = part_p[rows, :].astype(F32)
         ho = xo[rows, :].astype(F32) + p[:, :SHARE] + pp[:, SHARE:]
-        hp = mp[rows, :].astype(F32) + p[:, SHARE:] + pp[:, :SHARE]
+        hp = xp[rows, :].astype(F32) + p[:, SHARE:] + pp[:, :SHARE]
         center, rstd = moments(ho, hp)
         hs[rows, :] = ho
         rs2[rows, :] = jnp.broadcast_to(rstd, (step, LANES))
@@ -179,25 +213,22 @@
 
     lax.fori_loop(0, ROWS // step, rows_in, 0)
 
-    pa = ea[...].astype(F32)
-    pb = eb[...].astype(F32)
-    qb = e2[:EDGE, :].astype(F32)
-    qa = e2[EDGE:, :].astype(F32)
+    pa = ea[:EDGE, :].astype(F32)
+    pb = eb[:EDGE, :].astype(F32)
     sides = (
-        (slice(ROWS - EDGE, ROWS), slice(ROWS + EDGE, PACK), is_odd, 0, info[3]),
-        (slice(0, EDGE), slice(ROWS, ROWS + EDGE), jnp.logical_not(is_odd), PAD + ROWS, info[4]),
-    )
-    for x_rows, c_rows, from_a, at, valid in sides:
+        (slice(ROWS - EDGE, ROWS), is_odd, 0, left),
+        (slice(0, EDGE), jnp.logical_not(is_odd), PAD + ROWS, right),
+    )
+    for x_rows, from_a, at, valid in sides:
         def pick(one, two):
             return jnp.where(from_a, one.astype(F32), two.astype(F32))
 
         pe = pick(pa, pb)
-        pe_p = pick(qa, qb)
-        ho = pick(a0[x_rows, :], b0[x_rows, :]) + pe[:, :SHARE] + pe_p[:, SHARE:]
-        hp = pick(a1[x_rows, :], b1[x_rows, :]) + pe[:, SHARE:] + pe_p[:, :SHARE]
+        ho = pick(a0[x_rows, :], b0[x_rows, :]) + pe[:, :SHARE]
+        hp = pick(a1[x_rows, :], b1[x_rows, :]) + pe[:, SHARE:]
         center, rstd = moments(ho, hp)
-        ctan = pick(a0[c_rows, :], b0[c_rows, :])
-        ctan_p = pick(a1[c_rows, :], b1[c_rows, :])
+        ctan = pick(ea[EDGE:, :SHARE], eb[EDGE:, :SHARE])
+        ctan_p = pick(ea[EDGE:, SHARE:], eb[EDGE:, SHARE:])
         inside = valid == 1
         for c in range(HALF_CHUNKS):
             f = slice(c * LANES, (c + 1) * LANES)
@@ -279,46 +310,46 @@
     return nn(ds, kh), tn(ds, qh), tn(p.astype(BF16), gh)
 
 
-def back_b_kernel(q, kb, vb, datt, att, e, weight, dq, dkv):
+def back_halo_kernel(q, k, v, datt, att, e, weight, *refs, which):
+    dq, dkv = refs[-2:]
+    at = pl.ds(ROWS, ROWS) if which == 0 else pl.ds(0, ROWS)
     for head in range(HEADS):
         f = lanes_of(head)
         gh = datt[:, f]
         delta = row_sum(gh.astype(F32) * att[:, f].astype(F32))
         d_q, d_k, d_v = pair_grad(
-            q[:, f], kb[:, f], vb[:, f], gh, e[head], weight[1, head][:, :1], delta
+            q[:, f], k[:, f], v[:, f], gh, e[head, :, at], weight[which, head][:, :1], delta
         )
-        dq[:, f] = d_q
+        dq[:, f] = d_q + refs[0][:, f] if which == 0 else d_q
         dkv[0, :, f] = d_k.astype(BF16)
         dkv[1, :, f] = d_v.astype(BF16)
 
 
-def back_own_kernel(info, q, k, v, ka, va, datt, att, e, weight, dq_b, wq, dkv_a, dkv, pin):
+def back_own_kernel(q, k, v, datt, att, e, weight, dq_ab, wq, after, dkv, pin):
     dq = []
     for head in range(HEADS):
         f = lanes_of(head)
         gh = datt[:, f]
         delta = row_sum(gh.astype(F32) * att[:, f].astype(F32))
-        wh = weight[0, head][:, :1]
-        q_a, k_a, v_a = pair_grad(q[:, f], ka[:, f], va[:, f], gh, e[head, :, ROWS:], wh, delta)
-        dkv_a[0, :, f] = k_a.astype(BF16)
-        dkv_a[1, :, f] = v_a.astype(BF16)
-        q_o, k_o, v_o = pair_grad(q[:, f], k[:, f], v[:, f], gh, e[head, :, :ROWS], wh, delta)
-        dkv[0, :, f] = k_o
-        dkv[1, :, f] = v_o
-        dq.append((dq_b[:, f] + q_a + q_o).astype(BF16))
-    own, other = own_other(info[0])
+        d_q, d_k, d_v = pair_grad(
+            q[:, f], k[:, f], v[:, f], gh, e[head, :, :ROWS], weight[0, head][:, :1], delta
+        )
+        dkv[0, :, f] = d_k
+        dkv[1, :, f] = d_v
+        dq.append((d_q + dq_ab[:, f]).astype(BF16))
+    own, other = own_other()
     dq = jnp.concatenate(dq, axis=1)
     pin[:, :SHARE] = nt(dq, wq[own, :])
     pin[:, SHARE:] = nt(dq, wq[other, :])
 
 
-def project_kernel(info, xo, mp, dkv, got_a, got_b, pin, wk, wv, send, keep, stat):
-    own, other = own_other(info[0])
+def project_kernel(xo, xp, dkv, got_a, got_b, pin, wk, wv, after, send, keep, stat):
+    own, other = own_other()
     dk = (dkv[0] + got_a[0].astype(F32) + got_b[0].astype(F32)).astype(BF16)
     dv = (dkv[1] + got_a[1].astype(F32) + got_b[1].astype(F32)).astype(BF16)
     p_own = pin[:, :SHARE] + nt(dk, wk[own, :]) + nt(dv, wv[own, :])
     p_other = pin[:, SHARE:] + nt(dk, wk[other, :]) + nt(dv, wv[other, :])
-    no, np_, _ = norm_pair(xo[...], mp[:ROWS, :])
+    no, np_, _ = norm_pair(xo[...], xp[...])
     s0 = row_sum(p_own) + row_sum(p_other)
     s1 = row_sum(p_own * no) + row_sum(p_other * np_)
     keep[...] = p_own
@@ -334,8 +365,8 @@
     stat[...] = jnp.where(lane == 0, s0, jnp.where(lane == 2, s1, 0.0))
 
 
-def final_kernel(xo, mp, keep, stat, got, dh, grad):
-    no, _, rstd = norm_pair(xo[...], mp[:ROWS, :])
+def final_kernel(xo, xp, keep, stat, got, dh, after, grad):
+    no, _, rstd = norm_pair(xo[...], xp[...])
     dn1 = keep[...] + got[:, :SHARE].astype(F32)
     lane = lax.broadcasted_iota(jnp.int32, (ROWS, LANES), 1)
     sums = stat[...] + got[:, SHARE:].astype(F32)
@@ -344,20 +375,60 @@
     grad[...] = (dh[...] + rstd * (dn1 - s0 - no * s1)).astype(BF16)
 
 
-def call(kernel, args, outs, scratch=(), smem=True, us=1.0):
+def sum_kernel(*refs):
+    refs[-1][...] = sum(ref[...] for ref in refs[:-1])
+
+
+def stage_kernel(*refs):
+    half = (len(refs) - 2) // 2
+    pack, sems = refs[-2:]
+    copies = [
+        pltpu.make_async_copy(refs[i], refs[half + i], sems.at[i]) for i in range(half)
+    ]
+    for copy in copies:
+        copy.start()
+    for copy in copies:
+        copy.wait()
+    co, taps = refs[2 * half - 2:2 * half]
+    pack[:ROWS, :] = co[...]
+    rest = taps[...]
+    for n in range(3):
+        piece = rest.astype(BF16)
+        pack[ROWS + n * EDGE:ROWS + n * EDGE + KW, :] = piece
+        rest = rest - piece.astype(F32)
+
+
+def unpack_taps(pack):
+    return sum(
+        pack[ROWS + n * EDGE:ROWS + n * EDGE + KW, :].astype(F32) for n in (2, 1, 0)
+    )
+
+
+def stage(*arrays):
+    outs = [pltpu.VMEM(a.shape, a.dtype) for a in arrays]
+    outs.append(pltpu.VMEM((ROWS + 3 * EDGE, SHARE), BF16))
+    return pl.pallas_call(
+        stage_kernel,
+        out_shape=outs,
+        in_specs=[pl.BlockSpec(memory_space=pltpu.HBM)] * len(arrays),
+        out_specs=[pl.BlockSpec(memory_space=pltpu.VMEM)] * len(outs),
+        scratch_shapes=[pltpu.SemaphoreType.DMA((len(arrays),))],
+        compiler_params=pltpu.CompilerParams(vmem_limit_bytes=6 * 1024 * 1024),
+        cost_estimate=pl.CostEstimate(flops=0, bytes_accessed=64 * 1024 * 1024, transcendentals=0),
+    )(*[pltpu.with_memory_space_constraint(a, pltpu.HBM) for a in arrays])
+
+
+def call(kernel, args, outs, scratch=(), us=1.0, mib=6):
     whole = pl.BlockSpec(memory_space=pltpu.VMEM)
-    specs = [whole] * len(args)
-    if smem:
-        specs[0] = pl.BlockSpec(memory_space=pltpu.SMEM)
     return pl.pallas_call(
         kernel,
         out_shape=[jax.ShapeDtypeStruct(shape, dtype) for shape, dtype in outs],
-        in_specs=specs,
+        in_specs=[whole] * len(args),
         out_specs=[whole] * len(outs),
         scratch_shapes=[pltpu.VMEM(shape, dtype) for shape, dtype in scratch],
-        compiler_params=pltpu.CompilerParams(vmem_limit_bytes=40 * 1024 * 1024),
+        compiler_params=pltpu.CompilerParams(vmem_limit_bytes=mib * 1024 * 1024),
         cost_estimate=pl.CostEstimate(
-            flops=int(us * 1e9), bytes_accessed=int(us * 1e6), transcendentals=0
+            flops=int(us * 1e10), bytes_accessed=int(us * 1e7), transcendentals=0
         ),
     )(*args)
 
@@ -365,14 +436,6 @@
 def local(inputs, w_query, w_key, w_value, w_out, kernel, cotangent):
     count = lax.axis_size("tm")
     assert inputs.shape == (ROWS, SHARE) and count % 2 == 0
-    place = lax.axis_index("tm")
-    odd = place % 2
-    not_first = (place > 0).astype(jnp.int32)
-    not_last = (place < count - 1).astype(jnp.int32)
-    info = jnp.stack(
-        [lax.axis_index("head"), odd, jnp.where(odd == 1, not_last, not_first), not_first, not_last]
-    ).astype(jnp.int32)
-
     def over_head(value):
         return lax.ppermute(value, "head", [(0, 1), (1, 0)])
 
@@ -385,88 +448,102 @@
 
     big = ((ROWS, SHARE), BF16)
     state = ((HEADS, ROWS, LANES), F32)
-    mine = jnp.concatenate([inputs, cotangent[:EDGE], cotangent[ROWS - EDGE:]], axis=0)
-    mp = over_head(mine)
-    b0 = over_b(mine)
-    a0 = over_a(mine)
-    b1 = over_b(mp)
-    a1 = over_a(mp)
-    cot_p = over_head(cotangent)
-    taps_p = over_head(kernel)
+    xp = over_head(inputs)
+    b0 = over_b(inputs)
+    a0 = over_a(inputs)
+    *staged, pack = stage(w_query, w_key, w_value, w_out, inputs, cotangent, kernel)
+    pack_p = over_head(pack)
+    xp, a0, b0, *staged = lax.optimization_barrier((xp, a0, b0, *staged))
+    w_query, w_key, w_value, w_out, inputs, cotangent, kernel = staged
+    b1 = over_b(xp)
+    a1 = over_a(xp)
     q, k, v = call(
-        own_kernel, (info, inputs, mp, w_query, w_key, w_value), (big, big, big), us=2.0
+        own_kernel, (inputs, xp, w_query, w_key, w_value), (big, big, big), us=2.0
     )
     ka, va, e_one, acc, top, total = call(
         first_kernel,
-        (info, a0, a1, w_key, w_value, q, k, v),
+        (a0, a1, w_key, w_value, q, k, v, pack_p),
         (big, big, ((HEADS, ROWS, 2 * ROWS), BF16), ((ROWS, SHARE), F32), state, state),
-        us=4.0,
-    )
-    kb, vb, e_two, weight, att, part, edge_a, edge_b = call(
+        us=3.0,
+    )
+    edge = ((2 * EDGE, D), BF16)
+    kb, vb, e_two, weight, att, edges = call(
         second_kernel,
-        (info, b0, b1, w_key, w_value, w_out, q, acc, top, total),
+        (b0, b1, w_key, w_value, w_out, q, acc, top, total),
         (
             big,
             big,
             ((HEADS, ROWS, ROWS), BF16),
             ((2, HEADS, ROWS, LANES), F32),
             big,
-            ((ROWS, D), BF16),
-            ((EDGE, D), BF16),
-            ((EDGE, D), BF16),
+            edge,
         ),
         us=4.0,
     )
+    edges_p = over_head(edges)
+    (part,) = call(project_out_kernel, (att, w_out), (((ROWS, D), BF16),), us=1.0)
     part_p = over_head(part)
-    eb = over_b(edge_b)
-    ea = over_a(edge_a)
-    e2 = over_head(jnp.concatenate([eb, ea], axis=0))
+    to_a, to_b = call(
+        merge_kernel, (edges, edges_p, cotangent, pack_p), (edge, edge), us=3.0
+    )
+    eb = over_b(to_b)
+    ea = over_a(to_a)
     chunked = ((CHUNKS, EXT, LANES), F32)
     tall = ((ROWS, LANES), F32)
     output, dh, datt, gk = call(
         conv_kernel,
         (
-            info, inputs, mp, a0, a1, b0, b1, part, part_p, ea, eb, e2, cotangent, cot_p,
-            kernel, taps_p, w_out,
+            inputs, xp, a0, a1, b0, b1, part, part_p, ea, eb, cotangent, pack_p,
+            kernel, w_out,
         ),
         (big, ((ROWS, SHARE), F32), big, ((KW, SHARE), F32)),
         scratch=(
             chunked, chunked, chunked, ((CHUNKS, ROWS, LANES), F32), ((ROWS, SHARE), F32),
             ((CHUNKS, 16, LANES), F32), tall, tall, tall, ((ROWS, D), BF16),
         ),
-        us=6.0,
-    )
+        us=5.0,
+        mib=12,
+    )
+    chain = [gk]
+    assert count == 128
+    for steps in ((1,), (8, 16, 24), (32, 64, 96), (2, 4, 6)):
+        last = chain[-1]
+        parts = [
+            lax.ppermute(last, "tm", [(i, i ^ step) for i in range(count)]) for step in steps
+        ]
+        chain.extend(call(sum_kernel, (last, *parts), (((KW, SHARE), F32),), us=0.2, mib=1))
     pair = ((2, ROWS, SHARE), BF16)
     dq_b, dkv_b = call(
-        back_b_kernel,
+        functools.partial(back_halo_kernel, which=1),
         (q, kb, vb, datt, att, e_two, weight),
         (((ROWS, SHARE), F32), pair),
-        smem=False,
-        us=3.0,
+        us=1.5,
     )
     got_b = over_b(dkv_b)
-    dkv_a, dkv, pin = call(
+    dq_ab, dkv_a = call(
+        functools.partial(back_halo_kernel, which=0),
+        (q, ka, va, datt, att, e_one, weight, dq_b, chain[1]),
+        (((ROWS, SHARE), F32), pair),
+        us=1.5,
+    )
+    got_a = over_a(dkv_a)
+    dkv, pin = call(
         back_own_kernel,
-        (info, q, k, v, ka, va, datt, att, e_one, weight, dq_b, w_query),
-        (pair, ((2, ROWS, SHARE), F32), ((ROWS, D), F32)),
-        us=6.0,
-    )
-    got_a = over_a(dkv_a)
+        (q, k, v, datt, att, e_one, weight, dq_ab, w_query, chain[1]),
+        (((2, ROWS, SHARE), F32), ((ROWS, D), F32)),
+        us=2.0,
+    )
     send, keep, stat = call(
         project_kernel,
-        (info, inputs, mp, dkv, got_a, got_b, pin, w_key, w_value),
+        (inputs, xp, dkv, got_a, got_b, pin, w_key, w_value, chain[2]),
         (((ROWS, SHARE + LANES), BF16), ((ROWS, SHARE), F32), tall),
-        us=2.0,
+        us=1.5,
     )
     got = over_head(send)
     (grad,) = call(
-        final_kernel, (inputs, mp, keep, stat, got, dh), (big,), smem=False, us=1.0
-    )
-    step = 1
-    while step < count:
-        gk = gk + lax.ppermute(gk, "tm", [(i, i ^ step) for i in range(count)])
-        step *= 2
-    return output, grad, gk
+        final_kernel, (inputs, xp, keep, stat, got, dh, chain[3]), (big,), us=1.0
+    )
+    return output, grad, chain[-1]
 
 
 def solution(mesh):

time: 126 us -> 91.6 us (0.73)
  waiting for transfers between devices: 57.2 us -> 29 us
  local copies, waits for them, and re-layouts: 4.52 us -> 0.03 us
  other arithmetic: 1.7 us -> 0 us
    ppermute x7 -> x10, waiting for transfers between devices: 20.2 us -> 6.24 us  [local(): lax.ppermute(last, 'tm', [(i, i ^ step) for i in range(count)])]
    ppermute x6 -> x5, waiting for transfers between devices: 10.7 us -> 2.66 us  [over_head(): return lax.ppermute(value, 'head', [(0, 1), (1, 0)])]
    ppermute x7 -> x10, starting transfers between devices: 12.7 us -> 19.2 us  [local(): lax.ppermute(last, 'tm', [(i, i ^ step) for i in range(count)])]
    ppermute x4, waiting for transfers between devices: 26.3 us -> 19.8 us  [over_b(): return lax.ppermute(value, 'tm', pairs + [(j, i) for i, j in pairs])]
    ppermute x6 -> x5, starting transfers between devices: 12.3 us -> 7.96 us  [over_head(): return lax.ppermute(value, 'head', [(0, 1), (1, 0)])]
    unnamed x20 -> x12, local copies, waits for them, and re-layouts: 3.7 us -> 0.03 us
    pallas_call x8 -> x15, Pallas kernels: 21.6 us -> 19 us  [call(): pl.pallas_call(kernel, out_shape=[jax.ShapeDtypeStruct(shape, dtype) for...]
    pallas_call x0 -> x1, Pallas kernels: none -> 2.38 us  [stage(): pl.pallas_call(stage_kernel, out_shape=outs, in_specs=[pl.BlockSpec(memor...]
  transfers between devices with their start and end apart: 21 -> 23, of which waited for: 11 -> 12; matrix products, arithmetic and copies ran while one was open for 1% -> 0% of each run, Pallas kernels for 4% -> 13%
where the time goes in v2:
time: 91.6 us; the launch traced here: 91.1 us
  starting transfers between devices  39.7 us (43%)
  waiting for transfers between devices  29 us (32%)
  Pallas kernels  21.4 us (23%)
  between operations  0.95 us (1%)
    ppermute x4, waiting for transfers between devices, over_b(): return lax.ppermute(value, 'tm', pairs + [(j, i) for i, j in pairs])  19.8 us
    ppermute x10, starting transfers between devices, local(): lax.ppermute(last, 'tm', [(i, i ^ step) for i in range(count)])  19.2 us
    pallas_call x15, Pallas kernels, call(): pl.pallas_call(kernel, out_shape=[jax.ShapeDtypeStruct(shape, dtype) for...  19 us
    ppermute x4, starting transfers between devices, over_b(): return lax.ppermute(value, 'tm', pairs + [(j, i) for i, j in pairs])  12.2 us
    ppermute x5, starting transfers between devices, over_head(): return lax.ppermute(value, 'head', [(0, 1), (1, 0)])  7.96 us
    ppermute x10, waiting for transfers between devices, local(): lax.ppermute(last, 'tm', [(i, i ^ step) for i in range(count)])  6.24 us
    ppermute x5, waiting for transfers between devices, over_head(): return lax.ppermute(value, 'head', [(0, 1), (1, 0)])  2.66 us
    pallas_call x1, Pallas kernels, stage(): pl.pallas_call(stage_kernel, out_shape=outs, in_specs=[pl.BlockSpec(memor...  2.38 us
  transfers between devices with their start and end apart: 23, of which 12 were waited for; matrix products, arithmetic and copies ran while one was open for 0% of the time, Pallas kernels for 13%

profile of v2, /device:TPU:2, one launch (start us, length us, event | category | flops | bytes accessed | tf_op | source)
XLA Modules:
  0.0 91.1 jit_solution(3980103923033208469)
XLA Ops:
  0.6 0.1 collective-permute-start.1
  0.7 2.2 %collective-permute-start = (bf16[256,512]{1,0:T(8,128)(2,1)}, bf16[256,512]{1,0:T(8,128)(2,1)S(1)}, u32[]{:S(2)}, u32[]{:S(2)}) collective-permute-start(bf16[256,512]{1,0:T(8,128)(2,1)} %refs_4_.1), channel_id=1, source_target_pairs={{0,1},{1,0},{2,3},{3,2},{4,5},{5,4},{6,7},{7,6},{8,9},{9,8},{10,11... | collective-permute-start | bytes 786440 | tf_op jit(solution)/shard_map/ppermute | solution.py:440
  2.9 5.5 %collective-permute-start.2 = (bf16[256,512]{1,0:T(8,128)(2,1)}, bf16[256,512]{1,0:T(8,128)(2,1)S(1)}, u32[]{:S(2)}, u32[]{:S(2)}) collective-permute-start(bf16[256,512]{1,0:T(8,128)(2,1)} %refs_4_.1), channel_id=1, source_target_pairs={{2,4},{6,8},{10,12},{14,16},{18,20},{22,24},{26,28},{30,32},{34,36... | collective-permute-start | bytes 786440 | tf_op jit(solution)/shard_map/ppermute | solution.py:447
  8.5 2.4 %shard_map.94 = (bf16[1024,512]{1,0:T(8,128)(2,1)S(1)}, bf16[1024,512]{1,0:T(8,128)(2,1)S(1)}, bf16[1024,512]{1,0:T(8,128)(2,1)S(1)}, bf16[512,1024]{1,0:T(8,128...) custom-call(bf16[1024,512]{1,0:T(8,128)(2,1)} %refs_0_.1, ...), custom_call_target="tpu_custom_call" | custom-call | bytes 67108864 | tf_op jit(solution)/shard_map/pallas_call | solution.py:410
  10.9 0.0 copy-start
  10.9 0.1 collective-permute-start.5
  11.0 0.0 collective-permute-done.1.xo.a0
  11.0 0.2 collective-permute-done.xp
  11.2 7.6 %collective-permute-done.2.xo.b0 = bf16[256,512]{1,0:T(8,128)(2,1)S(1)} collective-permute-done((bf16[256,512]{1,0:T(8,128)(2,1)}, bf16[256,512]{1,0:T(8,128)(2,1)S(1)}, u32[]{:S(2)}, u32[]{:S(2)}) %collective-permute-start.2) | collective-permute-done | bytes 262176 | tf_op jit(solution)/shard_map/ppermute | solution.py:447
  18.8 2.0 %collective-permute-start.4 = (bf16[256,512]{1,0:T(8,128)(2,1)S(1)}, bf16[256,512]{1,0:T(8,128)(2,1)S(1)}, u32[]{:S(2)}, u32[]{:S(2)}) collective-permute-start(bf16[256,512]{1,0:T(8,128)(2,1)S(1)} %collective-permute-done.xp), channel_id=1, source_target_pairs={{2,4},{6,8},{10,12},{14,16},{18,20},{22,24},{26,28},{30,32},{34,36... | collective-permute-start | bytes 786440 | tf_op jit(solution)/shard_map/ppermute | solution.py:447
  20.8 0.1 collective-permute-start.3
  20.9 1.1 %shard_map.95 = (bf16[256,512]{1,0:T(8,128)(2,1)S(1)}, bf16[256,512]{1,0:T(8,128)(2,1)S(1)}, bf16[256,512]{1,0:T(8,128)(2,1)S(1)}) custom-call(bf16[256,512]{1,0:T(8,128)(2,1)S(1)} %get-tuple-element.58.xo, bf16[256,512]{1,0:T(8,128)(2,1)S(1)} %collective-permute-done.xp, bf16[1024,512]{1,0:T(8,128)(2,1)S(1)} %get-tuple-element.65.wq, ...), custom_call_target="tpu_custom_call" | custom-call | flops 20000000000 | bytes 20000000 | tf_op jit(solution)/shard_map/pallas_call | solution.py:423
  22.1 0.0 copy-done
  22.1 0.0 copy-start.2
  22.1 0.0 copy-start.4
  22.1 0.0 collective-permute-done.5.pack.cp
  22.1 0.3 collective-permute-done.3.xp.a1
  22.5 2.2 %shard_map.96 = (bf16[256,512]{1,0:T(8,128)(2,1)S(1)}, bf16[256,512]{1,0:T(8,128)(2,1)S(1)}, bf16[4,256,512]{2,1,0:T(8,128)(2,1)S(1)}, f32[256,512]{1,0:T(8,128)...) custom-call(bf16[256,512]{1,0:T(8,128)(2,1)S(1)} %collective-permute-done.1.xo.a0, ...), custom_call_target="tpu_custom_call" | custom-call | flops 30000001024 | bytes 30000000 | tf_op jit(solution)/shard_map/pallas_call | solution.py:423
  24.6 0.0 copy-done.2
  24.6 0.0 copy-done.4
  24.6 3.9 %collective-permute-done.4.xp.b1 = bf16[256,512]{1,0:T(8,128)(2,1)S(1)} collective-permute-done((bf16[256,512]{1,0:T(8,128)(2,1)S(1)}, bf16[256,512]{1,0:T(8,128)(2,1)S(1)}, u32[]{:S(2)}, u32[]{:S(2)}) %collective-permute-start.4) | collective-permute-done | bytes 262176 | tf_op jit(solution)/shard_map/ppermute | solution.py:447
  28.6 3.7 %shard_map.97 = (bf16[256,512]{1,0:T(8,128)(2,1)S(1)}, bf16[256,512]{1,0:T(8,128)(2,1)S(1)}, bf16[4,256,256]{2,1,0:T(8,128)(2,1)S(1)}, f32[2,4,256,128]{3,2,1,0:...) custom-call(bf16[256,512]{1,0:T(8,128)(2,1)S(1)} %collective-permute-done.2.xo.b0, ...), custom_call_target="tpu_custom_call" | custom-call | flops 40000000000 | bytes 40000000 | tf_op jit(solution)/shard_map/pallas_call | solution.py:423
  32.3 0.1 collective-permute-start.7
  32.4 0.4 shard_map.98.part
  32.8 3.6 %collective-permute-start.6 = (bf16[256,1024]{1,0:T(8,128)(2,1)S(1)}, bf16[256,1024]{1,0:T(8,128)(2,1)S(1)}, u32[]{:S(2)}, u32[]{:S(2)}) collective-permute-start(bf16[256,1024]{1,0:T(8,128)(2,1)S(1)} %shard_map.98.part), channel_id=1, source_target_pairs={{0,1},{1,0},{2,3},{3,2},{4,5},{5,4},{6,7},{7,6},{8,9},{9,8},{10,11... | collective-permute-start | bytes 1572872 | tf_op jit(solution)/shard_map/ppermute | solution.py:440
  36.4 2.5 %collective-permute-done.7.edges_p = bf16[32,1024]{1,0:T(8,128)(2,1)S(1)} collective-permute-done((bf16[32,1024]{1,0:T(8,128)(2,1)S(1)}, bf16[32,1024]{1,0:T(8,128)(2,1)S(1)}, u32[]{:S(2)}, u32[]{:S(2)}) %collective-permute-start.7) | collective-permute-done | bytes 65568 | tf_op jit(solution)/shard_map/ppermute | solution.py:440
  38.9 0.1 collective-permute-start.8
  39.0 1.9 %collective-permute-start.9 = (bf16[32,1024]{1,0:T(8,128)(2,1)S(1)}, bf16[32,1024]{1,0:T(8,128)(2,1)S(1)}, u32[]{:S(2)}, u32[]{:S(2)}) collective-permute-start(bf16[32,1024]{1,0:T(8,128)(2,1)S(1)} %get-tuple-element.77), channel_id=1, source_target_pairs={{2,4},{6,8},{10,12},{14,16},{18,20},{22,24},{26,28},{30,32},{34,36... | collective-permute-start | bytes 196616 | tf_op jit(solution)/shard_map/ppermute | solution.py:447
  41.0 0.0 collective-permute-done.8.ea
  41.0 8.2 %collective-permute-done.9.eb = bf16[32,1024]{1,0:T(8,128)(2,1)S(1)} collective-permute-done((bf16[32,1024]{1,0:T(8,128)(2,1)S(1)}, bf16[32,1024]{1,0:T(8,128)(2,1)S(1)}, u32[]{:S(2)}, u32[]{:S(2)}) %collective-permute-start.9) | collective-permute-done | bytes 65568 | tf_op jit(solution)/shard_map/ppermute | solution.py:447
  49.2 0.0 collective-permute-done.6.part_p
  49.2 4.7 %shard_map.100 = (bf16[256,512]{1,0:T(8,128)(2,1)}, f32[256,512]{1,0:T(8,128)S(1)}, bf16[256,512]{1,0:T(8,128)(2,1)S(1)}, f32[9,512]{1,0:T(8,128)S(1)}) custom-call(bf16[256,512]{1,0:T(8,128)(2,1)S(1)} %get-tuple-element.58.xo, bf16[256,512]{1,0:T(8,128)(2,1)S(1)} %collective-permute-done.xp, bf16[256,512]{1,0:T(8,128)(2,1)S(1)} %collective-permute-done.1.xo.a0, ...), custom_call_target="tpu_custom_call" | custom-call | flops 49999998976 | bytes 50000000 | tf_op jit(solution)/shard_map/pallas_call | solution.py:423
  53.9 0.0 collective-permute-start.10
  53.9 1.4 %shard_map.101 = (f32[256,512]{1,0:T(8,128)S(1)}, bf16[2,256,512]{2,1,0:T(8,128)(2,1)S(1)}) custom-call(bf16[256,512]{1,0:T(8,128)(2,1)S(1)} %get-tuple-element.66.q, bf16[256,512]{1,0:T(8,128)(2,1)S(1)} %get-tuple-element.85.k, bf16[256,512]{1,0:T(8,128)(2,1)S(1)} %get-tuple-element.86.v, bf16[256,512]{1,0:T(8,128)(2,1)S(1)} %get-tuple-element.80.datt, ...), custom_call_target="tpu_custom_call" | custom-call | flops 15000000512 | bytes 15000000 | tf_op jit(solution)/shard_map/pallas_call | solution.py:423
  55.3 2.7 %collective-permute-start.12 = (bf16[2,256,512]{2,1,0:T(8,128)(2,1)S(1)}, bf16[2,256,512]{2,1,0:T(8,128)(2,1)S(1)}, u32[]{:S(2)}, u32[]{:S(2)}) collective-permute-start(bf16[2,256,512]{2,1,0:T(8,128)(2,1)S(1)} %get-tuple-element.93), channel_id=1, source_target_pairs={{2,4},{6,8},{10,12},{14,16},{18,20},{22,24},{26,28},{30,32},{34,36... | collective-permute-start | bytes 1572872 | tf_op jit(solution)/shard_map/ppermute | solution.py:447
  58.0 0.0 collective-permute-done.10.refs_1_
  58.0 0.1 collective-permute-start.15
  58.1 2.0 %collective-permute-start.14 = (f32[9,512]{1,0:T(8,128)S(1)}, f32[9,512]{1,0:T(8,128)S(1)}, u32[]{:S(2)}, u32[]{:S(2)}) collective-permute-start(f32[9,512]{1,0:T(8,128)S(1)} %shard_map.102.refs_1_.after.refs_0_), channel_id=1, source_target_pairs={{0,32},{2,34},{4,36},{6,38},{8,40},{10,42},{12,44},{14,46},{16,48}... | collective-permute-start | bytes 55304 | tf_op jit(solution)/shard_map/ppermute | solution.py:512
  60.1 1.5 %collective-permute-start.13 = (f32[9,512]{1,0:T(8,128)S(1)}, f32[9,512]{1,0:T(8,128)S(1)}, u32[]{:S(2)}, u32[]{:S(2)}) collective-permute-start(f32[9,512]{1,0:T(8,128)S(1)} %shard_map.102.refs_1_.after.refs_0_), channel_id=1, source_target_pairs={{0,16},{2,18},{4,20},{6,22},{8,24},{10,26},{12,28},{14,30},{16,0},... | collective-permute-start | bytes 55304 | tf_op jit(solution)/shard_map/ppermute | solution.py:512
  61.6 1.3 %shard_map.103 = (f32[256,512]{1,0:T(8,128)S(1)}, bf16[2,256,512]{2,1,0:T(8,128)(2,1)S(1)}) custom-call(bf16[256,512]{1,0:T(8,128)(2,1)S(1)} %get-tuple-element.66.q, bf16[256,512]{1,0:T(8,128)(2,1)S(1)} %get-tuple-element.83.k, bf16[256,512]{1,0:T(8,128)(2,1)S(1)} %get-tuple-element.84.v, bf16[256,512]{1,0:T(8,128)(2,1)S(1)} %get-tuple-element.80.datt, ...), custom_call_target="tpu_custom_call" | custom-call | flops 15000000512 | bytes 15000000 | tf_op jit(solution)/shard_map/pallas_call | solution.py:423
  62.9 0.1 collective-permute-start.11
  63.0 1.5 %shard_map.104 = (f32[2,256,512]{2,1,0:T(8,128)S(1)}, f32[256,1024]{1,0:T(8,128)S(1)}) custom-call(bf16[256,512]{1,0:T(8,128)(2,1)S(1)} %get-tuple-element.66.q, bf16[256,512]{1,0:T(8,128)(2,1)S(1)} %copy-done.3, bf16[256,512]{1,0:T(8,128)(2,1)S(1)} %copy-done.5, bf16[256,512]{1,0:T(8,128)(2,1)S(1)} %get-tuple-element.80.datt, ...), custom_call_target="tpu_custom_call" | custom-call | flops 20000000000 | bytes 20000000 | tf_op jit(solution)/shard_map/pallas_call | solution.py:423
  64.6 0.9 %collective-permute-done.15.refs_3_ = f32[9,512]{1,0:T(8,128)S(1)} collective-permute-done((f32[9,512]{1,0:T(8,128)S(1)}, f32[9,512]{1,0:T(8,128)S(1)}, u32[]{:S(2)}, u32[]{:S(2)}) %collective-permute-start.15) | collective-permute-done | bytes 18464 | tf_op jit(solution)/shard_map/ppermute | solution.py:512
  65.5 0.0 collective-permute-done.14.refs_2_
  65.5 0.6 collective-permute-done.13.refs_1_
  66.1 9.0 %collective-permute-start.19 = (f32[9,512]{1,0:T(8,128)S(1)}, f32[9,512]{1,0:T(8,128)S(1)}, u32[]{:S(2)}, u32[]{:S(2)}) collective-permute-start(f32[9,512]{1,0:T(8,128)S(1)} %shard_map.105.after.refs_0_), channel_id=1, source_target_pairs={{0,192},{2,194},{4,196},{6,198},{8,200},{10,202},{12,204},{14,206}... | collective-permute-start | bytes 55304 | tf_op jit(solution)/shard_map/ppermute | solution.py:512
  75.1 0.6 collective-permute-start.18
  75.7 1.9 %collective-permute-start.17 = (f32[9,512]{1,0:T(8,128)S(1)}, f32[9,512]{1,0:T(8,128)S(1)}, u32[]{:S(2)}, u32[]{:S(2)}) collective-permute-start(f32[9,512]{1,0:T(8,128)S(1)} %shard_map.105.after.refs_0_), channel_id=1, source_target_pairs={{0,64},{2,66},{4,68},{6,70},{8,72},{10,74},{12,76},{14,78},{16,80}... | collective-permute-start | bytes 55304 | tf_op jit(solution)/shard_map/ppermute | solution.py:512
  77.6 0.0 collective-permute-done.12.got_b
  77.6 0.0 collective-permute-done.11.got_a
  77.6 0.9 shard_map.106
  78.5 2.0 %collective-permute-start.16 = (bf16[256,640]{1,0:T(8,128)(2,1)S(1)}, bf16[256,640]{1,0:T(8,128)(2,1)S(1)}, u32[]{:S(2)}, u32[]{:S(2)}) collective-permute-start(bf16[256,640]{1,0:T(8,128)(2,1)S(1)} %get-tuple-element.97), channel_id=1, source_target_pairs={{0,1},{1,0},{2,3},{3,2},{4,5},{5,4},{6,7},{7,6},{8,9},{9,8},{10,11... | collective-permute-start | bytes 983048 | tf_op jit(solution)/shard_map/ppermute | solution.py:440
  80.4 0.0 collective-permute-done.19.refs_3_
  80.5 2.5 %collective-permute-done.18.refs_2_ = f32[9,512]{1,0:T(8,128)S(1)} collective-permute-done((f32[9,512]{1,0:T(8,128)S(1)}, f32[9,512]{1,0:T(8,128)S(1)}, u32[]{:S(2)}, u32[]{:S(2)}) %collective-permute-start.18) | collective-permute-done | bytes 18464 | tf_op jit(solution)/shard_map/ppermute | solution.py:512
  82.9 0.0 collective-permute-done.17.refs_1_
  82.9 0.1 collective-permute-start.22
  83.0 0.1 collective-permute-start.21
  83.1 4.0 %collective-permute-start.20 = (f32[9,512]{1,0:T(8,128)S(1)}, f32[9,512]{1,0:T(8,128)S(1)}, u32[]{:S(2)}, u32[]{:S(2)}) collective-permute-start(f32[9,512]{1,0:T(8,128)S(1)} %shard_map.107.after.refs_0_), channel_id=1, source_target_pairs={{0,4},{2,6},{4,0},{6,2},{8,12},{10,14},{12,8},{14,10},{16,20},{18,... | collective-permute-start | bytes 55304 | tf_op jit(solution)/shard_map/ppermute | solution.py:512
  87.1 1.0 %collective-permute-done.22.refs_3_ = f32[9,512]{1,0:T(8,128)S(1)} collective-permute-done((f32[9,512]{1,0:T(8,128)S(1)}, f32[9,512]{1,0:T(8,128)S(1)}, u32[]{:S(2)}, u32[]{:S(2)}) %collective-permute-start.22) | collective-permute-done | bytes 18464 | tf_op jit(solution)/shard_map/ppermute | solution.py:512
  88.1 0.4 collective-permute-done.21.refs_2_
  88.5 0.8 collective-permute-done.20.refs_1_
  89.4 0.6 shard_map.109
  90.0 0.0 collective-permute-done.16.got
  90.0 1.1 %shard_map.108 = bf16[256,512]{1,0:T(8,128)(2,1)} custom-call(bf16[256,512]{1,0:T(8,128)(2,1)S(1)} %get-tuple-element.58.xo, bf16[256,512]{1,0:T(8,128)(2,1)S(1)} %collective-permute-done.xp, f32[256,512]{1,0:T(8,128)S(1)} %get-tuple-element.95.keep, f32[256,128]{1,0:T(8,128)S(1)} %get-tuple-element.96.stat, ...), custom_call_target="tpu_custom_call" | custom-call | flops 10000000000 | bytes 10000000 | tf_op jit(solution)/shard_map/pallas_call | solution.py:423
  (10 shorter events, 0.1 us)
Async XLA Ops:
  0.6 10.4 %collective-permute-start.1 = (bf16[256,512]{1,0:T(8,128)(2,1)}, bf16[256,512]{1,0:T(8,128)(2,1)S(1)}, u32[]{:S(2)}, u32[]{:S(2)}) collective-permute-start(bf16[256,512]{1,0:T(8,128)(2,1)} %refs_4_.1), channel_id=1, source_target_pairs={{0,2},{2,0},{4,6},{6,4},{8,10},{10,8},{12,14},{14,12},{16,18},{18,... | collective-permute-start | bytes 786440 | tf_op jit(solution)/shard_map/ppermute | solution.py:443
  0.7 10.4 %collective-permute-start = (bf16[256,512]{1,0:T(8,128)(2,1)}, bf16[256,512]{1,0:T(8,128)(2,1)S(1)}, u32[]{:S(2)}, u32[]{:S(2)}) collective-permute-start(bf16[256,512]{1,0:T(8,128)(2,1)} %refs_4_.1), channel_id=1, source_target_pairs={{0,1},{1,0},{2,3},{3,2},{4,5},{5,4},{6,7},{7,6},{8,9},{9,8},{10,11... | collective-permute-start | bytes 786440 | tf_op jit(solution)/shard_map/ppermute | solution.py:440
  2.9 15.8 %collective-permute-start.2 = (bf16[256,512]{1,0:T(8,128)(2,1)}, bf16[256,512]{1,0:T(8,128)(2,1)S(1)}, u32[]{:S(2)}, u32[]{:S(2)}) collective-permute-start(bf16[256,512]{1,0:T(8,128)(2,1)} %refs_4_.1), channel_id=1, source_target_pairs={{2,4},{6,8},{10,12},{14,16},{18,20},{22,24},{26,28},{30,32},{34,36... | collective-permute-start | bytes 786440 | tf_op jit(solution)/shard_map/ppermute | solution.py:447
  10.9 11.2 %copy-start = (bf16[1024,512]{1,0:T(8,128)(2,1)}, bf16[1024,512]{1,0:T(8,128)(2,1)S(1)}, u32[]{:S(2)}) copy-start(bf16[1024,512]{1,0:T(8,128)(2,1)S(1)} %get-tuple-element.65.wq) | copy-start | bytes 3145732
  10.9 11.2 %collective-permute-start.5 = (bf16[304,512]{1,0:T(8,128)(2,1)S(1)}, bf16[304,512]{1,0:T(8,128)(2,1)S(1)}, u32[]{:S(2)}, u32[]{:S(2)}) collective-permute-start(bf16[304,512]{1,0:T(8,128)(2,1)S(1)} %get-tuple-element.69), channel_id=1, source_target_pairs={{0,1},{1,0},{2,3},{3,2},{4,5},{5,4},{6,7},{7,6},{8,9},{9,8},{10,11... | collective-permute-start | bytes 933896 | tf_op jit(solution)/shard_map/ppermute | solution.py:440
  18.8 9.8 %collective-permute-start.4 = (bf16[256,512]{1,0:T(8,128)(2,1)S(1)}, bf16[256,512]{1,0:T(8,128)(2,1)S(1)}, u32[]{:S(2)}, u32[]{:S(2)}) collective-permute-start(bf16[256,512]{1,0:T(8,128)(2,1)S(1)} %collective-permute-done.xp), channel_id=1, source_target_pairs={{2,4},{6,8},{10,12},{14,16},{18,20},{22,24},{26,28},{30,32},{34,36... | collective-permute-start | bytes 786440 | tf_op jit(solution)/shard_map/ppermute | solution.py:447
  20.8 1.6 %collective-permute-start.3 = (bf16[256,512]{1,0:T(8,128)(2,1)S(1)}, bf16[256,512]{1,0:T(8,128)(2,1)S(1)}, u32[]{:S(2)}, u32[]{:S(2)}) collective-permute-start(bf16[256,512]{1,0:T(8,128)(2,1)S(1)} %collective-permute-done.xp), channel_id=1, source_target_pairs={{0,2},{2,0},{4,6},{6,4},{8,10},{10,8},{12,14},{14,12},{16,18},{18,... | collective-permute-start | bytes 786440 | tf_op jit(solution)/shard_map/ppermute | solution.py:443
  22.1 2.5 %copy-start.2 = (bf16[256,512]{1,0:T(8,128)(2,1)}, bf16[256,512]{1,0:T(8,128)(2,1)S(1)}, u32[]{:S(2)}) copy-start(bf16[256,512]{1,0:T(8,128)(2,1)S(1)} %get-tuple-element.67.k) | copy-start | bytes 786436
  22.1 2.5 %copy-start.4 = (bf16[256,512]{1,0:T(8,128)(2,1)}, bf16[256,512]{1,0:T(8,128)(2,1)S(1)}, u32[]{:S(2)}) copy-start(bf16[256,512]{1,0:T(8,128)(2,1)S(1)} %get-tuple-element.68.v) | copy-start | bytes 786436
  32.3 6.6 %collective-permute-start.7 = (bf16[32,1024]{1,0:T(8,128)(2,1)S(1)}, bf16[32,1024]{1,0:T(8,128)(2,1)S(1)}, u32[]{:S(2)}, u32[]{:S(2)}) collective-permute-start(bf16[32,1024]{1,0:T(8,128)(2,1)S(1)} %get-tuple-element.74.edges), channel_id=1, source_target_pairs={{0,1},{1,0},{2,3},{3,2},{4,5},{5,4},{6,7},{7,6},{8,9},{9,8},{10,11... | collective-permute-start | bytes 196616 | tf_op jit(solution)/shard_map/ppermute | solution.py:440
  32.8 16.4 %collective-permute-start.6 = (bf16[256,1024]{1,0:T(8,128)(2,1)S(1)}, bf16[256,1024]{1,0:T(8,128)(2,1)S(1)}, u32[]{:S(2)}, u32[]{:S(2)}) collective-permute-start(bf16[256,1024]{1,0:T(8,128)(2,1)S(1)} %shard_map.98.part), channel_id=1, source_target_pairs={{0,1},{1,0},{2,3},{3,2},{4,5},{5,4},{6,7},{7,6},{8,9},{9,8},{10,11... | collective-permute-start | bytes 1572872 | tf_op jit(solution)/shard_map/ppermute | solution.py:440
  38.9 2.0 %collective-permute-start.8 = (bf16[32,1024]{1,0:T(8,128)(2,1)S(1)}, bf16[32,1024]{1,0:T(8,128)(2,1)S(1)}, u32[]{:S(2)}, u32[]{:S(2)}) collective-permute-start(bf16[32,1024]{1,0:T(8,128)(2,1)S(1)} %get-tuple-element.76), channel_id=1, source_target_pairs={{0,2},{2,0},{4,6},{6,4},{8,10},{10,8},{12,14},{14,12},{16,18},{18,... | collective-permute-start | bytes 196616 | tf_op jit(solution)/shard_map/ppermute | solution.py:443
  39.0 10.2 %collective-permute-start.9 = (bf16[32,1024]{1,0:T(8,128)(2,1)S(1)}, bf16[32,1024]{1,0:T(8,128)(2,1)S(1)}, u32[]{:S(2)}, u32[]{:S(2)}) collective-permute-start(bf16[32,1024]{1,0:T(8,128)(2,1)S(1)} %get-tuple-element.77), channel_id=1, source_target_pairs={{2,4},{6,8},{10,12},{14,16},{18,20},{22,24},{26,28},{30,32},{34,36... | collective-permute-start | bytes 196616 | tf_op jit(solution)/shard_map/ppermute | solution.py:447
  53.9 4.1 %collective-permute-start.10 = (f32[9,512]{1,0:T(8,128)S(1)}, f32[9,512]{1,0:T(8,128)S(1)}, u32[]{:S(2)}, u32[]{:S(2)}) collective-permute-start(f32[9,512]{1,0:T(8,128)S(1)} %get-tuple-element.89.refs_0_), channel_id=1, source_target_pairs={{0,2},{2,0},{4,6},{6,4},{8,10},{10,8},{12,14},{14,12},{16,18},{18,... | collective-permute-start | bytes 55304 | tf_op jit(solution)/shard_map/ppermute | solution.py:512
  55.3 22.3 %collective-permute-start.12 = (bf16[2,256,512]{2,1,0:T(8,128)(2,1)S(1)}, bf16[2,256,512]{2,1,0:T(8,128)(2,1)S(1)}, u32[]{:S(2)}, u32[]{:S(2)}) collective-permute-start(bf16[2,256,512]{2,1,0:T(8,128)(2,1)S(1)} %get-tuple-element.93), channel_id=1, source_target_pairs={{2,4},{6,8},{10,12},{14,16},{18,20},{22,24},{26,28},{30,32},{34,36... | collective-permute-start | bytes 1572872 | tf_op jit(solution)/shard_map/ppermute | solution.py:447
  58.0 7.5 %collective-permute-start.15 = (f32[9,512]{1,0:T(8,128)S(1)}, f32[9,512]{1,0:T(8,128)S(1)}, u32[]{:S(2)}, u32[]{:S(2)}) collective-permute-start(f32[9,512]{1,0:T(8,128)S(1)} %shard_map.102.refs_1_.after.refs_0_), channel_id=1, source_target_pairs={{0,48},{2,50},{4,52},{6,54},{8,56},{10,58},{12,60},{14,62},{16,32}... | collective-permute-start | bytes 55304 | tf_op jit(solution)/shard_map/ppermute | solution.py:512
  58.1 7.4 %collective-permute-start.14 = (f32[9,512]{1,0:T(8,128)S(1)}, f32[9,512]{1,0:T(8,128)S(1)}, u32[]{:S(2)}, u32[]{:S(2)}) collective-permute-start(f32[9,512]{1,0:T(8,128)S(1)} %shard_map.102.refs_1_.after.refs_0_), channel_id=1, source_target_pairs={{0,32},{2,34},{4,36},{6,38},{8,40},{10,42},{12,44},{14,46},{16,48}... | collective-permute-start | bytes 55304 | tf_op jit(solution)/shard_map/ppermute | solution.py:512
  60.1 6.0 %collective-permute-start.13 = (f32[9,512]{1,0:T(8,128)S(1)}, f32[9,512]{1,0:T(8,128)S(1)}, u32[]{:S(2)}, u32[]{:S(2)}) collective-permute-start(f32[9,512]{1,0:T(8,128)S(1)} %shard_map.102.refs_1_.after.refs_0_), channel_id=1, source_target_pairs={{0,16},{2,18},{4,20},{6,22},{8,24},{10,26},{12,28},{14,30},{16,0},... | collective-permute-start | bytes 55304 | tf_op jit(solution)/shard_map/ppermute | solution.py:512
  61.6 1.4 %copy-start.1 = (bf16[1024,512]{1,0:T(8,128)(2,1)S(1)}, bf16[1024,512]{1,0:T(8,128)(2,1)}, u32[]{:S(2)}) copy-start(bf16[1024,512]{1,0:T(8,128)(2,1)} %copy-done) | copy-start | bytes 3145732
  61.6 1.4 %copy-start.3 = (bf16[256,512]{1,0:T(8,128)(2,1)S(1)}, bf16[256,512]{1,0:T(8,128)(2,1)}, u32[]{:S(2)}) copy-start(bf16[256,512]{1,0:T(8,128)(2,1)} %copy-done.2) | copy-start | bytes 786436
  61.6 1.4 %copy-start.5 = (bf16[256,512]{1,0:T(8,128)(2,1)S(1)}, bf16[256,512]{1,0:T(8,128)(2,1)}, u32[]{:S(2)}) copy-start(bf16[256,512]{1,0:T(8,128)(2,1)} %copy-done.4) | copy-start | bytes 786436
  62.9 14.7 %collective-permute-start.11 = (bf16[2,256,512]{2,1,0:T(8,128)(2,1)S(1)}, bf16[2,256,512]{2,1,0:T(8,128)(2,1)S(1)}, u32[]{:S(2)}, u32[]{:S(2)}) collective-permute-start(bf16[2,256,512]{2,1,0:T(8,128)(2,1)S(1)} %get-tuple-element.92), channel_id=1, source_target_pairs={{0,2},{2,0},{4,6},{6,4},{8,10},{10,8},{12,14},{14,12},{16,18},{18,... | collective-permute-start | bytes 1572872 | tf_op jit(solution)/shard_map/ppermute | solution.py:443
  66.1 14.3 %collective-permute-start.19 = (f32[9,512]{1,0:T(8,128)S(1)}, f32[9,512]{1,0:T(8,128)S(1)}, u32[]{:S(2)}, u32[]{:S(2)}) collective-permute-start(f32[9,512]{1,0:T(8,128)S(1)} %shard_map.105.after.refs_0_), channel_id=1, source_target_pairs={{0,192},{2,194},{4,196},{6,198},{8,200},{10,202},{12,204},{14,206}... | collective-permute-start | bytes 55304 | tf_op jit(solution)/shard_map/ppermute | solution.py:512
  75.1 7.8 %collective-permute-start.18 = (f32[9,512]{1,0:T(8,128)S(1)}, f32[9,512]{1,0:T(8,128)S(1)}, u32[]{:S(2)}, u32[]{:S(2)}) collective-permute-start(f32[9,512]{1,0:T(8,128)S(1)} %shard_map.105.after.refs_0_), channel_id=1, source_target_pairs={{0,128},{2,130},{4,132},{6,134},{8,136},{10,138},{12,140},{14,142}... | collective-permute-start | bytes 55304 | tf_op jit(solution)/shard_map/ppermute | solution.py:512
  75.7 7.3 %collective-permute-start.17 = (f32[9,512]{1,0:T(8,128)S(1)}, f32[9,512]{1,0:T(8,128)S(1)}, u32[]{:S(2)}, u32[]{:S(2)}) collective-permute-start(f32[9,512]{1,0:T(8,128)S(1)} %shard_map.105.after.refs_0_), channel_id=1, source_target_pairs={{0,64},{2,66},{4,68},{6,70},{8,72},{10,74},{12,76},{14,78},{16,80}... | collective-permute-start | bytes 55304 | tf_op jit(solution)/shard_map/ppermute | solution.py:512
  78.5 11.5 %collective-permute-start.16 = (bf16[256,640]{1,0:T(8,128)(2,1)S(1)}, bf16[256,640]{1,0:T(8,128)(2,1)S(1)}, u32[]{:S(2)}, u32[]{:S(2)}) collective-permute-start(bf16[256,640]{1,0:T(8,128)(2,1)S(1)} %get-tuple-element.97), channel_id=1, source_target_pairs={{0,1},{1,0},{2,3},{3,2},{4,5},{5,4},{6,7},{7,6},{8,9},{9,8},{10,11... | collective-permute-start | bytes 983048 | tf_op jit(solution)/shard_map/ppermute | solution.py:440
  82.9 5.2 %collective-permute-start.22 = (f32[9,512]{1,0:T(8,128)S(1)}, f32[9,512]{1,0:T(8,128)S(1)}, u32[]{:S(2)}, u32[]{:S(2)}) collective-permute-start(f32[9,512]{1,0:T(8,128)S(1)} %shard_map.107.after.refs_0_), channel_id=1, source_target_pairs={{0,12},{2,14},{4,8},{6,10},{8,4},{10,6},{12,0},{14,2},{16,28},{18,... | collective-permute-start | bytes 55304 | tf_op jit(solution)/shard_map/ppermute | solution.py:512
  83.0 5.5 %collective-permute-start.21 = (f32[9,512]{1,0:T(8,128)S(1)}, f32[9,512]{1,0:T(8,128)S(1)}, u32[]{:S(2)}, u32[]{:S(2)}) collective-permute-start(f32[9,512]{1,0:T(8,128)S(1)} %shard_map.107.after.refs_0_), channel_id=1, source_target_pairs={{0,8},{2,10},{4,12},{6,14},{8,0},{10,2},{12,4},{14,6},{16,24},{18,... | collective-permute-start | bytes 55304 | tf_op jit(solution)/shard_map/ppermute | solution.py:512
  83.1 6.2 %collective-permute-start.20 = (f32[9,512]{1,0:T(8,128)S(1)}, f32[9,512]{1,0:T(8,128)S(1)}, u32[]{:S(2)}, u32[]{:S(2)}) collective-permute-start(f32[9,512]{1,0:T(8,128)S(1)} %shard_map.107.after.refs_0_), channel_id=1, source_target_pairs={{0,4},{2,6},{4,0},{6,2},{8,12},{10,14},{12,8},{14,10},{16,20},{18,... | collective-permute-start | bytes 55304 | tf_op jit(solution)/shard_map/ppermute | solution.py:512

commit v3 on v2

--- a/solution.py
+++ b/solution.py
@@ -103,49 +103,32 @@
         out[...] = (nn(no, w[own, :]) + nn(np_, w[other, :])).astype(BF16)
 
 
-def first_kernel(xo, xp, wk, wv, q, k, v, pack, ka, va, e, acc, top, total):
-    halo_kv(xo, xp, wk, wv, ka, va)
-    odd, _, _ = placement()
-    bias = band_bias(1 - odd, 1)
+def attend_kernel(a0, a1, b0, b1, wk, wv, wo, q, k, v, ka, va, kb, vb, p, att, edges):
+    halo_kv(a0, a1, wk, wv, ka, va)
+    halo_kv(b0, b1, wk, wv, kb, vb)
+    odd, left, right = placement()
+    bias_a = band_bias(1 - odd, 1)
+    bias_b = band_bias(odd, jnp.where(odd == 1, right, left))
     for head in range(HEADS):
         f = lanes_of(head)
         qh = q[:, f]
-        s_own = nt(qh, k[:, f]) * SCALE
-        s_a = nt(qh, ka[:, f]) * SCALE + bias
-        m = jnp.maximum(jnp.max(s_own, axis=1, keepdims=True), jnp.max(s_a, axis=1, keepdims=True))
-        e_own = jnp.exp(s_own - m)
-        e_a = jnp.exp(s_a - m)
-        total[head] = jnp.broadcast_to(row_sum(e_own) + row_sum(e_a), (ROWS, LANES))
-        top[head] = jnp.broadcast_to(m, (ROWS, LANES))
-        e_own = e_own.astype(BF16)
-        e_a = e_a.astype(BF16)
-        e[head, :, :ROWS] = e_own
-        e[head, :, ROWS:] = e_a
-        acc[:, f] = nn(e_own, v[:, f]) + nn(e_a, va[:, f])
-
-
-def second_kernel(
-    xo, xp, wk, wv, wo, q, acc, top, total, kb, vb, e, weight, att, edges
-):
-    halo_kv(xo, xp, wk, wv, kb, vb)
-    odd, left, right = placement()
-    bias = band_bias(odd, jnp.where(odd == 1, right, left))
-    for head in range(HEADS):
-        f = lanes_of(head)
-        s = nt(q[:, f], kb[:, f]) * SCALE + bias
-        m1 = top[head][:, :1]
-        m = jnp.maximum(m1, jnp.max(s, axis=1, keepdims=True))
-        shrink = jnp.exp(m1 - m)
-        eb = jnp.exp(s - m)
-        inverse = 1.0 / (total[head][:, :1] * shrink + row_sum(eb))
-        eb = eb.astype(BF16)
-        e[head] = eb
-        o = (acc[:, f] * shrink + nn(eb, vb[:, f])) * inverse
-        att[:, f] = o.astype(BF16)
-        weight[0, head] = jnp.broadcast_to(shrink * inverse, (ROWS, LANES))
-        weight[1, head] = jnp.broadcast_to(inverse, (ROWS, LANES))
-    own, other = own_other()
-    rim = jnp.concatenate([att[at, :] for at in edge_rows(placement()[0])], axis=0)
+        scores = (
+            nt(qh, k[:, f]) * SCALE,
+            nt(qh, ka[:, f]) * SCALE + bias_a,
+            nt(qh, kb[:, f]) * SCALE + bias_b,
+        )
+        top = functools.reduce(jnp.maximum, scores)
+        top = jnp.max(top, axis=1, keepdims=True)
+        scores = [jnp.exp(s - top) for s in scores]
+        inverse = 1.0 / row_sum(sum(scores))
+        out = 0.0
+        for n, (s, values) in enumerate(zip(scores, (v, va, vb))):
+            s = (s * inverse).astype(BF16)
+            p[head, :, n * ROWS:(n + 1) * ROWS] = s
+            out = out + nn(s, values[:, f])
+        att[:, f] = out.astype(BF16)
+    own, other = own_other()
+    rim = jnp.concatenate([att[at, :] for at in edge_rows(odd)], axis=0)
     edges[:, :SHARE] = nn(rim, wo[:, own]).astype(BF16)
     edges[:, SHARE:] = nn(rim, wo[:, other]).astype(BF16)
 
@@ -303,37 +286,32 @@
     datt[...] = (nt(dhb[:, :SHARE], wo[:, own]) + nt(dhb[:, SHARE:], wo[:, other])).astype(BF16)
 
 
-def pair_grad(qh, kh, vh, gh, eh, wh, delta):
+def pair_grad(qh, kh, vh, gh, p, delta):
     dots = nt(gh, vh)
-    p = eh.astype(F32) * wh
-    ds = (p * (dots - delta) * SCALE).astype(BF16)
-    return nn(ds, kh), tn(ds, qh), tn(p.astype(BF16), gh)
-
-
-def back_halo_kernel(q, k, v, datt, att, e, weight, *refs, which):
+    ds = (p.astype(F32) * (dots - delta) * SCALE).astype(BF16)
+    return nn(ds, kh), tn(ds, qh), tn(p, gh)
+
+
+def back_halo_kernel(q, k, v, datt, att, p, *refs, which):
     dq, dkv = refs[-2:]
-    at = pl.ds(ROWS, ROWS) if which == 0 else pl.ds(0, ROWS)
+    at = slice(which * ROWS, (which + 1) * ROWS)
     for head in range(HEADS):
         f = lanes_of(head)
         gh = datt[:, f]
         delta = row_sum(gh.astype(F32) * att[:, f].astype(F32))
-        d_q, d_k, d_v = pair_grad(
-            q[:, f], k[:, f], v[:, f], gh, e[head, :, at], weight[which, head][:, :1], delta
-        )
-        dq[:, f] = d_q + refs[0][:, f] if which == 0 else d_q
+        d_q, d_k, d_v = pair_grad(q[:, f], k[:, f], v[:, f], gh, p[head, :, at], delta)
+        dq[:, f] = d_q + refs[0][:, f] if which == 1 else d_q
         dkv[0, :, f] = d_k.astype(BF16)
         dkv[1, :, f] = d_v.astype(BF16)
 
 
-def back_own_kernel(q, k, v, datt, att, e, weight, dq_ab, wq, after, dkv, pin):
+def back_own_kernel(q, k, v, datt, att, p, dq_ab, wq, after, dkv, pin):
     dq = []
     for head in range(HEADS):
         f = lanes_of(head)
         gh = datt[:, f]
         delta = row_sum(gh.astype(F32) * att[:, f].astype(F32))
-        d_q, d_k, d_v = pair_grad(
-            q[:, f], k[:, f], v[:, f], gh, e[head, :, :ROWS], weight[0, head][:, :1], delta
-        )
+        d_q, d_k, d_v = pair_grad(q[:, f], k[:, f], v[:, f], gh, p[head, :, :ROWS], delta)
         dkv[0, :, f] = d_k
         dkv[1, :, f] = d_v
         dq.append((d_q + dq_ab[:, f]).astype(BF16))
@@ -447,37 +425,30 @@
         return lax.ppermute(value, "tm", pairs + [(j, i) for i, j in pairs])
 
     big = ((ROWS, SHARE), BF16)
-    state = ((HEADS, ROWS, LANES), F32)
+    def over_b_and_head(value):
+        pairs = [(i, i + 1) for i in range(1, count - 1, 2)]
+        pairs = pairs + [(j, i) for i, j in pairs]
+        crossed = [(2 * i + h, 2 * j + 1 - h) for i, j in pairs for h in range(2)]
+        return lax.ppermute(value, ("tm", "head"), crossed)
+
     xp = over_head(inputs)
     b0 = over_b(inputs)
+    b1 = over_b_and_head(inputs)
     a0 = over_a(inputs)
     *staged, pack = stage(w_query, w_key, w_value, w_out, inputs, cotangent, kernel)
-    pack_p = over_head(pack)
-    xp, a0, b0, *staged = lax.optimization_barrier((xp, a0, b0, *staged))
+    xp, a0, *staged = lax.optimization_barrier((xp, a0, *staged))
     w_query, w_key, w_value, w_out, inputs, cotangent, kernel = staged
-    b1 = over_b(xp)
     a1 = over_a(xp)
     q, k, v = call(
-        own_kernel, (inputs, xp, w_query, w_key, w_value), (big, big, big), us=2.0
-    )
-    ka, va, e_one, acc, top, total = call(
-        first_kernel,
-        (a0, a1, w_key, w_value, q, k, v, pack_p),
-        (big, big, ((HEADS, ROWS, 2 * ROWS), BF16), ((ROWS, SHARE), F32), state, state),
-        us=3.0,
-    )
+        own_kernel, (inputs, xp, w_query, w_key, w_value), (big, big, big), us=0.0
+    )
+    q, pack = lax.optimization_barrier((q, pack))
+    pack_p = over_head(pack)
     edge = ((2 * EDGE, D), BF16)
-    kb, vb, e_two, weight, att, edges = call(
-        second_kernel,
-        (b0, b1, w_key, w_value, w_out, q, acc, top, total),
-        (
-            big,
-            big,
-            ((HEADS, ROWS, ROWS), BF16),
-            ((2, HEADS, ROWS, LANES), F32),
-            big,
-            edge,
-        ),
+    ka, va, kb, vb, probs, att, edges = call(
+        attend_kernel,
+        (a0, a1, b0, b1, w_key, w_value, w_out, q, k, v),
+        (big, big, big, big, ((HEADS, ROWS, 3 * ROWS), BF16), big, edge),
         us=4.0,
     )
     edges_p = over_head(edges)
@@ -506,7 +477,7 @@
     )
     chain = [gk]
     assert count == 128
-    for steps in ((1,), (8, 16, 24), (32, 64, 96), (2, 4, 6)):
+    for steps in ((1,), (32, 64, 96), (8, 16, 24), (2, 4, 6)):
         last = chain[-1]
         parts = [
             lax.ppermute(last, "tm", [(i, i ^ step) for i in range(count)]) for step in steps
@@ -514,22 +485,22 @@
         chain.extend(call(sum_kernel, (last, *parts), (((KW, SHARE), F32),), us=0.2, mib=1))
     pair = ((2, ROWS, SHARE), BF16)
     dq_b, dkv_b = call(
-        functools.partial(back_halo_kernel, which=1),
-        (q, kb, vb, datt, att, e_two, weight),
+        functools.partial(back_halo_kernel, which=2),
+        (q, kb, vb, datt, att, probs),
         (((ROWS, SHARE), F32), pair),
         us=1.5,
     )
     got_b = over_b(dkv_b)
     dq_ab, dkv_a = call(
-        functools.partial(back_halo_kernel, which=0),
-        (q, ka, va, datt, att, e_one, weight, dq_b, chain[1]),
+        functools.partial(back_halo_kernel, which=1),
+        (q, ka, va, datt, att, probs, dq_b, chain[1]),
         (((ROWS, SHARE), F32), pair),
         us=1.5,
     )
     got_a = over_a(dkv_a)
     dkv, pin = call(
         back_own_kernel,
-        (q, k, v, datt, att, e_one, weight, dq_ab, w_query, chain[1]),
+        (q, k, v, datt, att, probs, dq_ab, w_query, chain[1]),
         (((2, ROWS, SHARE), F32), ((ROWS, D), F32)),
         us=2.0,
     )

time: 91.6 us -> 83.1 us (0.907)
  waiting for transfers between devices: 29 us -> 23.4 us
  Pallas kernels: 21.4 us -> 19.1 us
    ppermute x4 -> x3, waiting for transfers between devices: 19.8 us -> 9.21 us  [over_b(): return lax.ppermute(value, 'tm', pairs + [(j, i) for i, j in pairs])]
    ppermute x0 -> x1, waiting for transfers between devices: none -> 4.61 us  [over_b_and_head(): return lax.ppermute(value, ('tm', 'head'), crossed)]
    ppermute x0 -> x1, starting transfers between devices: none -> 3.97 us  [over_b_and_head(): return lax.ppermute(value, ('tm', 'head'), crossed)]
    ppermute x4 -> x3, starting transfers between devices: 12.2 us -> 8.42 us  [over_b(): return lax.ppermute(value, 'tm', pairs + [(j, i) for i, j in pairs])]
    pallas_call x15 -> x14, Pallas kernels: 19 us -> 16.7 us  [call(): pl.pallas_call(kernel, out_shape=[jax.ShapeDtypeStruct(shape, dtype) for...]
  transfers between devices with their start and end apart: 23 -> 23, of which waited for: 12 -> 9; matrix products, arithmetic and copies ran while one was open for 0% -> 0% of each run, Pallas kernels for 13% -> 16%
where the time goes in v3:
time: 83.1 us; the launch traced here: 82.7 us
  starting transfers between devices  39.4 us (47%)
  waiting for transfers between devices  23.4 us (28%)
  Pallas kernels  19.1 us (23%)
  between operations  0.85 us (1%)
    ppermute x10, starting transfers between devices, local(): lax.ppermute(last, 'tm', [(i, i ^ step) for i in range(count)])  18.5 us
    pallas_call x14, Pallas kernels, call(): pl.pallas_call(kernel, out_shape=[jax.ShapeDtypeStruct(shape, dtype) for...  16.7 us
    ppermute x3, waiting for transfers between devices, over_b(): return lax.ppermute(value, 'tm', pairs + [(j, i) for i, j in pairs])  9.21 us
    ppermute x3, starting transfers between devices, over_b(): return lax.ppermute(value, 'tm', pairs + [(j, i) for i, j in pairs])  8.42 us
    ppermute x5, starting transfers between devices, over_head(): return lax.ppermute(value, 'head', [(0, 1), (1, 0)])  8.11 us
    ppermute x10, waiting for transfers between devices, local(): lax.ppermute(last, 'tm', [(i, i ^ step) for i in range(count)])  7.09 us
    ppermute x1, waiting for transfers between devices, over_b_and_head(): return lax.ppermute(value, ('tm', 'head'), crossed)  4.61 us
    ppermute x1, starting transfers between devices, over_b_and_head(): return lax.ppermute(value, ('tm', 'head'), crossed)  3.97 us
  transfers between devices with their start and end apart: 23, of which 9 were waited for; matrix products, arithmetic and copies ran while one was open for 0% of the time, Pallas kernels for 16%

profile of v3, /device:TPU:2, one launch (start us, length us, event | category | flops | bytes accessed | tf_op | source)
XLA Modules:
  0.0 82.7 jit_solution(17860214061542243098)
XLA Ops:
  0.6 0.1 collective-permute-start.1
  0.7 2.2 %collective-permute-start = (bf16[256,512]{1,0:T(8,128)(2,1)}, bf16[256,512]{1,0:T(8,128)(2,1)S(1)}, u32[]{:S(2)}, u32[]{:S(2)}) collective-permute-start(bf16[256,512]{1,0:T(8,128)(2,1)} %refs_4_.1), channel_id=1, source_target_pairs={{0,1},{1,0},{2,3},{3,2},{4,5},{5,4},{6,7},{7,6},{8,9},{9,8},{10,11... | collective-permute-start | bytes 786440 | tf_op jit(solution)/shard_map/ppermute | solution.py:418
  2.9 4.0 %collective-permute-start.4 = (bf16[256,512]{1,0:T(8,128)(2,1)}, bf16[256,512]{1,0:T(8,128)(2,1)S(1)}, u32[]{:S(2)}, u32[]{:S(2)}) collective-permute-start(bf16[256,512]{1,0:T(8,128)(2,1)} %refs_4_.1), channel_id=1, source_target_pairs={{2,5},{3,4},{6,9},{7,8},{10,13},{11,12},{14,17},{15,16},{18,21},{1... | collective-permute-start | bytes 786440 | tf_op jit(solution)/shard_map/ppermute | solution.py:432
  6.9 4.2 %collective-permute-start.3 = (bf16[256,512]{1,0:T(8,128)(2,1)}, bf16[256,512]{1,0:T(8,128)(2,1)S(1)}, u32[]{:S(2)}, u32[]{:S(2)}) collective-permute-start(bf16[256,512]{1,0:T(8,128)(2,1)} %refs_4_.1), channel_id=1, source_target_pairs={{2,4},{6,8},{10,12},{14,16},{18,20},{22,24},{26,28},{30,32},{34,36... | collective-permute-start | bytes 786440 | tf_op jit(solution)/shard_map/ppermute | solution.py:425
  11.2 2.4 %shard_map.94 = (bf16[1024,512]{1,0:T(8,128)(2,1)S(1)}, bf16[1024,512]{1,0:T(8,128)(2,1)S(1)}, bf16[1024,512]{1,0:T(8,128)(2,1)S(1)}, bf16[512,1024]{1,0:T(8,128...) custom-call(bf16[1024,512]{1,0:T(8,128)(2,1)} %refs_0_.1, ...), custom_call_target="tpu_custom_call" | custom-call | bytes 67108864 | tf_op jit(solution)/shard_map/pallas_call | solution.py:388
  13.6 0.0 copy-start
  13.6 0.0 collective-permute-done.1.a0
  13.6 0.0 collective-permute-done.xp
  13.6 0.1 collective-permute-start.2
  13.7 1.1 %shard_map.95 = (bf16[256,512]{1,0:T(8,128)(2,1)S(1)}, bf16[256,512]{1,0:T(8,128)(2,1)S(1)}, bf16[256,512]{1,0:T(8,128)(2,1)S(1)}) custom-call(bf16[256,512]{1,0:T(8,128)(2,1)S(1)} %get-tuple-element.54.xo, bf16[256,512]{1,0:T(8,128)(2,1)S(1)} %collective-permute-done.xp, bf16[1024,512]{1,0:T(8,128)(2,1)S(1)} %get-tuple-element.60.wq, ...), custom_call_target="tpu_custom_call" | custom-call | tf_op jit(solution)/shard_map/pallas_call | solution.py:401
  14.8 0.0 copy-done
  14.8 1.4 %collective-permute-start.7 = (bf16[304,512]{1,0:T(8,128)(2,1)S(1)}, bf16[304,512]{1,0:T(8,128)(2,1)S(1)}, u32[]{:S(2)}, u32[]{:S(2)}) collective-permute-start(bf16[304,512]{1,0:T(8,128)(2,1)S(1)} %get-tuple-element.69), channel_id=1, source_target_pairs={{0,1},{1,0},{2,3},{3,2},{4,5},{5,4},{6,7},{7,6},{8,9},{9,8},{10,11... | collective-permute-start | bytes 933896 | tf_op jit(solution)/shard_map/ppermute | solution.py:418
  16.2 4.6 %collective-permute-done.4.b1 = bf16[256,512]{1,0:T(8,128)(2,1)S(1)} collective-permute-done((bf16[256,512]{1,0:T(8,128)(2,1)}, bf16[256,512]{1,0:T(8,128)(2,1)S(1)}, u32[]{:S(2)}, u32[]{:S(2)}) %collective-permute-start.4) | collective-permute-done | bytes 262176 | tf_op jit(solution)/shard_map/ppermute | solution.py:432
  20.9 0.0 collective-permute-done.3.b0
  20.9 0.0 collective-permute-done.2.a1
  20.9 3.8 %shard_map.96 = (bf16[256,512]{1,0:T(8,128)(2,1)S(1)}, bf16[256,512]{1,0:T(8,128)(2,1)S(1)}, bf16[256,512]{1,0:T(8,128)(2,1)S(1)}, bf16[256,512]{1,0:T(8,128)(2,...) custom-call(bf16[256,512]{1,0:T(8,128)(2,1)S(1)} %collective-permute-done.1.a0,, ...), custom_call_target="tpu_custom_call" | custom-call | flops 40000000000 | bytes 40000000 | tf_op jit(solution)/shard_map/pallas_call | solution.py:401
  24.6 2.5 %collective-permute-start.6 = (bf16[32,1024]{1,0:T(8,128)(2,1)S(1)}, bf16[32,1024]{1,0:T(8,128)(2,1)S(1)}, u32[]{:S(2)}, u32[]{:S(2)}) collective-permute-start(bf16[32,1024]{1,0:T(8,128)(2,1)S(1)} %get-tuple-element.67.edges), channel_id=1, source_target_pairs={{0,1},{1,0},{2,3},{3,2},{4,5},{5,4},{6,7},{7,6},{8,9},{9,8},{10,11... | collective-permute-start | bytes 196616 | tf_op jit(solution)/shard_map/ppermute | solution.py:418
  27.1 0.4 shard_map.97.part
  27.5 1.2 %collective-permute-start.5 = (bf16[256,1024]{1,0:T(8,128)(2,1)S(1)}, bf16[256,1024]{1,0:T(8,128)(2,1)S(1)}, u32[]{:S(2)}, u32[]{:S(2)}) collective-permute-start(bf16[256,1024]{1,0:T(8,128)(2,1)S(1)} %shard_map.97.part), channel_id=1, source_target_pairs={{0,1},{1,0},{2,3},{3,2},{4,5},{5,4},{6,7},{7,6},{8,9},{9,8},{10,11... | collective-permute-start | bytes 1572872 | tf_op jit(solution)/shard_map/ppermute | solution.py:418
  28.8 0.0 collective-permute-done.7.cp
  28.8 2.4 %collective-permute-done.6.edges_p = bf16[32,1024]{1,0:T(8,128)(2,1)S(1)} collective-permute-done((bf16[32,1024]{1,0:T(8,128)(2,1)S(1)}, bf16[32,1024]{1,0:T(8,128)(2,1)S(1)}, u32[]{:S(2)}, u32[]{:S(2)}) %collective-permute-start.6) | collective-permute-done | bytes 65568 | tf_op jit(solution)/shard_map/ppermute | solution.py:418
  31.2 0.1 collective-permute-start.8
  31.3 1.9 %collective-permute-start.9 = (bf16[32,1024]{1,0:T(8,128)(2,1)S(1)}, bf16[32,1024]{1,0:T(8,128)(2,1)S(1)}, u32[]{:S(2)}, u32[]{:S(2)}) collective-permute-start(bf16[32,1024]{1,0:T(8,128)(2,1)S(1)} %get-tuple-element.71), channel_id=1, source_target_pairs={{2,4},{6,8},{10,12},{14,16},{18,20},{22,24},{26,28},{30,32},{34,36... | collective-permute-start | bytes 196616 | tf_op jit(solution)/shard_map/ppermute | solution.py:425
  33.2 0.0 collective-permute-done.8.ea
  33.2 9.2 %collective-permute-done.9.eb = bf16[32,1024]{1,0:T(8,128)(2,1)S(1)} collective-permute-done((bf16[32,1024]{1,0:T(8,128)(2,1)S(1)}, bf16[32,1024]{1,0:T(8,128)(2,1)S(1)}, u32[]{:S(2)}, u32[]{:S(2)}) %collective-permute-start.9) | collective-permute-done | bytes 65568 | tf_op jit(solution)/shard_map/ppermute | solution.py:425
  42.4 0.0 collective-permute-done.5.part_p
  42.4 4.7 %shard_map.99 = (bf16[256,512]{1,0:T(8,128)(2,1)}, f32[256,512]{1,0:T(8,128)S(1)}, bf16[256,512]{1,0:T(8,128)(2,1)S(1)}, f32[9,512]{1,0:T(8,128)S(1)}) custom-call(bf16[256,512]{1,0:T(8,128)(2,1)S(1)} %get-tuple-element.54.xo, bf16[256,512]{1,0:T(8,128)(2,1)S(1)} %collective-permute-done.xp, bf16[256,512]{1,0:T(8,128)(2,1)S(1)} %collective-permute-done.1.a0, ...), custom_call_target="tpu_custom_call" | custom-call | flops 49999998976 | bytes 50000000 | tf_op jit(solution)/shard_map/pallas_call | solution.py:401
  47.1 0.0 collective-permute-start.10
  47.1 1.4 %shard_map.100 = (f32[256,512]{1,0:T(8,128)S(1)}, bf16[2,256,512]{2,1,0:T(8,128)(2,1)S(1)}) custom-call(bf16[256,512]{1,0:T(8,128)(2,1)S(1)} %get-tuple-element.63.q, bf16[256,512]{1,0:T(8,128)(2,1)S(1)} %get-tuple-element.78.k, bf16[256,512]{1,0:T(8,128)(2,1)S(1)} %get-tuple-element.79.v, bf16[256,512]{1,0:T(8,128)(2,1)S(1)} %get-tuple-element.74.datt, ...), custom_call_target="tpu_custom_call" | custom-call | flops 15000000512 | bytes 15000000 | tf_op jit(solution)/shard_map/pallas_call | solution.py:401
  48.5 2.3 %collective-permute-start.12 = (bf16[2,256,512]{2,1,0:T(8,128)(2,1)S(1)}, bf16[2,256,512]{2,1,0:T(8,128)(2,1)S(1)}, u32[]{:S(2)}, u32[]{:S(2)}) collective-permute-start(bf16[2,256,512]{2,1,0:T(8,128)(2,1)S(1)} %get-tuple-element.85), channel_id=1, source_target_pairs={{2,4},{6,8},{10,12},{14,16},{18,20},{22,24},{26,28},{30,32},{34,36... | collective-permute-start | bytes 1572872 | tf_op jit(solution)/shard_map/ppermute | solution.py:425
  50.7 0.0 collective-permute-done.10.refs_1_
  50.8 6.6 %collective-permute-start.15 = (f32[9,512]{1,0:T(8,128)S(1)}, f32[9,512]{1,0:T(8,128)S(1)}, u32[]{:S(2)}, u32[]{:S(2)}) collective-permute-start(f32[9,512]{1,0:T(8,128)S(1)} %shard_map.101.refs_1_.after.refs_0_), channel_id=1, source_target_pairs={{0,192},{2,194},{4,196},{6,198},{8,200},{10,202},{12,204},{14,206}... | collective-permute-start | bytes 55304 | tf_op jit(solution)/shard_map/ppermute | solution.py:483
  57.3 1.0 %collective-permute-start.14 = (f32[9,512]{1,0:T(8,128)S(1)}, f32[9,512]{1,0:T(8,128)S(1)}, u32[]{:S(2)}, u32[]{:S(2)}) collective-permute-start(f32[9,512]{1,0:T(8,128)S(1)} %shard_map.101.refs_1_.after.refs_0_), channel_id=1, source_target_pairs={{0,128},{2,130},{4,132},{6,134},{8,136},{10,138},{12,140},{14,142}... | collective-permute-start | bytes 55304 | tf_op jit(solution)/shard_map/ppermute | solution.py:483
  58.3 1.5 %collective-permute-start.13 = (f32[9,512]{1,0:T(8,128)S(1)}, f32[9,512]{1,0:T(8,128)S(1)}, u32[]{:S(2)}, u32[]{:S(2)}) collective-permute-start(f32[9,512]{1,0:T(8,128)S(1)} %shard_map.101.refs_1_.after.refs_0_), channel_id=1, source_target_pairs={{0,64},{2,66},{4,68},{6,70},{8,72},{10,74},{12,76},{14,78},{16,80}... | collective-permute-start | bytes 55304 | tf_op jit(solution)/shard_map/ppermute | solution.py:483
  59.8 0.0 copy-start.1
  59.8 1.2 %shard_map.102 = (f32[256,512]{1,0:T(8,128)S(1)}, bf16[2,256,512]{2,1,0:T(8,128)(2,1)S(1)}) custom-call(bf16[256,512]{1,0:T(8,128)(2,1)S(1)} %get-tuple-element.63.q, bf16[256,512]{1,0:T(8,128)(2,1)S(1)} %get-tuple-element.76.k, bf16[256,512]{1,0:T(8,128)(2,1)S(1)} %get-tuple-element.77.v, bf16[256,512]{1,0:T(8,128)(2,1)S(1)} %get-tuple-element.74.datt, ...), custom_call_target="tpu_custom_call" | custom-call | flops 15000000512 | bytes 15000000 | tf_op jit(solution)/shard_map/pallas_call | solution.py:401
  61.0 0.1 collective-permute-start.11
  61.1 0.0 copy-done.1
  61.1 1.5 %shard_map.103 = (f32[2,256,512]{2,1,0:T(8,128)S(1)}, f32[256,1024]{1,0:T(8,128)S(1)}) custom-call(bf16[256,512]{1,0:T(8,128)(2,1)S(1)} %get-tuple-element.63.q, bf16[256,512]{1,0:T(8,128)(2,1)S(1)} %get-tuple-element.64.k, bf16[256,512]{1,0:T(8,128)(2,1)S(1)} %get-tuple-element.65.v, bf16[256,512]{1,0:T(8,128)(2,1)S(1)} %get-tuple-element.74.datt, ...), custom_call_target="tpu_custom_call" | custom-call | flops 20000000000 | bytes 20000000 | tf_op jit(solution)/shard_map/pallas_call | solution.py:401
  62.6 0.0 collective-permute-done.15.refs_3_
  62.6 2.9 %collective-permute-done.14.refs_2_ = f32[9,512]{1,0:T(8,128)S(1)} collective-permute-done((f32[9,512]{1,0:T(8,128)S(1)}, f32[9,512]{1,0:T(8,128)S(1)}, u32[]{:S(2)}, u32[]{:S(2)}) %collective-permute-start.14) | collective-permute-done | bytes 18464 | tf_op jit(solution)/shard_map/ppermute | solution.py:483
  65.5 0.0 collective-permute-done.13.refs_1_
  65.5 4.6 %collective-permute-start.19 = (f32[9,512]{1,0:T(8,128)S(1)}, f32[9,512]{1,0:T(8,128)S(1)}, u32[]{:S(2)}, u32[]{:S(2)}) collective-permute-start(f32[9,512]{1,0:T(8,128)S(1)} %shard_map.104.after.refs_0_), channel_id=1, source_target_pairs={{0,48},{2,50},{4,52},{6,54},{8,56},{10,58},{12,60},{14,62},{16,32}... | collective-permute-start | bytes 55304 | tf_op jit(solution)/shard_map/ppermute | solution.py:483
  70.2 0.0 collective-permute-start.18
  70.2 0.7 collective-permute-start.17
  70.8 0.0 collective-permute-done.12.got_b
  70.8 0.0 collective-permute-done.11.got_a
  70.8 0.9 %shard_map.105 = (bf16[256,640]{1,0:T(8,128)(2,1)S(1)}, f32[256,512]{1,0:T(8,128)S(1)}, f32[256,128]{1,0:T(8,128)S(1)}) custom-call(bf16[256,512]{1,0:T(8,128)(2,1)S(1)} %get-tuple-element.54.xo, bf16[256,512]{1,0:T(8,128)(2,1)S(1)} %collective-permute-done.xp, f32[2,256,512]{2,1,0:T(8,128)S(1)} %get-tuple-element.83.dkv, ...), custom_call_target="tpu_custom_call" | custom-call | flops 15000000512 | bytes 15000000 | tf_op jit(solution)/shard_map/pallas_call | solution.py:401
  71.8 0.8 collective-permute-start.16
  72.6 0.0 collective-permute-done.19.refs_3_
  72.6 1.5 %collective-permute-done.18.refs_2_ = f32[9,512]{1,0:T(8,128)S(1)} collective-permute-done((f32[9,512]{1,0:T(8,128)S(1)}, f32[9,512]{1,0:T(8,128)S(1)}, u32[]{:S(2)}, u32[]{:S(2)}) %collective-permute-start.18) | collective-permute-done | bytes 18464 | tf_op jit(solution)/shard_map/ppermute | solution.py:483
  74.1 0.4 collective-permute-done.17.refs_1_
  74.5 0.1 collective-permute-start.22
  74.6 0.7 collective-permute-start.21
  75.3 3.4 %collective-permute-start.20 = (f32[9,512]{1,0:T(8,128)S(1)}, f32[9,512]{1,0:T(8,128)S(1)}, u32[]{:S(2)}, u32[]{:S(2)}) collective-permute-start(f32[9,512]{1,0:T(8,128)S(1)} %shard_map.106.after.refs_0_), channel_id=1, source_target_pairs={{0,4},{2,6},{4,0},{6,2},{8,12},{10,14},{12,8},{14,10},{16,20},{18,... | collective-permute-start | bytes 55304 | tf_op jit(solution)/shard_map/ppermute | solution.py:483
  78.7 1.0 %collective-permute-done.22.refs_3_ = f32[9,512]{1,0:T(8,128)S(1)} collective-permute-done((f32[9,512]{1,0:T(8,128)S(1)}, f32[9,512]{1,0:T(8,128)S(1)}, u32[]{:S(2)}, u32[]{:S(2)}) %collective-permute-start.22) | collective-permute-done | bytes 18464 | tf_op jit(solution)/shard_map/ppermute | solution.py:483
  79.7 0.4 collective-permute-done.21.refs_2_
  80.1 0.8 collective-permute-done.20.refs_1_
  80.9 0.6 shard_map.108
  81.6 0.0 collective-permute-done.16.got
  81.6 1.1 %shard_map.107 = bf16[256,512]{1,0:T(8,128)(2,1)} custom-call(bf16[256,512]{1,0:T(8,128)(2,1)S(1)} %get-tuple-element.54.xo, bf16[256,512]{1,0:T(8,128)(2,1)S(1)} %collective-permute-done.xp, f32[256,512]{1,0:T(8,128)S(1)} %get-tuple-element.87.keep, f32[256,128]{1,0:T(8,128)S(1)} %get-tuple-element.88.stat, ...), custom_call_target="tpu_custom_call" | custom-call | flops 10000000000 | bytes 10000000 | tf_op jit(solution)/shard_map/pallas_call | solution.py:401
  (4 shorter events, 0.0 us)
Async XLA Ops:
  0.6 12.9 %collective-permute-start.1 = (bf16[256,512]{1,0:T(8,128)(2,1)}, bf16[256,512]{1,0:T(8,128)(2,1)S(1)}, u32[]{:S(2)}, u32[]{:S(2)}) collective-permute-start(bf16[256,512]{1,0:T(8,128)(2,1)} %refs_4_.1), channel_id=1, source_target_pairs={{0,2},{2,0},{4,6},{6,4},{8,10},{10,8},{12,14},{14,12},{16,18},{18,... | collective-permute-start | bytes 786440 | tf_op jit(solution)/shard_map/ppermute | solution.py:421
  0.7 12.8 %collective-permute-start = (bf16[256,512]{1,0:T(8,128)(2,1)}, bf16[256,512]{1,0:T(8,128)(2,1)S(1)}, u32[]{:S(2)}, u32[]{:S(2)}) collective-permute-start(bf16[256,512]{1,0:T(8,128)(2,1)} %refs_4_.1), channel_id=1, source_target_pairs={{0,1},{1,0},{2,3},{3,2},{4,5},{5,4},{6,7},{7,6},{8,9},{9,8},{10,11... | collective-permute-start | bytes 786440 | tf_op jit(solution)/shard_map/ppermute | solution.py:418
  2.9 17.9 %collective-permute-start.4 = (bf16[256,512]{1,0:T(8,128)(2,1)}, bf16[256,512]{1,0:T(8,128)(2,1)S(1)}, u32[]{:S(2)}, u32[]{:S(2)}) collective-permute-start(bf16[256,512]{1,0:T(8,128)(2,1)} %refs_4_.1), channel_id=1, source_target_pairs={{2,5},{3,4},{6,9},{7,8},{10,13},{11,12},{14,17},{15,16},{18,21},{1... | collective-permute-start | bytes 786440 | tf_op jit(solution)/shard_map/ppermute | solution.py:432
  6.9 13.9 %collective-permute-start.3 = (bf16[256,512]{1,0:T(8,128)(2,1)}, bf16[256,512]{1,0:T(8,128)(2,1)S(1)}, u32[]{:S(2)}, u32[]{:S(2)}) collective-permute-start(bf16[256,512]{1,0:T(8,128)(2,1)} %refs_4_.1), channel_id=1, source_target_pairs={{2,4},{6,8},{10,12},{14,16},{18,20},{22,24},{26,28},{30,32},{34,36... | collective-permute-start | bytes 786440 | tf_op jit(solution)/shard_map/ppermute | solution.py:425
  13.6 1.3 %copy-start = (bf16[1024,512]{1,0:T(8,128)(2,1)}, bf16[1024,512]{1,0:T(8,128)(2,1)S(1)}, u32[]{:S(2)}) copy-start(bf16[1024,512]{1,0:T(8,128)(2,1)S(1)} %get-tuple-element.60.wq) | copy-start | bytes 3145732
  13.6 7.3 %collective-permute-start.2 = (bf16[256,512]{1,0:T(8,128)(2,1)S(1)}, bf16[256,512]{1,0:T(8,128)(2,1)S(1)}, u32[]{:S(2)}, u32[]{:S(2)}) collective-permute-start(bf16[256,512]{1,0:T(8,128)(2,1)S(1)} %collective-permute-done.xp), channel_id=1, source_target_pairs={{0,2},{2,0},{4,6},{6,4},{8,10},{10,8},{12,14},{14,12},{16,18},{18,... | collective-permute-start | bytes 786440 | tf_op jit(solution)/shard_map/ppermute | solution.py:421
  14.8 13.9 %collective-permute-start.7 = (bf16[304,512]{1,0:T(8,128)(2,1)S(1)}, bf16[304,512]{1,0:T(8,128)(2,1)S(1)}, u32[]{:S(2)}, u32[]{:S(2)}) collective-permute-start(bf16[304,512]{1,0:T(8,128)(2,1)S(1)} %get-tuple-element.69), channel_id=1, source_target_pairs={{0,1},{1,0},{2,3},{3,2},{4,5},{5,4},{6,7},{7,6},{8,9},{9,8},{10,11... | collective-permute-start | bytes 933896 | tf_op jit(solution)/shard_map/ppermute | solution.py:418
  24.6 6.5 %collective-permute-start.6 = (bf16[32,1024]{1,0:T(8,128)(2,1)S(1)}, bf16[32,1024]{1,0:T(8,128)(2,1)S(1)}, u32[]{:S(2)}, u32[]{:S(2)}) collective-permute-start(bf16[32,1024]{1,0:T(8,128)(2,1)S(1)} %get-tuple-element.67.edges), channel_id=1, source_target_pairs={{0,1},{1,0},{2,3},{3,2},{4,5},{5,4},{6,7},{7,6},{8,9},{9,8},{10,11... | collective-permute-start | bytes 196616 | tf_op jit(solution)/shard_map/ppermute | solution.py:418
  27.5 14.9 %collective-permute-start.5 = (bf16[256,1024]{1,0:T(8,128)(2,1)S(1)}, bf16[256,1024]{1,0:T(8,128)(2,1)S(1)}, u32[]{:S(2)}, u32[]{:S(2)}) collective-permute-start(bf16[256,1024]{1,0:T(8,128)(2,1)S(1)} %shard_map.97.part), channel_id=1, source_target_pairs={{0,1},{1,0},{2,3},{3,2},{4,5},{5,4},{6,7},{7,6},{8,9},{9,8},{10,11... | collective-permute-start | bytes 1572872 | tf_op jit(solution)/shard_map/ppermute | solution.py:418
  31.2 2.0 %collective-permute-start.8 = (bf16[32,1024]{1,0:T(8,128)(2,1)S(1)}, bf16[32,1024]{1,0:T(8,128)(2,1)S(1)}, u32[]{:S(2)}, u32[]{:S(2)}) collective-permute-start(bf16[32,1024]{1,0:T(8,128)(2,1)S(1)} %get-tuple-element.70), channel_id=1, source_target_pairs={{0,2},{2,0},{4,6},{6,4},{8,10},{10,8},{12,14},{14,12},{16,18},{18,... | collective-permute-start | bytes 196616 | tf_op jit(solution)/shard_map/ppermute | solution.py:421
  31.3 11.1 %collective-permute-start.9 = (bf16[32,1024]{1,0:T(8,128)(2,1)S(1)}, bf16[32,1024]{1,0:T(8,128)(2,1)S(1)}, u32[]{:S(2)}, u32[]{:S(2)}) collective-permute-start(bf16[32,1024]{1,0:T(8,128)(2,1)S(1)} %get-tuple-element.71), channel_id=1, source_target_pairs={{2,4},{6,8},{10,12},{14,16},{18,20},{22,24},{26,28},{30,32},{34,36... | collective-permute-start | bytes 196616 | tf_op jit(solution)/shard_map/ppermute | solution.py:425
  47.1 3.6 %collective-permute-start.10 = (f32[9,512]{1,0:T(8,128)S(1)}, f32[9,512]{1,0:T(8,128)S(1)}, u32[]{:S(2)}, u32[]{:S(2)}) collective-permute-start(f32[9,512]{1,0:T(8,128)S(1)} %get-tuple-element.81.refs_0_), channel_id=1, source_target_pairs={{0,2},{2,0},{4,6},{6,4},{8,10},{10,8},{12,14},{14,12},{16,18},{18,... | collective-permute-start | bytes 55304 | tf_op jit(solution)/shard_map/ppermute | solution.py:483
  48.5 22.4 %collective-permute-start.12 = (bf16[2,256,512]{2,1,0:T(8,128)(2,1)S(1)}, bf16[2,256,512]{2,1,0:T(8,128)(2,1)S(1)}, u32[]{:S(2)}, u32[]{:S(2)}) collective-permute-start(bf16[2,256,512]{2,1,0:T(8,128)(2,1)S(1)} %get-tuple-element.85), channel_id=1, source_target_pairs={{2,4},{6,8},{10,12},{14,16},{18,20},{22,24},{26,28},{30,32},{34,36... | collective-permute-start | bytes 1572872 | tf_op jit(solution)/shard_map/ppermute | solution.py:425
  50.8 11.8 %collective-permute-start.15 = (f32[9,512]{1,0:T(8,128)S(1)}, f32[9,512]{1,0:T(8,128)S(1)}, u32[]{:S(2)}, u32[]{:S(2)}) collective-permute-start(f32[9,512]{1,0:T(8,128)S(1)} %shard_map.101.refs_1_.after.refs_0_), channel_id=1, source_target_pairs={{0,192},{2,194},{4,196},{6,198},{8,200},{10,202},{12,204},{14,206}... | collective-permute-start | bytes 55304 | tf_op jit(solution)/shard_map/ppermute | solution.py:483
  57.3 8.2 %collective-permute-start.14 = (f32[9,512]{1,0:T(8,128)S(1)}, f32[9,512]{1,0:T(8,128)S(1)}, u32[]{:S(2)}, u32[]{:S(2)}) collective-permute-start(f32[9,512]{1,0:T(8,128)S(1)} %shard_map.101.refs_1_.after.refs_0_), channel_id=1, source_target_pairs={{0,128},{2,130},{4,132},{6,134},{8,136},{10,138},{12,140},{14,142}... | collective-permute-start | bytes 55304 | tf_op jit(solution)/shard_map/ppermute | solution.py:483
  58.3 7.2 %collective-permute-start.13 = (f32[9,512]{1,0:T(8,128)S(1)}, f32[9,512]{1,0:T(8,128)S(1)}, u32[]{:S(2)}, u32[]{:S(2)}) collective-permute-start(f32[9,512]{1,0:T(8,128)S(1)} %shard_map.101.refs_1_.after.refs_0_), channel_id=1, source_target_pairs={{0,64},{2,66},{4,68},{6,70},{8,72},{10,74},{12,76},{14,78},{16,80}... | collective-permute-start | bytes 55304 | tf_op jit(solution)/shard_map/ppermute | solution.py:483
  59.8 1.3 %copy-start.1 = (bf16[1024,512]{1,0:T(8,128)(2,1)S(1)}, bf16[1024,512]{1,0:T(8,128)(2,1)}, u32[]{:S(2)}) copy-start(bf16[1024,512]{1,0:T(8,128)(2,1)} %copy-done) | copy-start | bytes 3145732
  61.0 9.9 %collective-permute-start.11 = (bf16[2,256,512]{2,1,0:T(8,128)(2,1)S(1)}, bf16[2,256,512]{2,1,0:T(8,128)(2,1)S(1)}, u32[]{:S(2)}, u32[]{:S(2)}) collective-permute-start(bf16[2,256,512]{2,1,0:T(8,128)(2,1)S(1)} %get-tuple-element.84), channel_id=1, source_target_pairs={{0,2},{2,0},{4,6},{6,4},{8,10},{10,8},{12,14},{14,12},{16,18},{18,... | collective-permute-start | bytes 1572872 | tf_op jit(solution)/shard_map/ppermute | solution.py:421
  65.5 7.0 %collective-permute-start.19 = (f32[9,512]{1,0:T(8,128)S(1)}, f32[9,512]{1,0:T(8,128)S(1)}, u32[]{:S(2)}, u32[]{:S(2)}) collective-permute-start(f32[9,512]{1,0:T(8,128)S(1)} %shard_map.104.after.refs_0_), channel_id=1, source_target_pairs={{0,48},{2,50},{4,52},{6,54},{8,56},{10,58},{12,60},{14,62},{16,32}... | collective-permute-start | bytes 55304 | tf_op jit(solution)/shard_map/ppermute | solution.py:483
  70.2 3.9 %collective-permute-start.18 = (f32[9,512]{1,0:T(8,128)S(1)}, f32[9,512]{1,0:T(8,128)S(1)}, u32[]{:S(2)}, u32[]{:S(2)}) collective-permute-start(f32[9,512]{1,0:T(8,128)S(1)} %shard_map.104.after.refs_0_), channel_id=1, source_target_pairs={{0,32},{2,34},{4,36},{6,38},{8,40},{10,42},{12,44},{14,46},{16,48}... | collective-permute-start | bytes 55304 | tf_op jit(solution)/shard_map/ppermute | solution.py:483
  70.2 4.3 %collective-permute-start.17 = (f32[9,512]{1,0:T(8,128)S(1)}, f32[9,512]{1,0:T(8,128)S(1)}, u32[]{:S(2)}, u32[]{:S(2)}) collective-permute-start(f32[9,512]{1,0:T(8,128)S(1)} %shard_map.104.after.refs_0_), channel_id=1, source_target_pairs={{0,16},{2,18},{4,20},{6,22},{8,24},{10,26},{12,28},{14,30},{16,0},... | collective-permute-start | bytes 55304 | tf_op jit(solution)/shard_map/ppermute | solution.py:483
  71.8 9.8 %collective-permute-start.16 = (bf16[256,640]{1,0:T(8,128)(2,1)S(1)}, bf16[256,640]{1,0:T(8,128)(2,1)S(1)}, u32[]{:S(2)}, u32[]{:S(2)}) collective-permute-start(bf16[256,640]{1,0:T(8,128)(2,1)S(1)} %get-tuple-element.89), channel_id=1, source_target_pairs={{0,1},{1,0},{2,3},{3,2},{4,5},{5,4},{6,7},{7,6},{8,9},{9,8},{10,11... | collective-permute-start | bytes 983048 | tf_op jit(solution)/shard_map/ppermute | solution.py:418
  74.5 5.2 %collective-permute-start.22 = (f32[9,512]{1,0:T(8,128)S(1)}, f32[9,512]{1,0:T(8,128)S(1)}, u32[]{:S(2)}, u32[]{:S(2)}) collective-permute-start(f32[9,512]{1,0:T(8,128)S(1)} %shard_map.106.after.refs_0_), channel_id=1, source_target_pairs={{0,12},{2,14},{4,8},{6,10},{8,4},{10,6},{12,0},{14,2},{16,28},{18,... | collective-permute-start | bytes 55304 | tf_op jit(solution)/shard_map/ppermute | solution.py:483
  74.6 5.5 %collective-permute-start.21 = (f32[9,512]{1,0:T(8,128)S(1)}, f32[9,512]{1,0:T(8,128)S(1)}, u32[]{:S(2)}, u32[]{:S(2)}) collective-permute-start(f32[9,512]{1,0:T(8,128)S(1)} %shard_map.106.after.refs_0_), channel_id=1, source_target_pairs={{0,8},{2,10},{4,12},{6,14},{8,0},{10,2},{12,4},{14,6},{16,24},{18,... | collective-permute-start | bytes 55304 | tf_op jit(solution)/shard_map/ppermute | solution.py:483
  75.3 5.6 %collective-permute-start.20 = (f32[9,512]{1,0:T(8,128)S(1)}, f32[9,512]{1,0:T(8,128)S(1)}, u32[]{:S(2)}, u32[]{:S(2)}) collective-permute-start(f32[9,512]{1,0:T(8,128)S(1)} %shard_map.106.after.refs_0_), channel_id=1, source_target_pairs={{0,4},{2,6},{4,0},{6,2},{8,12},{10,14},{12,8},{14,10},{16,20},{18,... | collective-permute-start | bytes 55304 | tf_op jit(solution)/shard_map/ppermute | solution.py:483

commit v4 on v3

--- a/solution.py
+++ b/solution.py
@@ -19,6 +19,8 @@
 HEADS = SHARE // HEAD_DIM
 LANES = 128
 EDGE = 16
+RIM = 32
+MID = ROWS - 2 * RIM
 CHUNKS = D // LANES
 HALF_CHUNKS = SHARE // LANES
 PAD = 16
@@ -78,9 +80,9 @@
     return slice(head * HEAD_DIM, (head + 1) * HEAD_DIM)
 
 
-def band_bias(right, valid):
-    row = (lax.broadcasted_iota(jnp.int32, (ROWS, ROWS), 0) >= BLOCK).astype(jnp.int32)
-    col = (lax.broadcasted_iota(jnp.int32, (ROWS, ROWS), 1) >= BLOCK).astype(jnp.int32)
+def band_bias(right, valid, rows):
+    row = (lax.broadcasted_iota(jnp.int32, (rows, ROWS), 0) >= rows // 2).astype(jnp.int32)
+    col = (lax.broadcasted_iota(jnp.int32, (rows, ROWS), 1) >= BLOCK).astype(jnp.int32)
     hidden = ((row - col) == 1 - 2 * right) | (valid == 0)
     return jnp.where(hidden, MASKED, 0.0).astype(F32)
 
@@ -103,15 +105,14 @@
         out[...] = (nn(no, w[own, :]) + nn(np_, w[other, :])).astype(BF16)
 
 
-def attend_kernel(a0, a1, b0, b1, wk, wv, wo, q, k, v, ka, va, kb, vb, p, att, edges):
-    halo_kv(a0, a1, wk, wv, ka, va)
-    halo_kv(b0, b1, wk, wv, kb, vb)
+def attend(rows, q, k, v, ka, va, kb, vb, wo, p, att, part):
     odd, left, right = placement()
-    bias_a = band_bias(1 - odd, 1)
-    bias_b = band_bias(odd, jnp.where(odd == 1, right, left))
+    height = att.shape[0]
+    bias_a = band_bias(1 - odd, 1, height)
+    bias_b = band_bias(odd, jnp.where(odd == 1, right, left), height)
     for head in range(HEADS):
         f = lanes_of(head)
-        qh = q[:, f]
+        qh = jnp.concatenate([q[at, f] for at in rows], axis=0)
         scores = (
             nt(qh, k[:, f]) * SCALE,
             nt(qh, ka[:, f]) * SCALE + bias_a,
@@ -128,38 +129,46 @@
             out = out + nn(s, values[:, f])
         att[:, f] = out.astype(BF16)
     own, other = own_other()
-    rim = jnp.concatenate([att[at, :] for at in edge_rows(odd)], axis=0)
-    edges[:, :SHARE] = nn(rim, wo[:, own]).astype(BF16)
-    edges[:, SHARE:] = nn(rim, wo[:, other]).astype(BF16)
-
-
-def project_out_kernel(att, wo, part):
-    own, other = own_other()
     part[:, :SHARE] = nn(att[...], wo[:, own]).astype(BF16)
     part[:, SHARE:] = nn(att[...], wo[:, other]).astype(BF16)
 
 
-def edge_rows(odd):
-    last = ROWS - EDGE
+def attend_rim_kernel(a0, a1, b0, b1, wk, wv, wo, q, k, v, ka, va, kb, vb, p, att, part):
+    halo_kv(a0, a1, wk, wv, ka, va)
+    halo_kv(b0, b1, wk, wv, kb, vb)
+    rows = (slice(0, RIM), slice(ROWS - RIM, ROWS))
+    attend(rows, q, k, v, ka, va, kb, vb, wo, p, att, part)
+
+
+def attend_mid_kernel(wo, q, k, v, ka, va, kb, vb, p, att, part):
+    attend((slice(RIM, ROWS - RIM),), q, k, v, ka, va, kb, vb, wo, p, att, part)
+
+
+def in_order(rim, mid):
+    return jnp.concatenate([rim[:RIM], mid, rim[RIM:]], axis=0)
+
+
+def edge_rows(rows):
+    odd, _, _ = placement()
+    last = rows - EDGE
     return (
         pl.ds(pl.multiple_of((1 - odd) * last, EDGE), EDGE),
         pl.ds(pl.multiple_of(odd * last, EDGE), EDGE),
     )
 
 
-def merge_kernel(edges, edges_p, co, cp, to_a, to_b):
-    for n, (at, out) in enumerate(zip(edge_rows(placement()[0]), (to_a, to_b))):
-        rows = slice(n * EDGE, (n + 1) * EDGE)
-        mine = edges[rows, :].astype(F32)
-        theirs = edges_p[rows, :].astype(F32)
+def merge_kernel(part, part_p, co, cp, to_a, to_b):
+    for at, at_c, out in zip(edge_rows(2 * RIM), edge_rows(ROWS), (to_a, to_b)):
+        mine = part[at, :].astype(F32)
+        theirs = part_p[at, :].astype(F32)
         out[:EDGE, :SHARE] = (mine[:, :SHARE] + theirs[:, SHARE:]).astype(BF16)
         out[:EDGE, SHARE:] = (mine[:, SHARE:] + theirs[:, :SHARE]).astype(BF16)
-        out[EDGE:, :SHARE] = co[at, :]
-        out[EDGE:, SHARE:] = cp[at, :]
+        out[EDGE:, :SHARE] = co[at_c, :]
+        out[EDGE:, SHARE:] = cp[at_c, :]
 
 
 def conv_kernel(
-    xo, xp, a0, a1, b0, b1, part, part_p, ea, eb, co, cp, to, wo,
+    xo, xp, a0, a1, b0, b1, rim, rim_p, mid, mid_p, ea, eb, co, cp, to, wo,
     output, dh, datt, gk,
     n2s, cs, dzs, dns, hs, taps, rs2, sum0, sum1, dhb,
 ):
@@ -173,12 +182,13 @@
         taps[c, :KW, :] = to[:, f]
         taps[HALF_CHUNKS + c, :KW, :] = tp[:, f]
 
-    def rows_in(index, carry):
+    def rows_in(index, carry, part, part_p, shift):
         r = pl.multiple_of(index * step, step)
+        source = pl.ds(pl.multiple_of(r - shift, step), step)
         rows = pl.ds(r, step)
         held = pl.ds(pl.multiple_of(PAD + r, PAD), step)
-        p = part[rows, :].astype(F32)
-        pp = part_p[rows, :].astype(F32)
+        p = part[source, :].astype(F32)
+        pp = part_p[source, :].astype(F32)
         ho = xo[rows, :].astype(F32) + p[:, :SHARE] + pp[:, SHARE:]
         hp = xp[rows, :].astype(F32) + p[:, SHARE:] + pp[:, :SHARE]
         center, rstd = moments(ho, hp)
@@ -194,7 +204,13 @@
             cs[HALF_CHUNKS + c, held, :] = ctan_p[:, f]
         return carry
 
-    lax.fori_loop(0, ROWS // step, rows_in, 0)
+    for first, last, part, part_p, shift in (
+        (0, RIM, rim, rim_p, 0),
+        (RIM, ROWS - RIM, mid, mid_p, RIM),
+        (ROWS - RIM, ROWS, rim, rim_p, MID),
+    ):
+        body = functools.partial(rows_in, part=part, part_p=part_p, shift=shift)
+        lax.fori_loop(first // step, last // step, body, 0)
 
     pa = ea[:EDGE, :].astype(F32)
     pb = eb[:EDGE, :].astype(F32)
@@ -292,26 +308,28 @@
     return nn(ds, kh), tn(ds, qh), tn(p, gh)
 
 
-def back_halo_kernel(q, k, v, datt, att, p, *refs, which):
+def back_halo_kernel(q, k, v, datt, att, att_mid, p, p_mid, *refs, which):
     dq, dkv = refs[-2:]
     at = slice(which * ROWS, (which + 1) * ROWS)
     for head in range(HEADS):
         f = lanes_of(head)
         gh = datt[:, f]
-        delta = row_sum(gh.astype(F32) * att[:, f].astype(F32))
-        d_q, d_k, d_v = pair_grad(q[:, f], k[:, f], v[:, f], gh, p[head, :, at], delta)
+        delta = row_sum(gh.astype(F32) * in_order(att[:, f], att_mid[:, f]).astype(F32))
+        probs = in_order(p[head, :, at], p_mid[head, :, at])
+        d_q, d_k, d_v = pair_grad(q[:, f], k[:, f], v[:, f], gh, probs, delta)
         dq[:, f] = d_q + refs[0][:, f] if which == 1 else d_q
         dkv[0, :, f] = d_k.astype(BF16)
         dkv[1, :, f] = d_v.astype(BF16)
 
 
-def back_own_kernel(q, k, v, datt, att, p, dq_ab, wq, after, dkv, pin):
+def back_own_kernel(q, k, v, datt, att, att_mid, p, p_mid, dq_ab, wq, after, dkv, pin):
     dq = []
     for head in range(HEADS):
         f = lanes_of(head)
         gh = datt[:, f]
-        delta = row_sum(gh.astype(F32) * att[:, f].astype(F32))
-        d_q, d_k, d_v = pair_grad(q[:, f], k[:, f], v[:, f], gh, p[head, :, :ROWS], delta)
+        delta = row_sum(gh.astype(F32) * in_order(att[:, f], att_mid[:, f]).astype(F32))
+        probs = in_order(p[head, :, :ROWS], p_mid[head, :, :ROWS])
+        d_q, d_k, d_v = pair_grad(q[:, f], k[:, f], v[:, f], gh, probs, delta)
         dkv[0, :, f] = d_k
         dkv[1, :, f] = d_v
         dq.append((d_q + dq_ab[:, f]).astype(BF16))
@@ -445,17 +463,24 @@
     q, pack = lax.optimization_barrier((q, pack))
     pack_p = over_head(pack)
     edge = ((2 * EDGE, D), BF16)
-    ka, va, kb, vb, probs, att, edges = call(
-        attend_kernel,
+    chunk = [
+        (((HEADS, rows, 3 * ROWS), BF16), ((rows, SHARE), BF16), ((rows, D), BF16))
+        for rows in (2 * RIM, MID)
+    ]
+    ka, va, kb, vb, p_rim, att_rim, rim = call(
+        attend_rim_kernel,
         (a0, a1, b0, b1, w_key, w_value, w_out, q, k, v),
-        (big, big, big, big, ((HEADS, ROWS, 3 * ROWS), BF16), big, edge),
-        us=4.0,
-    )
-    edges_p = over_head(edges)
-    (part,) = call(project_out_kernel, (att, w_out), (((ROWS, D), BF16),), us=1.0)
-    part_p = over_head(part)
+        (big, big, big, big, *chunk[0]),
+        us=2.0,
+    )
+    rim_p = over_head(rim)
+    p_mid, att_mid, mid = call(
+        attend_mid_kernel, (w_out, q, k, v, ka, va, kb, vb), chunk[1], us=2.0
+    )
+    mid_p = over_head(mid)
+    attended = (att_rim, att_mid, p_rim, p_mid)
     to_a, to_b = call(
-        merge_kernel, (edges, edges_p, cotangent, pack_p), (edge, edge), us=3.0
+        merge_kernel, (rim, rim_p, cotangent, pack_p), (edge, edge), us=3.0
     )
     eb = over_b(to_b)
     ea = over_a(to_a)
@@ -464,7 +489,7 @@
     output, dh, datt, gk = call(
         conv_kernel,
         (
-            inputs, xp, a0, a1, b0, b1, part, part_p, ea, eb, cotangent, pack_p,
+            inputs, xp, a0, a1, b0, b1, rim, rim_p, mid, mid_p, ea, eb, cotangent, pack_p,
             kernel, w_out,
         ),
         (big, ((ROWS, SHARE), F32), big, ((KW, SHARE), F32)),
@@ -486,21 +511,21 @@
     pair = ((2, ROWS, SHARE), BF16)
     dq_b, dkv_b = call(
         functools.partial(back_halo_kernel, which=2),
-        (q, kb, vb, datt, att, probs),
+        (q, kb, vb, datt, *attended),
         (((ROWS, SHARE), F32), pair),
         us=1.5,
     )
     got_b = over_b(dkv_b)
     dq_ab, dkv_a = call(
         functools.partial(back_halo_kernel, which=1),
-        (q, ka, va, datt, att, probs, dq_b, chain[1]),
+        (q, ka, va, datt, *attended, dq_b, chain[1]),
         (((ROWS, SHARE), F32), pair),
         us=1.5,
     )
     got_a = over_a(dkv_a)
     dkv, pin = call(
         back_own_kernel,
-        (q, k, v, datt, att, probs, dq_ab, w_query, chain[1]),
+        (q, k, v, datt, *attended, dq_ab, w_query, chain[1]),
         (((2, ROWS, SHARE), F32), ((ROWS, D), F32)),
         us=2.0,
     )

time: 83.1 us -> 81.1 us (0.976)
  waiting for transfers between devices: 23.4 us -> 19.4 us
  Pallas kernels: 19.1 us -> 20.3 us
    ppermute x3, waiting for transfers between devices: 9.21 us -> 7.04 us  [over_b(): return lax.ppermute(value, 'tm', pairs + [(j, i) for i, j in pairs])]
    ppermute x3, starting transfers between devices: 8.42 us -> 9.7 us  [over_b(): return lax.ppermute(value, 'tm', pairs + [(j, i) for i, j in pairs])]
    pallas_call x14, Pallas kernels: 16.7 us -> 17.9 us  [call(): pl.pallas_call(kernel, out_shape=[jax.ShapeDtypeStruct(shape, dtype) for...]
    ppermute x10, starting transfers between devices: 18.5 us -> 17.4 us  [local(): lax.ppermute(last, 'tm', [(i, i ^ step) for i in range(count)])]
    ppermute x5, waiting for transfers between devices: 2.43 us -> 1.35 us  [over_head(): return lax.ppermute(value, 'head', [(0, 1), (1, 0)])]
  transfers between devices with their start and end apart: 23 -> 23, of which waited for: 9 -> 9; matrix products, arithmetic and copies ran while one was open for 0% -> 0% of each run, Pallas kernels for 16% -> 18%
where the time goes in v4:
time: 81.1 us; the launch traced here: 80.6 us
  starting transfers between devices  40 us (49%)
  Pallas kernels  20.3 us (25%)
  waiting for transfers between devices  19.4 us (24%)
  between operations  0.91 us (1%)
    pallas_call x14, Pallas kernels, call(): pl.pallas_call(kernel, out_shape=[jax.ShapeDtypeStruct(shape, dtype) for...  17.9 us
    ppermute x10, starting transfers between devices, local(): lax.ppermute(last, 'tm', [(i, i ^ step) for i in range(count)])  17.4 us
    ppermute x3, starting transfers between devices, over_b(): return lax.ppermute(value, 'tm', pairs + [(j, i) for i, j in pairs])  9.7 us
    ppermute x5, starting transfers between devices, over_head(): return lax.ppermute(value, 'head', [(0, 1), (1, 0)])  8.6 us
    ppermute x3, waiting for transfers between devices, over_b(): return lax.ppermute(value, 'tm', pairs + [(j, i) for i, j in pairs])  7.04 us
    ppermute x10, waiting for transfers between devices, local(): lax.ppermute(last, 'tm', [(i, i ^ step) for i in range(count)])  6.45 us
    ppermute x1, waiting for transfers between devices, over_b_and_head(): return lax.ppermute(value, ('tm', 'head'), crossed)  4.59 us
    ppermute x1, starting transfers between devices, over_b_and_head(): return lax.ppermute(value, ('tm', 'head'), crossed)  3.97 us
  transfers between devices with their start and end apart: 23, of which 9 were waited for; matrix products, arithmetic and copies ran while one was open for 0% of the time, Pallas kernels for 18%

profile of v4, /device:TPU:2, one launch (start us, length us, event | category | flops | bytes accessed | tf_op | source)
XLA Modules:
  0.0 80.6 jit_solution(14239523256325629452)
XLA Ops:
  0.6 0.1 collective-permute-start.1
  0.7 2.2 %collective-permute-start = (bf16[256,512]{1,0:T(8,128)(2,1)}, bf16[256,512]{1,0:T(8,128)(2,1)S(1)}, u32[]{:S(2)}, u32[]{:S(2)}) collective-permute-start(bf16[256,512]{1,0:T(8,128)(2,1)} %refs_4_.1), channel_id=1, source_target_pairs={{0,1},{1,0},{2,3},{3,2},{4,5},{5,4},{6,7},{7,6},{8,9},{9,8},{10,11... | collective-permute-start | bytes 786440 | tf_op jit(solution)/shard_map/ppermute | solution.py:436
  2.9 4.0 %collective-permute-start.4 = (bf16[256,512]{1,0:T(8,128)(2,1)}, bf16[256,512]{1,0:T(8,128)(2,1)S(1)}, u32[]{:S(2)}, u32[]{:S(2)}) collective-permute-start(bf16[256,512]{1,0:T(8,128)(2,1)} %refs_4_.1), channel_id=1, source_target_pairs={{2,5},{3,4},{6,9},{7,8},{10,13},{11,12},{14,17},{15,16},{18,21},{1... | collective-permute-start | bytes 786440 | tf_op jit(solution)/shard_map/ppermute | solution.py:450
  6.9 4.2 %collective-permute-start.3 = (bf16[256,512]{1,0:T(8,128)(2,1)}, bf16[256,512]{1,0:T(8,128)(2,1)S(1)}, u32[]{:S(2)}, u32[]{:S(2)}) collective-permute-start(bf16[256,512]{1,0:T(8,128)(2,1)} %refs_4_.1), channel_id=1, source_target_pairs={{2,4},{6,8},{10,12},{14,16},{18,20},{22,24},{26,28},{30,32},{34,36... | collective-permute-start | bytes 786440 | tf_op jit(solution)/shard_map/ppermute | solution.py:443
  11.2 2.4 %shard_map.94 = (bf16[1024,512]{1,0:T(8,128)(2,1)S(1)}, bf16[1024,512]{1,0:T(8,128)(2,1)S(1)}, bf16[1024,512]{1,0:T(8,128)(2,1)S(1)}, bf16[512,1024]{1,0:T(8,128...) custom-call(bf16[1024,512]{1,0:T(8,128)(2,1)} %refs_0_.1, ...), custom_call_target="tpu_custom_call" | custom-call | bytes 67108864 | tf_op jit(solution)/shard_map/pallas_call | solution.py:406
  13.6 0.0 copy-start.4
  13.6 0.0 copy-start
  13.6 0.0 copy-start.2
  13.6 0.0 collective-permute-done.1.a0
  13.6 0.0 collective-permute-done.xp
  13.6 0.1 collective-permute-start.2
  13.7 1.1 %shard_map.95 = (bf16[256,512]{1,0:T(8,128)(2,1)S(1)}, bf16[256,512]{1,0:T(8,128)(2,1)S(1)}, bf16[256,512]{1,0:T(8,128)(2,1)S(1)}) custom-call(bf16[256,512]{1,0:T(8,128)(2,1)S(1)} %get-tuple-element.57.xo, bf16[256,512]{1,0:T(8,128)(2,1)S(1)} %collective-permute-done.xp, bf16[1024,512]{1,0:T(8,128)(2,1)S(1)} %get-tuple-element.63.wq, ...), custom_call_target="tpu_custom_call" | custom-call | tf_op jit(solution)/shard_map/pallas_call | solution.py:419
  14.9 0.0 copy-done.4
  14.9 1.4 %collective-permute-start.7 = (bf16[304,512]{1,0:T(8,128)(2,1)S(1)}, bf16[304,512]{1,0:T(8,128)(2,1)S(1)}, u32[]{:S(2)}, u32[]{:S(2)}) collective-permute-start(bf16[304,512]{1,0:T(8,128)(2,1)S(1)} %get-tuple-element.76), channel_id=1, source_target_pairs={{0,1},{1,0},{2,3},{3,2},{4,5},{5,4},{6,7},{7,6},{8,9},{9,8},{10,11... | collective-permute-start | bytes 933896 | tf_op jit(solution)/shard_map/ppermute | solution.py:436
  16.3 4.6 %collective-permute-done.4.b1 = bf16[256,512]{1,0:T(8,128)(2,1)S(1)} collective-permute-done((bf16[256,512]{1,0:T(8,128)(2,1)}, bf16[256,512]{1,0:T(8,128)(2,1)S(1)}, u32[]{:S(2)}, u32[]{:S(2)}) %collective-permute-start.4) | collective-permute-done | bytes 262176 | tf_op jit(solution)/shard_map/ppermute | solution.py:450
  20.9 0.0 collective-permute-done.3.b0
  20.9 0.0 collective-permute-done.2.a1
  20.9 0.0 copy-done
  20.9 0.0 copy-done.2
  20.9 3.2 %shard_map.96 = (bf16[256,512]{1,0:T(8,128)(2,1)S(1)}, bf16[256,512]{1,0:T(8,128)(2,1)S(1)}, bf16[256,512]{1,0:T(8,128)(2,1)S(1)}, bf16[256,512]{1,0:T(8,128)(2,...) custom-call(bf16[256,512]{1,0:T(8,128)(2,1)S(1)} %collective-permute-done.1.a0, ...), custom_call_target="tpu_custom_call" | custom-call | flops 20000000000 | bytes 20000000 | tf_op jit(solution)/shard_map/pallas_call | solution.py:419
  24.1 2.5 %collective-permute-start.5 = (bf16[64,1024]{1,0:T(8,128)(2,1)S(1)}, bf16[64,1024]{1,0:T(8,128)(2,1)S(1)}, u32[]{:S(2)}, u32[]{:S(2)}) collective-permute-start(bf16[64,1024]{1,0:T(8,128)(2,1)S(1)} %get-tuple-element.69.part.rim), channel_id=1, source_target_pairs={{0,1},{1,0},{2,3},{3,2},{4,5},{5,4},{6,7},{7,6},{8,9},{9,8},{10,11... | collective-permute-start | bytes 393224 | tf_op jit(solution)/shard_map/ppermute | solution.py:436
  26.6 2.2 %shard_map.97 = (bf16[4,192,768]{2,1,0:T(8,128)(2,1)S(1)}, bf16[192,512]{1,0:T(8,128)(2,1)S(1)}, bf16[192,1024]{1,0:T(8,128)(2,1)S(1)}) custom-call(bf16[512,1024]{1,0:T(8,128)(2,1)S(1)} %get-tuple-element.62.wo, bf16[256,512]{1,0:T(8,128)(2,1)S(1)} %get-tuple-element.66.q, bf16[256,512]{1,0:T(8,128)(2,1)S(1)} %get-tuple-element.67.k, ...), custom_call_target="tpu_custom_call" | custom-call | flops 20000000000 | bytes 20000000 | tf_op jit(solution)/shard_map/pallas_call | solution.py:419
  28.9 1.2 %collective-permute-start.6 = (bf16[192,1024]{1,0:T(8,128)(2,1)S(1)}, bf16[192,1024]{1,0:T(8,128)(2,1)S(1)}, u32[]{:S(2)}, u32[]{:S(2)}) collective-permute-start(bf16[192,1024]{1,0:T(8,128)(2,1)S(1)} %get-tuple-element.74.mid), channel_id=1, source_target_pairs={{0,1},{1,0},{2,3},{3,2},{4,5},{5,4},{6,7},{7,6},{8,9},{9,8},{10,11... | collective-permute-start | bytes 1179656 | tf_op jit(solution)/shard_map/ppermute | solution.py:436
  30.0 0.0 collective-permute-done.7.cp
  30.0 1.3 %collective-permute-done.5.part_p.rim_p = bf16[64,1024]{1,0:T(8,128)(2,1)S(1)} collective-permute-done((bf16[64,1024]{1,0:T(8,128)(2,1)S(1)}, bf16[64,1024]{1,0:T(8,128)(2,1)S(1)}, u32[]{:S(2)}, u32[]{:S(2)}) %collective-permute-start.5) | collective-permute-done | bytes 131104 | tf_op jit(solution)/shard_map/ppermute | solution.py:436
  31.4 0.1 collective-permute-start.8
  31.5 2.4 %collective-permute-start.9 = (bf16[32,1024]{1,0:T(8,128)(2,1)S(1)}, bf16[32,1024]{1,0:T(8,128)(2,1)S(1)}, u32[]{:S(2)}, u32[]{:S(2)}) collective-permute-start(bf16[32,1024]{1,0:T(8,128)(2,1)S(1)} %get-tuple-element.78), channel_id=1, source_target_pairs={{2,4},{6,8},{10,12},{14,16},{18,20},{22,24},{26,28},{30,32},{34,36... | collective-permute-start | bytes 196616 | tf_op jit(solution)/shard_map/ppermute | solution.py:443
  33.9 0.0 collective-permute-done.8.ea
  33.9 7.0 %collective-permute-done.9.eb = bf16[32,1024]{1,0:T(8,128)(2,1)S(1)} collective-permute-done((bf16[32,1024]{1,0:T(8,128)(2,1)S(1)}, bf16[32,1024]{1,0:T(8,128)(2,1)S(1)}, u32[]{:S(2)}, u32[]{:S(2)}) %collective-permute-start.9) | collective-permute-done | bytes 65568 | tf_op jit(solution)/shard_map/ppermute | solution.py:443
  40.9 0.0 collective-permute-done.6.mid_p
  41.0 4.6 %shard_map.99 = (bf16[256,512]{1,0:T(8,128)(2,1)}, f32[256,512]{1,0:T(8,128)S(1)}, bf16[256,512]{1,0:T(8,128)(2,1)S(1)}, f32[9,512]{1,0:T(8,128)S(1)}) custom-call(bf16[256,512]{1,0:T(8,128)(2,1)S(1)} %get-tuple-element.57.xo, bf16[256,512]{1,0:T(8,128)(2,1)S(1)} %collective-permute-done.xp, bf16[256,512]{1,0:T(8,128)(2,1)S(1)} %collective-permute-done.1.a0, ...), custom_call_target="tpu_custom_call" | custom-call | flops 49999998976 | bytes 50000000 | tf_op jit(solution)/shard_map/pallas_call | solution.py:419
  45.5 0.0 collective-permute-start.10
  45.5 1.4 %shard_map.100 = (f32[256,512]{1,0:T(8,128)S(1)}, bf16[2,256,512]{2,1,0:T(8,128)(2,1)S(1)}) custom-call(bf16[256,512]{1,0:T(8,128)(2,1)S(1)} %get-tuple-element.66.q, bf16[256,512]{1,0:T(8,128)(2,1)S(1)} %get-tuple-element.72.kb.k, bf16[256,512]{1,0:T(8,128)(2,1)S(1)} %get-tuple-element.73.vb.v, bf16[256,512]{1,0:T(8,128)(2,1)S(1)} %get-tuple-element.81.datt, ...), custom_call_target="tpu_custom_call" | custom-call | flops 15000000512 | bytes 15000000 | tf_op jit(solution)/shard_map/pallas_call | solution.py:419
  46.9 3.1 %collective-permute-start.12 = (bf16[2,256,512]{2,1,0:T(8,128)(2,1)S(1)}, bf16[2,256,512]{2,1,0:T(8,128)(2,1)S(1)}, u32[]{:S(2)}, u32[]{:S(2)}) collective-permute-start(bf16[2,256,512]{2,1,0:T(8,128)(2,1)S(1)} %get-tuple-element.91), channel_id=1, source_target_pairs={{2,4},{6,8},{10,12},{14,16},{18,20},{22,24},{26,28},{30,32},{34,36... | collective-permute-start | bytes 1572872 | tf_op jit(solution)/shard_map/ppermute | solution.py:443
  50.0 0.0 collective-permute-done.10.refs_1_
  50.0 6.4 %collective-permute-start.15 = (f32[9,512]{1,0:T(8,128)S(1)}, f32[9,512]{1,0:T(8,128)S(1)}, u32[]{:S(2)}, u32[]{:S(2)}) collective-permute-start(f32[9,512]{1,0:T(8,128)S(1)} %shard_map.101.refs_1_.after.refs_0_), channel_id=1, source_target_pairs={{0,192},{2,194},{4,196},{6,198},{8,200},{10,202},{12,204},{14,206}... | collective-permute-start | bytes 55304 | tf_op jit(solution)/shard_map/ppermute | solution.py:508
  56.4 1.0 %collective-permute-start.14 = (f32[9,512]{1,0:T(8,128)S(1)}, f32[9,512]{1,0:T(8,128)S(1)}, u32[]{:S(2)}, u32[]{:S(2)}) collective-permute-start(f32[9,512]{1,0:T(8,128)S(1)} %shard_map.101.refs_1_.after.refs_0_), channel_id=1, source_target_pairs={{0,128},{2,130},{4,132},{6,134},{8,136},{10,138},{12,140},{14,142}... | collective-permute-start | bytes 55304 | tf_op jit(solution)/shard_map/ppermute | solution.py:508
  57.4 1.5 %collective-permute-start.13 = (f32[9,512]{1,0:T(8,128)S(1)}, f32[9,512]{1,0:T(8,128)S(1)}, u32[]{:S(2)}, u32[]{:S(2)}) collective-permute-start(f32[9,512]{1,0:T(8,128)S(1)} %shard_map.101.refs_1_.after.refs_0_), channel_id=1, source_target_pairs={{0,64},{2,66},{4,68},{6,70},{8,72},{10,74},{12,76},{14,78},{16,80}... | collective-permute-start | bytes 55304 | tf_op jit(solution)/shard_map/ppermute | solution.py:508
  58.8 1.2 %shard_map.102 = (f32[256,512]{1,0:T(8,128)S(1)}, bf16[2,256,512]{2,1,0:T(8,128)(2,1)S(1)}) custom-call(bf16[256,512]{1,0:T(8,128)(2,1)S(1)} %get-tuple-element.66.q, bf16[256,512]{1,0:T(8,128)(2,1)S(1)} %get-tuple-element.70.ka.k, bf16[256,512]{1,0:T(8,128)(2,1)S(1)} %get-tuple-element.71.va.v, bf16[256,512]{1,0:T(8,128)(2,1)S(1)} %get-tuple-element.81.datt, ...), custom_call_target="tpu_custom_call" | custom-call | flops 15000000512 | bytes 15000000 | tf_op jit(solution)/shard_map/pallas_call | solution.py:419
  60.0 0.1 collective-permute-start.11
  60.1 1.5 %shard_map.103 = (f32[2,256,512]{2,1,0:T(8,128)S(1)}, f32[256,1024]{1,0:T(8,128)S(1)}) custom-call(bf16[256,512]{1,0:T(8,128)(2,1)S(1)} %get-tuple-element.66.q, bf16[256,512]{1,0:T(8,128)(2,1)S(1)} %get-tuple-element.67.k, bf16[256,512]{1,0:T(8,128)(2,1)S(1)} %get-tuple-element.68.v, bf16[256,512]{1,0:T(8,128)(2,1)S(1)} %get-tuple-element.81.datt, ...), custom_call_target="tpu_custom_call" | custom-call | flops 20000000000 | bytes 20000000 | tf_op jit(solution)/shard_map/pallas_call | solution.py:419
  61.7 0.0 collective-permute-done.15.refs_3_
  61.7 2.8 %collective-permute-done.14.refs_2_ = f32[9,512]{1,0:T(8,128)S(1)} collective-permute-done((f32[9,512]{1,0:T(8,128)S(1)}, f32[9,512]{1,0:T(8,128)S(1)}, u32[]{:S(2)}, u32[]{:S(2)}) %collective-permute-start.14) | collective-permute-done | bytes 18464 | tf_op jit(solution)/shard_map/ppermute | solution.py:508
  64.4 0.0 collective-permute-done.13.refs_1_
  64.5 3.7 %collective-permute-start.19 = (f32[9,512]{1,0:T(8,128)S(1)}, f32[9,512]{1,0:T(8,128)S(1)}, u32[]{:S(2)}, u32[]{:S(2)}) collective-permute-start(f32[9,512]{1,0:T(8,128)S(1)} %shard_map.104.after.refs_0_), channel_id=1, source_target_pairs={{0,48},{2,50},{4,52},{6,54},{8,56},{10,58},{12,60},{14,62},{16,32}... | collective-permute-start | bytes 55304 | tf_op jit(solution)/shard_map/ppermute | solution.py:508
  68.1 0.0 collective-permute-start.18
  68.1 0.7 collective-permute-start.17
  68.8 0.0 collective-permute-done.12.got_b
  68.8 0.0 collective-permute-done.11.got_a
  68.8 0.0 copy-done.3
  68.8 0.9 %shard_map.105 = (bf16[256,640]{1,0:T(8,128)(2,1)S(1)}, f32[256,512]{1,0:T(8,128)S(1)}, f32[256,128]{1,0:T(8,128)S(1)}) custom-call(bf16[256,512]{1,0:T(8,128)(2,1)S(1)} %get-tuple-element.57.xo, bf16[256,512]{1,0:T(8,128)(2,1)S(1)} %collective-permute-done.xp, f32[2,256,512]{2,1,0:T(8,128)S(1)} %get-tuple-element.89.dkv, ...), custom_call_target="tpu_custom_call" | custom-call | flops 15000000512 | bytes 15000000 | tf_op jit(solution)/shard_map/pallas_call | solution.py:419
  69.7 1.3 %collective-permute-start.16 = (bf16[256,640]{1,0:T(8,128)(2,1)S(1)}, bf16[256,640]{1,0:T(8,128)(2,1)S(1)}, u32[]{:S(2)}, u32[]{:S(2)}) collective-permute-start(bf16[256,640]{1,0:T(8,128)(2,1)S(1)} %get-tuple-element.95), channel_id=1, source_target_pairs={{0,1},{1,0},{2,3},{3,2},{4,5},{5,4},{6,7},{7,6},{8,9},{9,8},{10,11... | collective-permute-start | bytes 983048 | tf_op jit(solution)/shard_map/ppermute | solution.py:436
  71.0 0.0 collective-permute-done.19.refs_3_
  71.0 1.0 %collective-permute-done.18.refs_2_ = f32[9,512]{1,0:T(8,128)S(1)} collective-permute-done((f32[9,512]{1,0:T(8,128)S(1)}, f32[9,512]{1,0:T(8,128)S(1)}, u32[]{:S(2)}, u32[]{:S(2)}) %collective-permute-start.18) | collective-permute-done | bytes 18464 | tf_op jit(solution)/shard_map/ppermute | solution.py:508
  72.0 0.4 collective-permute-done.17.refs_1_
  72.5 0.1 collective-permute-start.22
  72.6 1.4 %collective-permute-start.21 = (f32[9,512]{1,0:T(8,128)S(1)}, f32[9,512]{1,0:T(8,128)S(1)}, u32[]{:S(2)}, u32[]{:S(2)}) collective-permute-start(f32[9,512]{1,0:T(8,128)S(1)} %shard_map.106.after.refs_0_), channel_id=1, source_target_pairs={{0,8},{2,10},{4,12},{6,14},{8,0},{10,2},{12,4},{14,6},{16,24},{18,... | collective-permute-start | bytes 55304 | tf_op jit(solution)/shard_map/ppermute | solution.py:508
  73.9 2.7 %collective-permute-start.20 = (f32[9,512]{1,0:T(8,128)S(1)}, f32[9,512]{1,0:T(8,128)S(1)}, u32[]{:S(2)}, u32[]{:S(2)}) collective-permute-start(f32[9,512]{1,0:T(8,128)S(1)} %shard_map.106.after.refs_0_), channel_id=1, source_target_pairs={{0,4},{2,6},{4,0},{6,2},{8,12},{10,14},{12,8},{14,10},{16,20},{18,... | collective-permute-start | bytes 55304 | tf_op jit(solution)/shard_map/ppermute | solution.py:508
  76.7 1.0 %collective-permute-done.22.refs_3_ = f32[9,512]{1,0:T(8,128)S(1)} collective-permute-done((f32[9,512]{1,0:T(8,128)S(1)}, f32[9,512]{1,0:T(8,128)S(1)}, u32[]{:S(2)}, u32[]{:S(2)}) %collective-permute-start.22) | collective-permute-done | bytes 18464 | tf_op jit(solution)/shard_map/ppermute | solution.py:508
  77.7 0.4 collective-permute-done.21.refs_2_
  78.1 0.8 %collective-permute-done.20.refs_1_ = f32[9,512]{1,0:T(8,128)S(1)} collective-permute-done((f32[9,512]{1,0:T(8,128)S(1)}, f32[9,512]{1,0:T(8,128)S(1)}, u32[]{:S(2)}, u32[]{:S(2)}) %collective-permute-start.20) | collective-permute-done | bytes 18464 | tf_op jit(solution)/shard_map/ppermute | solution.py:508
  78.9 0.6 shard_map.108
  79.5 0.0 collective-permute-done.16.got
  79.5 1.1 %shard_map.107 = bf16[256,512]{1,0:T(8,128)(2,1)} custom-call(bf16[256,512]{1,0:T(8,128)(2,1)S(1)} %get-tuple-element.57.xo, bf16[256,512]{1,0:T(8,128)(2,1)S(1)} %collective-permute-done.xp, f32[256,512]{1,0:T(8,128)S(1)} %get-tuple-element.93.keep, f32[256,128]{1,0:T(8,128)S(1)} %get-tuple-element.94.stat, ...), custom_call_target="tpu_custom_call" | custom-call | flops 10000000000 | bytes 10000000 | tf_op jit(solution)/shard_map/pallas_call | solution.py:419
  (9 shorter events, 0.1 us)
Async XLA Ops:
  0.6 13.0 %collective-permute-start.1 = (bf16[256,512]{1,0:T(8,128)(2,1)}, bf16[256,512]{1,0:T(8,128)(2,1)S(1)}, u32[]{:S(2)}, u32[]{:S(2)}) collective-permute-start(bf16[256,512]{1,0:T(8,128)(2,1)} %refs_4_.1), channel_id=1, source_target_pairs={{0,2},{2,0},{4,6},{6,4},{8,10},{10,8},{12,14},{14,12},{16,18},{18,... | collective-permute-start | bytes 786440 | tf_op jit(solution)/shard_map/ppermute | solution.py:439
  0.7 12.9 %collective-permute-start = (bf16[256,512]{1,0:T(8,128)(2,1)}, bf16[256,512]{1,0:T(8,128)(2,1)S(1)}, u32[]{:S(2)}, u32[]{:S(2)}) collective-permute-start(bf16[256,512]{1,0:T(8,128)(2,1)} %refs_4_.1), channel_id=1, source_target_pairs={{0,1},{1,0},{2,3},{3,2},{4,5},{5,4},{6,7},{7,6},{8,9},{9,8},{10,11... | collective-permute-start | bytes 786440 | tf_op jit(solution)/shard_map/ppermute | solution.py:436
  2.9 17.9 %collective-permute-start.4 = (bf16[256,512]{1,0:T(8,128)(2,1)}, bf16[256,512]{1,0:T(8,128)(2,1)S(1)}, u32[]{:S(2)}, u32[]{:S(2)}) collective-permute-start(bf16[256,512]{1,0:T(8,128)(2,1)} %refs_4_.1), channel_id=1, source_target_pairs={{2,5},{3,4},{6,9},{7,8},{10,13},{11,12},{14,17},{15,16},{18,21},{1... | collective-permute-start | bytes 786440 | tf_op jit(solution)/shard_map/ppermute | solution.py:450
  6.9 13.9 %collective-permute-start.3 = (bf16[256,512]{1,0:T(8,128)(2,1)}, bf16[256,512]{1,0:T(8,128)(2,1)S(1)}, u32[]{:S(2)}, u32[]{:S(2)}) collective-permute-start(bf16[256,512]{1,0:T(8,128)(2,1)} %refs_4_.1), channel_id=1, source_target_pairs={{2,4},{6,8},{10,12},{14,16},{18,20},{22,24},{26,28},{30,32},{34,36... | collective-permute-start | bytes 786440 | tf_op jit(solution)/shard_map/ppermute | solution.py:443
  13.6 1.3 %copy-start.4 = (bf16[1024,512]{1,0:T(8,128)(2,1)}, bf16[1024,512]{1,0:T(8,128)(2,1)S(1)}, u32[]{:S(2)}) copy-start(bf16[1024,512]{1,0:T(8,128)(2,1)S(1)} %get-tuple-element.63.wq) | copy-start | bytes 3145732
  13.6 7.3 %copy-start = (bf16[1024,512]{1,0:T(8,128)(2,1)}, bf16[1024,512]{1,0:T(8,128)(2,1)S(1)}, u32[]{:S(2)}) copy-start(bf16[1024,512]{1,0:T(8,128)(2,1)S(1)} %get-tuple-element.60.wk) | copy-start | bytes 3145732
  13.6 7.3 %copy-start.2 = (bf16[1024,512]{1,0:T(8,128)(2,1)}, bf16[1024,512]{1,0:T(8,128)(2,1)S(1)}, u32[]{:S(2)}) copy-start(bf16[1024,512]{1,0:T(8,128)(2,1)S(1)} %get-tuple-element.61.wv) | copy-start | bytes 3145732
  13.6 7.3 %collective-permute-start.2 = (bf16[256,512]{1,0:T(8,128)(2,1)S(1)}, bf16[256,512]{1,0:T(8,128)(2,1)S(1)}, u32[]{:S(2)}, u32[]{:S(2)}) collective-permute-start(bf16[256,512]{1,0:T(8,128)(2,1)S(1)} %collective-permute-done.xp), channel_id=1, source_target_pairs={{0,2},{2,0},{4,6},{6,4},{8,10},{10,8},{12,14},{14,12},{16,18},{18,... | collective-permute-start | bytes 786440 | tf_op jit(solution)/shard_map/ppermute | solution.py:439
  14.9 15.2 %collective-permute-start.7 = (bf16[304,512]{1,0:T(8,128)(2,1)S(1)}, bf16[304,512]{1,0:T(8,128)(2,1)S(1)}, u32[]{:S(2)}, u32[]{:S(2)}) collective-permute-start(bf16[304,512]{1,0:T(8,128)(2,1)S(1)} %get-tuple-element.76), channel_id=1, source_target_pairs={{0,1},{1,0},{2,3},{3,2},{4,5},{5,4},{6,7},{7,6},{8,9},{9,8},{10,11... | collective-permute-start | bytes 933896 | tf_op jit(solution)/shard_map/ppermute | solution.py:436
  24.1 7.3 %collective-permute-start.5 = (bf16[64,1024]{1,0:T(8,128)(2,1)S(1)}, bf16[64,1024]{1,0:T(8,128)(2,1)S(1)}, u32[]{:S(2)}, u32[]{:S(2)}) collective-permute-start(bf16[64,1024]{1,0:T(8,128)(2,1)S(1)} %get-tuple-element.69.part.rim), channel_id=1, source_target_pairs={{0,1},{1,0},{2,3},{3,2},{4,5},{5,4},{6,7},{7,6},{8,9},{9,8},{10,11... | collective-permute-start | bytes 393224 | tf_op jit(solution)/shard_map/ppermute | solution.py:436
  28.9 12.1 %collective-permute-start.6 = (bf16[192,1024]{1,0:T(8,128)(2,1)S(1)}, bf16[192,1024]{1,0:T(8,128)(2,1)S(1)}, u32[]{:S(2)}, u32[]{:S(2)}) collective-permute-start(bf16[192,1024]{1,0:T(8,128)(2,1)S(1)} %get-tuple-element.74.mid), channel_id=1, source_target_pairs={{0,1},{1,0},{2,3},{3,2},{4,5},{5,4},{6,7},{7,6},{8,9},{9,8},{10,11... | collective-permute-start | bytes 1179656 | tf_op jit(solution)/shard_map/ppermute | solution.py:436
  31.4 2.5 %collective-permute-start.8 = (bf16[32,1024]{1,0:T(8,128)(2,1)S(1)}, bf16[32,1024]{1,0:T(8,128)(2,1)S(1)}, u32[]{:S(2)}, u32[]{:S(2)}) collective-permute-start(bf16[32,1024]{1,0:T(8,128)(2,1)S(1)} %get-tuple-element.77), channel_id=1, source_target_pairs={{0,2},{2,0},{4,6},{6,4},{8,10},{10,8},{12,14},{14,12},{16,18},{18,... | collective-permute-start | bytes 196616 | tf_op jit(solution)/shard_map/ppermute | solution.py:439
  31.5 9.4 %collective-permute-start.9 = (bf16[32,1024]{1,0:T(8,128)(2,1)S(1)}, bf16[32,1024]{1,0:T(8,128)(2,1)S(1)}, u32[]{:S(2)}, u32[]{:S(2)}) collective-permute-start(bf16[32,1024]{1,0:T(8,128)(2,1)S(1)} %get-tuple-element.78), channel_id=1, source_target_pairs={{2,4},{6,8},{10,12},{14,16},{18,20},{22,24},{26,28},{30,32},{34,36... | collective-permute-start | bytes 196616 | tf_op jit(solution)/shard_map/ppermute | solution.py:443
  45.5 4.5 %collective-permute-start.10 = (f32[9,512]{1,0:T(8,128)S(1)}, f32[9,512]{1,0:T(8,128)S(1)}, u32[]{:S(2)}, u32[]{:S(2)}) collective-permute-start(f32[9,512]{1,0:T(8,128)S(1)} %get-tuple-element.87.refs_0_), channel_id=1, source_target_pairs={{0,2},{2,0},{4,6},{6,4},{8,10},{10,8},{12,14},{14,12},{16,18},{18,... | collective-permute-start | bytes 55304 | tf_op jit(solution)/shard_map/ppermute | solution.py:508
  46.9 21.9 %collective-permute-start.12 = (bf16[2,256,512]{2,1,0:T(8,128)(2,1)S(1)}, bf16[2,256,512]{2,1,0:T(8,128)(2,1)S(1)}, u32[]{:S(2)}, u32[]{:S(2)}) collective-permute-start(bf16[2,256,512]{2,1,0:T(8,128)(2,1)S(1)} %get-tuple-element.91), channel_id=1, source_target_pairs={{2,4},{6,8},{10,12},{14,16},{18,20},{22,24},{26,28},{30,32},{34,36... | collective-permute-start | bytes 1572872 | tf_op jit(solution)/shard_map/ppermute | solution.py:443
  50.0 11.7 %collective-permute-start.15 = (f32[9,512]{1,0:T(8,128)S(1)}, f32[9,512]{1,0:T(8,128)S(1)}, u32[]{:S(2)}, u32[]{:S(2)}) collective-permute-start(f32[9,512]{1,0:T(8,128)S(1)} %shard_map.101.refs_1_.after.refs_0_), channel_id=1, source_target_pairs={{0,192},{2,194},{4,196},{6,198},{8,200},{10,202},{12,204},{14,206}... | collective-permute-start | bytes 55304 | tf_op jit(solution)/shard_map/ppermute | solution.py:508
  56.4 8.1 %collective-permute-start.14 = (f32[9,512]{1,0:T(8,128)S(1)}, f32[9,512]{1,0:T(8,128)S(1)}, u32[]{:S(2)}, u32[]{:S(2)}) collective-permute-start(f32[9,512]{1,0:T(8,128)S(1)} %shard_map.101.refs_1_.after.refs_0_), channel_id=1, source_target_pairs={{0,128},{2,130},{4,132},{6,134},{8,136},{10,138},{12,140},{14,142}... | collective-permute-start | bytes 55304 | tf_op jit(solution)/shard_map/ppermute | solution.py:508
  57.4 7.1 %collective-permute-start.13 = (f32[9,512]{1,0:T(8,128)S(1)}, f32[9,512]{1,0:T(8,128)S(1)}, u32[]{:S(2)}, u32[]{:S(2)}) collective-permute-start(f32[9,512]{1,0:T(8,128)S(1)} %shard_map.101.refs_1_.after.refs_0_), channel_id=1, source_target_pairs={{0,64},{2,66},{4,68},{6,70},{8,72},{10,74},{12,76},{14,78},{16,80}... | collective-permute-start | bytes 55304 | tf_op jit(solution)/shard_map/ppermute | solution.py:508
  58.8 1.3 %copy-start.5 = (bf16[1024,512]{1,0:T(8,128)(2,1)S(1)}, bf16[1024,512]{1,0:T(8,128)(2,1)}, u32[]{:S(2)}) copy-start(bf16[1024,512]{1,0:T(8,128)(2,1)} %copy-done.4) | copy-start | bytes 3145732
  60.0 8.8 %collective-permute-start.11 = (bf16[2,256,512]{2,1,0:T(8,128)(2,1)S(1)}, bf16[2,256,512]{2,1,0:T(8,128)(2,1)S(1)}, u32[]{:S(2)}, u32[]{:S(2)}) collective-permute-start(bf16[2,256,512]{2,1,0:T(8,128)(2,1)S(1)} %get-tuple-element.90), channel_id=1, source_target_pairs={{0,2},{2,0},{4,6},{6,4},{8,10},{10,8},{12,14},{14,12},{16,18},{18,... | collective-permute-start | bytes 1572872 | tf_op jit(solution)/shard_map/ppermute | solution.py:439
  61.6 7.2 %copy-start.1 = (bf16[1024,512]{1,0:T(8,128)(2,1)S(1)}, bf16[1024,512]{1,0:T(8,128)(2,1)}, u32[]{:S(2)}) copy-start(bf16[1024,512]{1,0:T(8,128)(2,1)} %copy-done) | copy-start | bytes 3145732
  61.6 7.2 %copy-start.3 = (bf16[1024,512]{1,0:T(8,128)(2,1)S(1)}, bf16[1024,512]{1,0:T(8,128)(2,1)}, u32[]{:S(2)}) copy-start(bf16[1024,512]{1,0:T(8,128)(2,1)} %copy-done.2) | copy-start | bytes 3145732
  64.5 6.6 %collective-permute-start.19 = (f32[9,512]{1,0:T(8,128)S(1)}, f32[9,512]{1,0:T(8,128)S(1)}, u32[]{:S(2)}, u32[]{:S(2)}) collective-permute-start(f32[9,512]{1,0:T(8,128)S(1)} %shard_map.104.after.refs_0_), channel_id=1, source_target_pairs={{0,48},{2,50},{4,52},{6,54},{8,56},{10,58},{12,60},{14,62},{16,32}... | collective-permute-start | bytes 55304 | tf_op jit(solution)/shard_map/ppermute | solution.py:508
  68.1 3.9 %collective-permute-start.18 = (f32[9,512]{1,0:T(8,128)S(1)}, f32[9,512]{1,0:T(8,128)S(1)}, u32[]{:S(2)}, u32[]{:S(2)}) collective-permute-start(f32[9,512]{1,0:T(8,128)S(1)} %shard_map.104.after.refs_0_), channel_id=1, source_target_pairs={{0,32},{2,34},{4,36},{6,38},{8,40},{10,42},{12,44},{14,46},{16,48}... | collective-permute-start | bytes 55304 | tf_op jit(solution)/shard_map/ppermute | solution.py:508
  68.1 4.3 %collective-permute-start.17 = (f32[9,512]{1,0:T(8,128)S(1)}, f32[9,512]{1,0:T(8,128)S(1)}, u32[]{:S(2)}, u32[]{:S(2)}) collective-permute-start(f32[9,512]{1,0:T(8,128)S(1)} %shard_map.104.after.refs_0_), channel_id=1, source_target_pairs={{0,16},{2,18},{4,20},{6,22},{8,24},{10,26},{12,28},{14,30},{16,0},... | collective-permute-start | bytes 55304 | tf_op jit(solution)/shard_map/ppermute | solution.py:508
  69.7 9.8 %collective-permute-start.16 = (bf16[256,640]{1,0:T(8,128)(2,1)S(1)}, bf16[256,640]{1,0:T(8,128)(2,1)S(1)}, u32[]{:S(2)}, u32[]{:S(2)}) collective-permute-start(bf16[256,640]{1,0:T(8,128)(2,1)S(1)} %get-tuple-element.95), channel_id=1, source_target_pairs={{0,1},{1,0},{2,3},{3,2},{4,5},{5,4},{6,7},{7,6},{8,9},{9,8},{10,11... | collective-permute-start | bytes 983048 | tf_op jit(solution)/shard_map/ppermute | solution.py:436
  72.5 5.2 %collective-permute-start.22 = (f32[9,512]{1,0:T(8,128)S(1)}, f32[9,512]{1,0:T(8,128)S(1)}, u32[]{:S(2)}, u32[]{:S(2)}) collective-permute-start(f32[9,512]{1,0:T(8,128)S(1)} %shard_map.106.after.refs_0_), channel_id=1, source_target_pairs={{0,12},{2,14},{4,8},{6,10},{8,4},{10,6},{12,0},{14,2},{16,28},{18,... | collective-permute-start | bytes 55304 | tf_op jit(solution)/shard_map/ppermute | solution.py:508
  72.6 5.5 %collective-permute-start.21 = (f32[9,512]{1,0:T(8,128)S(1)}, f32[9,512]{1,0:T(8,128)S(1)}, u32[]{:S(2)}, u32[]{:S(2)}) collective-permute-start(f32[9,512]{1,0:T(8,128)S(1)} %shard_map.106.after.refs_0_), channel_id=1, source_target_pairs={{0,8},{2,10},{4,12},{6,14},{8,0},{10,2},{12,4},{14,6},{16,24},{18,... | collective-permute-start | bytes 55304 | tf_op jit(solution)/shard_map/ppermute | solution.py:508
  73.9 4.9 %collective-permute-start.20 = (f32[9,512]{1,0:T(8,128)S(1)}, f32[9,512]{1,0:T(8,128)S(1)}, u32[]{:S(2)}, u32[]{:S(2)}) collective-permute-start(f32[9,512]{1,0:T(8,128)S(1)} %shard_map.106.after.refs_0_), channel_id=1, source_target_pairs={{0,4},{2,6},{4,0},{6,2},{8,12},{10,14},{12,8},{14,10},{16,20},{18,... | collective-permute-start | bytes 55304 | tf_op jit(solution)/shard_map/ppermute | solution.py:508

commit v5 on v4

--- a/solution.py
+++ b/solution.py
@@ -133,8 +133,7 @@
     part[:, SHARE:] = nn(att[...], wo[:, other]).astype(BF16)
 
 
-def attend_rim_kernel(a0, a1, b0, b1, wk, wv, wo, q, k, v, ka, va, kb, vb, p, att, part):
-    halo_kv(a0, a1, wk, wv, ka, va)
+def attend_rim_kernel(b0, b1, wk, wv, wo, q, k, v, ka, va, kb, vb, p, att, part):
     halo_kv(b0, b1, wk, wv, kb, vb)
     rows = (slice(0, RIM), slice(ROWS - RIM, ROWS))
     attend(rows, q, k, v, ka, va, kb, vb, wo, p, att, part)
@@ -157,20 +156,31 @@
     )
 
 
-def merge_kernel(part, part_p, co, cp, to_a, to_b):
+def merge_kernel(part, part_p, co, cp, xo, xp, to_a, to_b):
     for at, at_c, out in zip(edge_rows(2 * RIM), edge_rows(ROWS), (to_a, to_b)):
         mine = part[at, :].astype(F32)
         theirs = part_p[at, :].astype(F32)
         out[:EDGE, :SHARE] = (mine[:, :SHARE] + theirs[:, SHARE:]).astype(BF16)
         out[:EDGE, SHARE:] = (mine[:, SHARE:] + theirs[:, :SHARE]).astype(BF16)
-        out[EDGE:, :SHARE] = co[at_c, :]
-        out[EDGE:, SHARE:] = cp[at_c, :]
+        out[EDGE:2 * EDGE, :SHARE] = co[at_c, :]
+        out[EDGE:2 * EDGE, SHARE:] = cp[at_c, :]
+        out[2 * EDGE:, :SHARE] = xo[at_c, :]
+        out[2 * EDGE:, SHARE:] = xp[at_c, :]
+
+
+def prepare_kernel(xo, xp, co, cp, no, np_, rstd, cs):
+    no[...], np_[...], scale = norm_pair(xo[...], xp[...])
+    rstd[...] = jnp.broadcast_to(scale, (ROWS, LANES))
+    for c in range(HALF_CHUNKS):
+        f = slice(c * LANES, (c + 1) * LANES)
+        cs[c] = co[:, f].astype(F32)
+        cs[HALF_CHUNKS + c] = cp[:ROWS, f].astype(F32)
 
 
 def conv_kernel(
-    xo, xp, a0, a1, b0, b1, rim, rim_p, mid, mid_p, ea, eb, co, cp, to, wo,
+    xo, xp, rim, rim_p, mid, mid_p, ea, eb, cs, cp, to, wo,
     output, dh, datt, gk,
-    n2s, cs, dzs, dns, hs, taps, rs2, sum0, sum1, dhb,
+    n2s, ends, dzs, dns, hs, taps, rs2, sum0, sum1, dhb,
 ):
     odd, left, right = placement()
     own, other = own_other()
@@ -194,14 +204,10 @@
         center, rstd = moments(ho, hp)
         hs[rows, :] = ho
         rs2[rows, :] = jnp.broadcast_to(rstd, (step, LANES))
-        ctan = co[rows, :].astype(F32)
-        ctan_p = cp[rows, :].astype(F32)
         for c in range(HALF_CHUNKS):
             f = slice(c * LANES, (c + 1) * LANES)
             n2s[c, held, :] = (ho[:, f] - center) * rstd
             n2s[HALF_CHUNKS + c, held, :] = (hp[:, f] - center) * rstd
-            cs[c, held, :] = ctan[:, f]
-            cs[HALF_CHUNKS + c, held, :] = ctan_p[:, f]
         return carry
 
     for first, last, part, part_p, shift in (
@@ -210,30 +216,30 @@
         (ROWS - RIM, ROWS, rim, rim_p, MID),
     ):
         body = functools.partial(rows_in, part=part, part_p=part_p, shift=shift)
-        lax.fori_loop(first // step, last // step, body, 0)
+        lax.fori_loop(first // step, last // step, body, 0, unroll=True)
 
     pa = ea[:EDGE, :].astype(F32)
     pb = eb[:EDGE, :].astype(F32)
     sides = (
-        (slice(ROWS - EDGE, ROWS), is_odd, 0, left),
-        (slice(0, EDGE), jnp.logical_not(is_odd), PAD + ROWS, right),
-    )
-    for x_rows, from_a, at, valid in sides:
+        (is_odd, 0, 0, left),
+        (jnp.logical_not(is_odd), PAD + ROWS, EDGE, right),
+    )
+    for from_a, at, end, valid in sides:
         def pick(one, two):
             return jnp.where(from_a, one.astype(F32), two.astype(F32))
 
         pe = pick(pa, pb)
-        ho = pick(a0[x_rows, :], b0[x_rows, :]) + pe[:, :SHARE]
-        hp = pick(a1[x_rows, :], b1[x_rows, :]) + pe[:, SHARE:]
+        ho = pick(ea[2 * EDGE:, :SHARE], eb[2 * EDGE:, :SHARE]) + pe[:, :SHARE]
+        hp = pick(ea[2 * EDGE:, SHARE:], eb[2 * EDGE:, SHARE:]) + pe[:, SHARE:]
         center, rstd = moments(ho, hp)
-        ctan = pick(ea[EDGE:, :SHARE], eb[EDGE:, :SHARE])
-        ctan_p = pick(ea[EDGE:, SHARE:], eb[EDGE:, SHARE:])
+        ctan = pick(ea[EDGE:2 * EDGE, :SHARE], eb[EDGE:2 * EDGE, :SHARE])
+        ctan_p = pick(ea[EDGE:2 * EDGE, SHARE:], eb[EDGE:2 * EDGE, SHARE:])
         inside = valid == 1
         for c in range(HALF_CHUNKS):
             f = slice(c * LANES, (c + 1) * LANES)
             for d, hh, cc in ((c, ho, ctan), (HALF_CHUNKS + c, hp, ctan_p)):
                 n2s[d, at:at + EDGE, :] = jnp.where(inside, (hh[:, f] - center) * rstd, 0.0)
-                cs[d, at:at + EDGE, :] = jnp.where(inside, cc[:, f], 0.0)
+                ends[d, end:end + EDGE, :] = jnp.where(inside, cc[:, f], 0.0)
 
     piece = 136
 
@@ -245,51 +251,52 @@
                 at = r0 + tap - HALF
                 z = z + w[tap:tap + 1, :] * n2s[c, at:at + piece, :]
             gate = jax.nn.sigmoid(z)
-            dzs[c, r0:r0 + piece, :] = cs[c, r0:r0 + piece, :] * gate * (1.0 + z * (1.0 - gate))
+            if r0 < PAD:
+                ctan = jnp.concatenate([ends[c, r0:PAD, :], cs[c, :r0 + piece - PAD, :]], axis=0)
+            else:
+                ctan = jnp.concatenate([cs[c, r0 - PAD:, :], ends[c, EDGE:PAD + 8, :]], axis=0)
+            dzs[c, r0:r0 + piece, :] = ctan * gate * (1.0 + z * (1.0 - gate))
             if mine:
                 lo = max(r0, PAD)
                 hi = min(r0 + piece, PAD + ROWS)
                 lane = pl.ds(pl.multiple_of(c * LANES, LANES), LANES)
                 mix = (z * gate)[lo - r0:hi - r0, :]
-                hs[lo - PAD:hi - PAD, lane] = hs[lo - PAD:hi - PAD, lane] + mix
-        if mine:
-            lane = pl.ds(pl.multiple_of(c * LANES, LANES), LANES)
-            dz = dzs[c, PAD:PAD + ROWS, :]
-            for tap in range(KW):
-                at = PAD + tap - HALF
-                gk[tap:tap + 1, lane] = jnp.sum(
-                    dz * n2s[c, at:at + ROWS, :], axis=0, keepdims=True
-                )
+                output[lo - PAD:hi - PAD, lane] = (hs[lo - PAD:hi - PAD, lane] + mix).astype(BF16)
         return carry
 
-    lax.fori_loop(0, HALF_CHUNKS, functools.partial(forward, mine=True), 0)
-    lax.fori_loop(HALF_CHUNKS, CHUNKS, functools.partial(forward, mine=False), 0)
-    output[...] = hs[...].astype(BF16)
+    lax.fori_loop(0, HALF_CHUNKS, functools.partial(forward, mine=True), 0, unroll=2)
+    lax.fori_loop(HALF_CHUNKS, CHUNKS, functools.partial(forward, mine=False), 0, unroll=2)
 
     sum0[...] = jnp.zeros_like(sum0)
     sum1[...] = jnp.zeros_like(sum1)
 
-    def backward(c, carry):
+    def backward(c, carry, mine):
         w = taps[c]
         for r0 in (0, ROWS // 2):
-            at = PAD + r0 + HALF
-            g = w[0:1, :] * dzs[c, at:at + ROWS // 2, :]
-            for tap in range(1, KW):
+            half = slice(r0, r0 + ROWS // 2)
+            n2 = n2s[c, PAD + r0:PAD + r0 + ROWS // 2, :]
+            g = 0.0
+            for tap in range(KW):
                 at = PAD + r0 + HALF - tap
-                g = g + w[tap:tap + 1, :] * dzs[c, at:at + ROWS // 2, :]
-            dns[c, r0:r0 + ROWS // 2, :] = g
-            half = slice(r0, r0 + ROWS // 2)
+                dz = dzs[c, at:at + ROWS // 2, :]
+                g = g + w[tap:tap + 1, :] * dz
+                if mine:
+                    lane = pl.ds(pl.multiple_of(c * LANES, LANES), LANES)
+                    part = jnp.sum(dz * n2, axis=0, keepdims=True)
+                    gk[tap:tap + 1, lane] = part if r0 == 0 else gk[tap:tap + 1, lane] + part
+            dns[c, half, :] = g
             sum0[half, :] = sum0[half, :] + g
-            sum1[half, :] = sum1[half, :] + g * n2s[c, PAD + r0:PAD + r0 + ROWS // 2, :]
+            sum1[half, :] = sum1[half, :] + g * n2
         return carry
 
-    lax.fori_loop(0, CHUNKS, backward, 0)
+    lax.fori_loop(0, HALF_CHUNKS, functools.partial(backward, mine=True), 0, unroll=2)
+    lax.fori_loop(HALF_CHUNKS, CHUNKS, functools.partial(backward, mine=False), 0, unroll=2)
     sum0[...] = jnp.broadcast_to(row_sum(sum0[...]) * (1.0 / D), (ROWS, LANES))
     sum1[...] = jnp.broadcast_to(row_sum(sum1[...]) * (1.0 / D), (ROWS, LANES))
 
     def finish(c, carry, mine):
         lane = pl.ds(pl.multiple_of(c * LANES, LANES), LANES)
-        value = cs[c, PAD:PAD + ROWS, :] + rs2[...] * (
+        value = cs[c] + rs2[...] * (
             dns[c] - sum0[...] - n2s[c, PAD:PAD + ROWS, :] * sum1[...]
         )
         if mine:
@@ -297,8 +304,8 @@
         dhb[:, lane] = value.astype(BF16)
         return carry
 
-    lax.fori_loop(0, HALF_CHUNKS, functools.partial(finish, mine=True), 0)
-    lax.fori_loop(HALF_CHUNKS, CHUNKS, functools.partial(finish, mine=False), 0)
+    lax.fori_loop(0, HALF_CHUNKS, functools.partial(finish, mine=True), 0, unroll=True)
+    lax.fori_loop(HALF_CHUNKS, CHUNKS, functools.partial(finish, mine=False), 0, unroll=True)
     datt[...] = (nt(dhb[:, :SHARE], wo[:, own]) + nt(dhb[:, SHARE:], wo[:, other])).astype(BF16)
 
 
@@ -339,15 +346,14 @@
     pin[:, SHARE:] = nt(dq, wq[other, :])
 
 
-def project_kernel(xo, xp, dkv, got_a, got_b, pin, wk, wv, after, send, keep, stat):
+def project_kernel(n1o, n1p, dkv, got_a, got_b, pin, wk, wv, after, send, keep, stat):
     own, other = own_other()
     dk = (dkv[0] + got_a[0].astype(F32) + got_b[0].astype(F32)).astype(BF16)
     dv = (dkv[1] + got_a[1].astype(F32) + got_b[1].astype(F32)).astype(BF16)
     p_own = pin[:, :SHARE] + nt(dk, wk[own, :]) + nt(dv, wv[own, :])
     p_other = pin[:, SHARE:] + nt(dk, wk[other, :]) + nt(dv, wv[other, :])
-    no, np_, _ = norm_pair(xo[...], xp[...])
     s0 = row_sum(p_own) + row_sum(p_other)
-    s1 = row_sum(p_own * no) + row_sum(p_other * np_)
+    s1 = row_sum(p_own * n1o[...]) + row_sum(p_other * n1p[...])
     keep[...] = p_own
     send[:, :SHARE] = p_other.astype(BF16)
     lane = lax.broadcasted_iota(jnp.int32, (ROWS, LANES), 1)
@@ -361,14 +367,14 @@
     stat[...] = jnp.where(lane == 0, s0, jnp.where(lane == 2, s1, 0.0))
 
 
-def final_kernel(xo, xp, keep, stat, got, dh, after, grad):
-    no, _, rstd = norm_pair(xo[...], xp[...])
+def final_kernel(n1o, rstd, keep, stat, got, dh, row, one, two, three, grad, taps):
+    taps[...] = (row[...] + one[...]) + (two[...] + three[...])
     dn1 = keep[...] + got[:, :SHARE].astype(F32)
     lane = lax.broadcasted_iota(jnp.int32, (ROWS, LANES), 1)
     sums = stat[...] + got[:, SHARE:].astype(F32)
     s0 = row_sum(jnp.where(lane < 2, sums, 0.0)) * (1.0 / D)
     s1 = row_sum(jnp.where(lane < 2, 0.0, sums)) * (1.0 / D)
-    grad[...] = (dh[...] + rstd * (dn1 - s0 - no * s1)).astype(BF16)
+    grad[...] = (dh[...] + rstd[:, :1] * (dn1 - s0 - n1o[...] * s1)).astype(BF16)
 
 
 def sum_kernel(*refs):
@@ -452,25 +458,25 @@
     xp = over_head(inputs)
     b0 = over_b(inputs)
     b1 = over_b_and_head(inputs)
-    a0 = over_a(inputs)
     *staged, pack = stage(w_query, w_key, w_value, w_out, inputs, cotangent, kernel)
-    xp, a0, *staged = lax.optimization_barrier((xp, a0, *staged))
+    xp, *staged = lax.optimization_barrier((xp, *staged))
     w_query, w_key, w_value, w_out, inputs, cotangent, kernel = staged
-    a1 = over_a(xp)
     q, k, v = call(
         own_kernel, (inputs, xp, w_query, w_key, w_value), (big, big, big), us=0.0
     )
+    ka = over_a(k)
+    va = over_a(v)
     q, pack = lax.optimization_barrier((q, pack))
     pack_p = over_head(pack)
-    edge = ((2 * EDGE, D), BF16)
+    edge = ((3 * EDGE, D), BF16)
     chunk = [
         (((HEADS, rows, 3 * ROWS), BF16), ((rows, SHARE), BF16), ((rows, D), BF16))
         for rows in (2 * RIM, MID)
     ]
-    ka, va, kb, vb, p_rim, att_rim, rim = call(
+    kb, vb, p_rim, att_rim, rim = call(
         attend_rim_kernel,
-        (a0, a1, b0, b1, w_key, w_value, w_out, q, k, v),
-        (big, big, big, big, *chunk[0]),
+        (b0, b1, w_key, w_value, w_out, q, k, v, ka, va),
+        (big, big, *chunk[0]),
         us=2.0,
     )
     rim_p = over_head(rim)
@@ -480,7 +486,13 @@
     mid_p = over_head(mid)
     attended = (att_rim, att_mid, p_rim, p_mid)
     to_a, to_b = call(
-        merge_kernel, (rim, rim_p, cotangent, pack_p), (edge, edge), us=3.0
+        merge_kernel, (rim, rim_p, cotangent, pack_p, inputs, xp), (edge, edge), us=3.0
+    )
+    chunked_rows = ((CHUNKS, ROWS, LANES), F32)
+    wide = ((ROWS, SHARE), F32)
+    tall = ((ROWS, LANES), F32)
+    n1o, n1p, rstd, cot_chunks = call(
+        prepare_kernel, (inputs, xp, cotangent, pack_p), (wide, wide, tall, chunked_rows), us=3.0
     )
     eb = over_b(to_b)
     ea = over_a(to_a)
@@ -489,25 +501,29 @@
     output, dh, datt, gk = call(
         conv_kernel,
         (
-            inputs, xp, a0, a1, b0, b1, rim, rim_p, mid, mid_p, ea, eb, cotangent, pack_p,
+            inputs, xp, rim, rim_p, mid, mid_p, ea, eb, cot_chunks, pack_p,
             kernel, w_out,
         ),
         (big, ((ROWS, SHARE), F32), big, ((KW, SHARE), F32)),
         scratch=(
-            chunked, chunked, chunked, ((CHUNKS, ROWS, LANES), F32), ((ROWS, SHARE), F32),
+            chunked, ((CHUNKS, 2 * EDGE, LANES), F32), chunked, chunked_rows, ((ROWS, SHARE), F32),
             ((CHUNKS, 16, LANES), F32), tall, tall, tall, ((ROWS, D), BF16),
         ),
         us=5.0,
         mib=12,
     )
+    assert count == 128
+    tap_sums = ((KW, SHARE), F32)
+
+    def swaps(value, steps):
+        return [
+            lax.ppermute(value, "tm", [(i, i ^ step) for i in range(count)]) for step in steps
+        ]
+
     chain = [gk]
-    assert count == 128
-    for steps in ((1,), (32, 64, 96), (8, 16, 24), (2, 4, 6)):
-        last = chain[-1]
-        parts = [
-            lax.ppermute(last, "tm", [(i, i ^ step) for i in range(count)]) for step in steps
-        ]
-        chain.extend(call(sum_kernel, (last, *parts), (((KW, SHARE), F32),), us=0.2, mib=1))
+    for steps in ((1,), (32, 64, 96), (8, 16, 24)):
+        parts = (chain[-1], *swaps(chain[-1], steps))
+        chain.extend(call(sum_kernel, parts, (tap_sums,), us=0.6, mib=1))
     pair = ((2, ROWS, SHARE), BF16)
     dq_b, dkv_b = call(
         functools.partial(back_halo_kernel, which=2),
@@ -531,15 +547,18 @@
     )
     send, keep, stat = call(
         project_kernel,
-        (inputs, xp, dkv, got_a, got_b, pin, w_key, w_value, chain[2]),
+        (n1o, n1p, dkv, got_a, got_b, pin, w_key, w_value, chain[2]),
         (((ROWS, SHARE + LANES), BF16), ((ROWS, SHARE), F32), tall),
         us=1.5,
     )
     got = over_head(send)
-    (grad,) = call(
-        final_kernel, (inputs, xp, keep, stat, got, dh, chain[3]), (big,), us=1.0
-    )
-    return output, grad, chain[-1]
+    grad, grad_taps = call(
+        final_kernel,
+        (n1o, rstd, keep, stat, got, dh, chain[3], *swaps(chain[3], (2, 4, 6))),
+        (big, tap_sums),
+        us=1.0,
+    )
+    return output, grad, grad_taps
 
 
 def solution(mesh):

time: 81.1 us -> 79.8 us (0.984)
  Pallas kernels: 20.3 us -> 18.7 us
    pallas_call x14, Pallas kernels: 17.9 us -> 16.3 us  [call(): pl.pallas_call(kernel, out_shape=[jax.ShapeDtypeStruct(shape, dtype) for...]
    ppermute x5, starting transfers between devices: 8.6 us -> 7.72 us  [over_head(): return lax.ppermute(value, 'head', [(0, 1), (1, 0)])]
  transfers between devices with their start and end apart: 23 -> 23, of which waited for: 9 -> 9; matrix products, arithmetic and copies ran while one was open for 0% -> 0% of each run, Pallas kernels for 18% -> 17%
where the time goes in v5:
time: 79.8 us; the launch traced here: 79.2 us
  starting transfers between devices  40.2 us (50%)
  waiting for transfers between devices  19.2 us (24%)
  Pallas kernels  18.7 us (23%)
  between operations  0.93 us (1%)
    ppermute x10, starting transfers between devices, swaps(): lax.ppermute(value, 'tm', [(i, i ^ step) for i in range(count)])  18 us
    pallas_call x14, Pallas kernels, call(): pl.pallas_call(kernel, out_shape=[jax.ShapeDtypeStruct(shape, dtype) for...  16.3 us
    ppermute x3, starting transfers between devices, over_b(): return lax.ppermute(value, 'tm', pairs + [(j, i) for i, j in pairs])  10.3 us
    ppermute x5, starting transfers between devices, over_head(): return lax.ppermute(value, 'head', [(0, 1), (1, 0)])  7.72 us
    ppermute x3, waiting for transfers between devices, over_b(): return lax.ppermute(value, 'tm', pairs + [(j, i) for i, j in pairs])  7.35 us
    ppermute x10, waiting for transfers between devices, swaps(): lax.ppermute(value, 'tm', [(i, i ^ step) for i in range(count)])  7.05 us
    ppermute x1, waiting for transfers between devices, over_b_and_head(): return lax.ppermute(value, ('tm', 'head'), crossed)  3.97 us
    ppermute x1, starting transfers between devices, over_b_and_head(): return lax.ppermute(value, ('tm', 'head'), crossed)  3.38 us
  transfers between devices with their start and end apart: 23, of which 9 were waited for; matrix products, arithmetic and copies ran while one was open for 0% of the time, Pallas kernels for 17%

profile of v5, /device:TPU:2, one launch (start us, length us, event | category | flops | bytes accessed | tf_op | source)
XLA Modules:
  0.0 79.2 jit_solution(8785186212048884794)
XLA Ops:
  0.6 2.2 %collective-permute-start = (bf16[256,512]{1,0:T(8,128)(2,1)}, bf16[256,512]{1,0:T(8,128)(2,1)S(1)}, u32[]{:S(2)}, u32[]{:S(2)}) collective-permute-start(bf16[256,512]{1,0:T(8,128)(2,1)} %refs_4_.1), channel_id=1, source_target_pairs={{0,1},{1,0},{2,3},{3,2},{4,5},{5,4},{6,7},{7,6},{8,9},{9,8},{10,11... | collective-permute-start | bytes 786440 | tf_op jit(solution)/shard_map/ppermute | solution.py:442
  2.8 3.4 %collective-permute-start.2 = (bf16[256,512]{1,0:T(8,128)(2,1)}, bf16[256,512]{1,0:T(8,128)(2,1)S(1)}, u32[]{:S(2)}, u32[]{:S(2)}) collective-permute-start(bf16[256,512]{1,0:T(8,128)(2,1)} %refs_4_.1), channel_id=1, source_target_pairs={{2,5},{3,4},{6,9},{7,8},{10,13},{11,12},{14,17},{15,16},{18,21},{1... | collective-permute-start | bytes 786440 | tf_op jit(solution)/shard_map/ppermute | solution.py:456
  6.2 4.8 %collective-permute-start.1 = (bf16[256,512]{1,0:T(8,128)(2,1)}, bf16[256,512]{1,0:T(8,128)(2,1)S(1)}, u32[]{:S(2)}, u32[]{:S(2)}) collective-permute-start(bf16[256,512]{1,0:T(8,128)(2,1)} %refs_4_.1), channel_id=1, source_target_pairs={{2,4},{6,8},{10,12},{14,16},{18,20},{22,24},{26,28},{30,32},{34,36... | collective-permute-start | bytes 786440 | tf_op jit(solution)/shard_map/ppermute | solution.py:449
  11.1 2.4 %shard_map.94 = (bf16[1024,512]{1,0:T(8,128)(2,1)S(1)}, bf16[1024,512]{1,0:T(8,128)(2,1)S(1)}, bf16[1024,512]{1,0:T(8,128)(2,1)S(1)}, bf16[512,1024]{1,0:T(8,128...) custom-call(bf16[1024,512]{1,0:T(8,128)(2,1)} %refs_0_.1, ...), custom_call_target="tpu_custom_call" | custom-call | bytes 67108864 | tf_op jit(solution)/shard_map/pallas_call | solution.py:412
  13.5 0.0 copy-start.4
  13.5 0.0 copy-start
  13.5 0.0 collective-permute-done.xp
  13.5 1.1 %shard_map.95 = (bf16[256,512]{1,0:T(8,128)(2,1)S(1)}, bf16[256,512]{1,0:T(8,128)(2,1)S(1)}, bf16[256,512]{1,0:T(8,128)(2,1)S(1)}) custom-call(bf16[256,512]{1,0:T(8,128)(2,1)S(1)} %get-tuple-element.60.xo, bf16[256,512]{1,0:T(8,128)(2,1)S(1)} %collective-permute-done.xp, bf16[1024,512]{1,0:T(8,128)(2,1)S(1)} %get-tuple-element.65.wq, ...), custom_call_target="tpu_custom_call" | custom-call | tf_op jit(solution)/shard_map/pallas_call | solution.py:425
  14.7 0.0 copy-start.6
  14.7 0.1 collective-permute-start.3
  14.8 0.5 collective-permute-start.4
  15.3 0.9 %collective-permute-start.7 = (bf16[304,512]{1,0:T(8,128)(2,1)S(1)}, bf16[304,512]{1,0:T(8,128)(2,1)S(1)}, u32[]{:S(2)}, u32[]{:S(2)}) collective-permute-start(bf16[304,512]{1,0:T(8,128)(2,1)S(1)} %get-tuple-element.76), channel_id=1, source_target_pairs={{0,1},{1,0},{2,3},{3,2},{4,5},{5,4},{6,7},{7,6},{8,9},{9,8},{10,11... | collective-permute-start | bytes 933896 | tf_op jit(solution)/shard_map/ppermute | solution.py:442
  16.2 4.0 %collective-permute-done.2.b1 = bf16[256,512]{1,0:T(8,128)(2,1)S(1)} collective-permute-done((bf16[256,512]{1,0:T(8,128)(2,1)}, bf16[256,512]{1,0:T(8,128)(2,1)S(1)}, u32[]{:S(2)}, u32[]{:S(2)}) %collective-permute-start.2) | collective-permute-done | bytes 262176 | tf_op jit(solution)/shard_map/ppermute | solution.py:456
  20.2 0.0 collective-permute-done.1.b0
  20.2 0.0 collective-permute-done.3.ka.k
  20.2 0.0 collective-permute-done.4.va.v
  20.2 2.7 %shard_map.96 = (bf16[256,512]{1,0:T(8,128)(2,1)S(1)}, bf16[256,512]{1,0:T(8,128)(2,1)S(1)}, bf16[4,64,768]{2,1,0:T(8,128)(2,1)S(1)}, bf16[64,512]{1,0:T(8,128)(2,1)S(1)}, bf16[64,1024]{1,0:T(8,128)(2,1)S(1)}) custom-call(bf16[256,512]{1,0:T(8,128)(2,1)S(1)} %collective-permute-done.1.b0, bf16[256,512]{1,0:T(8,128)(2,1)S(1)} %collective-permute-done.2.b1, ...), custom_call_target="tpu_custom_call" | custom-call | flops 20000000000 | bytes 20000000 | tf_op jit(solution)/shard_map/pallas_call | solution.py:425
  22.9 2.5 %collective-permute-start.5 = (bf16[64,1024]{1,0:T(8,128)(2,1)S(1)}, bf16[64,1024]{1,0:T(8,128)(2,1)S(1)}, u32[]{:S(2)}, u32[]{:S(2)}) collective-permute-start(bf16[64,1024]{1,0:T(8,128)(2,1)S(1)} %get-tuple-element.71.part.rim), channel_id=1, source_target_pairs={{0,1},{1,0},{2,3},{3,2},{4,5},{5,4},{6,7},{7,6},{8,9},{9,8},{10,11... | collective-permute-start | bytes 393224 | tf_op jit(solution)/shard_map/ppermute | solution.py:442
  25.4 0.0 copy-done.6
  25.4 2.2 %shard_map.97 = (bf16[4,192,768]{2,1,0:T(8,128)(2,1)S(1)}, bf16[192,512]{1,0:T(8,128)(2,1)S(1)}, bf16[192,1024]{1,0:T(8,128)(2,1)S(1)}) custom-call(bf16[512,1024]{1,0:T(8,128)(2,1)S(1)} %get-tuple-element.64.wo, bf16[256,512]{1,0:T(8,128)(2,1)S(1)} %get-tuple-element.68.q, bf16[256,512]{1,0:T(8,128)(2,1)S(1)} %get-tuple-element.69.k, ...), custom_call_target="tpu_custom_call" | custom-call | flops 20000000000 | bytes 20000000 | tf_op jit(solution)/shard_map/pallas_call | solution.py:425
  27.6 1.2 %collective-permute-start.6 = (bf16[192,1024]{1,0:T(8,128)(2,1)S(1)}, bf16[192,1024]{1,0:T(8,128)(2,1)S(1)}, u32[]{:S(2)}, u32[]{:S(2)}) collective-permute-start(bf16[192,1024]{1,0:T(8,128)(2,1)S(1)} %get-tuple-element.74.mid), channel_id=1, source_target_pairs={{0,1},{1,0},{2,3},{3,2},{4,5},{5,4},{6,7},{7,6},{8,9},{9,8},{10,11... | collective-permute-start | bytes 1179656 | tf_op jit(solution)/shard_map/ppermute | solution.py:442
  28.8 0.0 collective-permute-done.7.cp
  28.8 0.9 %collective-permute-done.5.part_p.rim_p = bf16[64,1024]{1,0:T(8,128)(2,1)S(1)} collective-permute-done((bf16[64,1024]{1,0:T(8,128)(2,1)S(1)}, bf16[64,1024]{1,0:T(8,128)(2,1)S(1)}, u32[]{:S(2)}, u32[]{:S(2)}) %collective-permute-start.5) | collective-permute-done | bytes 131104 | tf_op jit(solution)/shard_map/ppermute | solution.py:442
  29.7 0.1 collective-permute-start.8
  29.8 2.8 %collective-permute-start.9 = (bf16[48,1024]{1,0:T(8,128)(2,1)S(1)}, bf16[48,1024]{1,0:T(8,128)(2,1)S(1)}, u32[]{:S(2)}, u32[]{:S(2)}) collective-permute-start(bf16[48,1024]{1,0:T(8,128)(2,1)S(1)} %get-tuple-element.78), channel_id=1, source_target_pairs={{2,4},{6,8},{10,12},{14,16},{18,20},{22,24},{26,28},{30,32},{34,36... | collective-permute-start | bytes 294920 | tf_op jit(solution)/shard_map/ppermute | solution.py:449
  32.6 0.4 shard_map.99
  33.0 0.0 collective-permute-done.8.ea
  33.0 7.3 %collective-permute-done.9.eb = bf16[48,1024]{1,0:T(8,128)(2,1)S(1)} collective-permute-done((bf16[48,1024]{1,0:T(8,128)(2,1)S(1)}, bf16[48,1024]{1,0:T(8,128)(2,1)S(1)}, u32[]{:S(2)}, u32[]{:S(2)}) %collective-permute-start.9) | collective-permute-done | bytes 98336 | tf_op jit(solution)/shard_map/ppermute | solution.py:449
  40.4 0.0 collective-permute-done.6.mid_p
  40.4 4.0 %shard_map.100 = (bf16[256,512]{1,0:T(8,128)(2,1)}, f32[256,512]{1,0:T(8,128)S(1)}, bf16[256,512]{1,0:T(8,128)(2,1)S(1)}, f32[9,512]{1,0:T(8,128)S(1)}) custom-call(bf16[256,512]{1,0:T(8,128)(2,1)S(1)} %get-tuple-element.60.xo, bf16[256,512]{1,0:T(8,128)(2,1)S(1)} %collective-permute-done.xp, bf16[64,1024]{1,0:T(8,128)(2,1)S(1)} %get-tuple-element.71.part.rim, ...), custom_call_target="tpu_custom_call" | custom-call | flops 49999998976 | bytes 50000000 | tf_op jit(solution)/shard_map/pallas_call | solution.py:425
  44.4 0.0 collective-permute-start.10
  44.4 1.4 %shard_map.101 = (f32[256,512]{1,0:T(8,128)S(1)}, bf16[2,256,512]{2,1,0:T(8,128)(2,1)S(1)}) custom-call(bf16[256,512]{1,0:T(8,128)(2,1)S(1)} %get-tuple-element.68.q, bf16[256,512]{1,0:T(8,128)(2,1)S(1)} %get-tuple-element.72.kb.k, bf16[256,512]{1,0:T(8,128)(2,1)S(1)} %get-tuple-element.73.vb.v, bf16[256,512]{1,0:T(8,128)(2,1)S(1)} %get-tuple-element.85.datt, ...), custom_call_target="tpu_custom_call" | custom-call | flops 15000000512 | bytes 15000000 | tf_op jit(solution)/shard_map/pallas_call | solution.py:425
  45.7 2.6 %collective-permute-start.12 = (bf16[2,256,512]{2,1,0:T(8,128)(2,1)S(1)}, bf16[2,256,512]{2,1,0:T(8,128)(2,1)S(1)}, u32[]{:S(2)}, u32[]{:S(2)}) collective-permute-start(bf16[2,256,512]{2,1,0:T(8,128)(2,1)S(1)} %get-tuple-element.95), channel_id=1, source_target_pairs={{2,4},{6,8},{10,12},{14,16},{18,20},{22,24},{26,28},{30,32},{34,36... | collective-permute-start | bytes 1572872 | tf_op jit(solution)/shard_map/ppermute | solution.py:449
  48.4 0.0 collective-permute-done.10.refs_1_
  48.4 6.4 %collective-permute-start.15 = (f32[9,512]{1,0:T(8,128)S(1)}, f32[9,512]{1,0:T(8,128)S(1)}, u32[]{:S(2)}, u32[]{:S(2)}) collective-permute-start(f32[9,512]{1,0:T(8,128)S(1)} %shard_map.102.refs_1_.after.refs_0_), channel_id=1, source_target_pairs={{0,192},{2,194},{4,196},{6,198},{8,200},{10,202},{12,204},{14,206}... | collective-permute-start | bytes 55304 | tf_op jit(solution)/shard_map/ppermute | solution.py:520
  54.8 1.0 %collective-permute-start.14 = (f32[9,512]{1,0:T(8,128)S(1)}, f32[9,512]{1,0:T(8,128)S(1)}, u32[]{:S(2)}, u32[]{:S(2)}) collective-permute-start(f32[9,512]{1,0:T(8,128)S(1)} %shard_map.102.refs_1_.after.refs_0_), channel_id=1, source_target_pairs={{0,128},{2,130},{4,132},{6,134},{8,136},{10,138},{12,140},{14,142}... | collective-permute-start | bytes 55304 | tf_op jit(solution)/shard_map/ppermute | solution.py:520
  55.8 1.5 %collective-permute-start.13 = (f32[9,512]{1,0:T(8,128)S(1)}, f32[9,512]{1,0:T(8,128)S(1)}, u32[]{:S(2)}, u32[]{:S(2)}) collective-permute-start(f32[9,512]{1,0:T(8,128)S(1)} %shard_map.102.refs_1_.after.refs_0_), channel_id=1, source_target_pairs={{0,64},{2,66},{4,68},{6,70},{8,72},{10,74},{12,76},{14,78},{16,80}... | collective-permute-start | bytes 55304 | tf_op jit(solution)/shard_map/ppermute | solution.py:520
  57.3 1.2 %shard_map.103 = (f32[256,512]{1,0:T(8,128)S(1)}, bf16[2,256,512]{2,1,0:T(8,128)(2,1)S(1)}) custom-call(bf16[256,512]{1,0:T(8,128)(2,1)S(1)} %get-tuple-element.68.q, bf16[256,512]{1,0:T(8,128)(2,1)S(1)} %collective-permute-done.3.ka.k, bf16[256,512]{1,0:T(8,128)(2,1)S(1)} %collective-permute-done.4.va.v, bf16[256,512]{1,0:T(8,128)(2,1)S(1)} %get-tuple-element.85.datt, ...), custom_call_target="tpu_custom_call" | custom-call | flops 15000000512 | bytes 15000000 | tf_op jit(solution)/shard_map/pallas_call | solution.py:425
  58.5 0.0 copy-done.5
  58.5 0.0 copy-done.7
  58.5 0.1 copy-done.9
  58.6 1.5 %shard_map.104 = (f32[2,256,512]{2,1,0:T(8,128)S(1)}, f32[256,1024]{1,0:T(8,128)S(1)}) custom-call(bf16[256,512]{1,0:T(8,128)(2,1)S(1)} %get-tuple-element.68.q, bf16[256,512]{1,0:T(8,128)(2,1)S(1)} %copy-done.7, bf16[256,512]{1,0:T(8,128)(2,1)S(1)} %copy-done.9, bf16[256,512]{1,0:T(8,128)(2,1)S(1)} %get-tuple-element.85.datt, ...), custom_call_target="tpu_custom_call" | custom-call | flops 20000000000 | bytes 20000000 | tf_op jit(solution)/shard_map/pallas_call | solution.py:425
  60.1 0.1 collective-permute-start.11
  60.2 0.0 collective-permute-done.15.refs_3_
  60.2 2.9 %collective-permute-done.14.refs_2_ = f32[9,512]{1,0:T(8,128)S(1)} collective-permute-done((f32[9,512]{1,0:T(8,128)S(1)}, f32[9,512]{1,0:T(8,128)S(1)}, u32[]{:S(2)}, u32[]{:S(2)}) %collective-permute-start.14) | collective-permute-done | bytes 18464 | tf_op jit(solution)/shard_map/ppermute | solution.py:520
  63.1 0.0 collective-permute-done.13.refs_1_
  63.2 4.4 %collective-permute-start.19 = (f32[9,512]{1,0:T(8,128)S(1)}, f32[9,512]{1,0:T(8,128)S(1)}, u32[]{:S(2)}, u32[]{:S(2)}) collective-permute-start(f32[9,512]{1,0:T(8,128)S(1)} %shard_map.105.after.refs_0_), channel_id=1, source_target_pairs={{0,48},{2,50},{4,52},{6,54},{8,56},{10,58},{12,60},{14,62},{16,32}... | collective-permute-start | bytes 55304 | tf_op jit(solution)/shard_map/ppermute | solution.py:520
  67.5 0.0 collective-permute-start.18
  67.5 0.7 collective-permute-start.17
  68.2 0.0 collective-permute-done.12.got_b
  68.2 0.0 collective-permute-done.11.got_a
  68.2 0.9 %shard_map.106 = (bf16[256,640]{1,0:T(8,128)(2,1)S(1)}, f32[256,512]{1,0:T(8,128)S(1)}, f32[256,128]{1,0:T(8,128)S(1)}) custom-call(f32[256,512]{1,0:T(8,128)S(1)} %get-tuple-element.82.n1o, f32[256,512]{1,0:T(8,128)S(1)} %get-tuple-element.84.n1p, f32[2,256,512]{2,1,0:T(8,128)S(1)} %get-tuple-element.93.dkv, ...), custom_call_target="tpu_custom_call" | custom-call | flops 15000000512 | bytes 15000000 | tf_op jit(solution)/shard_map/pallas_call | solution.py:425
  69.1 0.9 %collective-permute-start.16 = (bf16[256,640]{1,0:T(8,128)(2,1)S(1)}, bf16[256,640]{1,0:T(8,128)(2,1)S(1)}, u32[]{:S(2)}, u32[]{:S(2)}) collective-permute-start(bf16[256,640]{1,0:T(8,128)(2,1)S(1)} %get-tuple-element.99), channel_id=1, source_target_pairs={{0,1},{1,0},{2,3},{3,2},{4,5},{5,4},{6,7},{7,6},{8,9},{9,8},{10,11... | collective-permute-start | bytes 983048 | tf_op jit(solution)/shard_map/ppermute | solution.py:442
  70.0 0.0 collective-permute-done.19.refs_3_
  70.0 1.5 %collective-permute-done.18.refs_2_ = f32[9,512]{1,0:T(8,128)S(1)} collective-permute-done((f32[9,512]{1,0:T(8,128)S(1)}, f32[9,512]{1,0:T(8,128)S(1)}, u32[]{:S(2)}, u32[]{:S(2)}) %collective-permute-start.18) | collective-permute-done | bytes 18464 | tf_op jit(solution)/shard_map/ppermute | solution.py:520
  71.4 0.4 collective-permute-done.17.refs_1_
  71.8 0.1 collective-permute-start.22
  71.9 0.1 collective-permute-start.21
  72.0 4.0 %collective-permute-start.20 = (f32[9,512]{1,0:T(8,128)S(1)}, f32[9,512]{1,0:T(8,128)S(1)}, u32[]{:S(2)}, u32[]{:S(2)}) collective-permute-start(f32[9,512]{1,0:T(8,128)S(1)} %shard_map.107.row), channel_id=1, source_target_pairs={{0,4},{2,6},{4,0},{6,2},{8,12},{10,14},{12,8},{14,10},{16,20},{18,... | collective-permute-start | bytes 55304 | tf_op jit(solution)/shard_map/ppermute | solution.py:520
  76.0 1.0 %collective-permute-done.22.three = f32[9,512]{1,0:T(8,128)S(1)} collective-permute-done((f32[9,512]{1,0:T(8,128)S(1)}, f32[9,512]{1,0:T(8,128)S(1)}, u32[]{:S(2)}, u32[]{:S(2)}) %collective-permute-start.22) | collective-permute-done | bytes 18464 | tf_op jit(solution)/shard_map/ppermute | solution.py:520
  77.1 0.4 collective-permute-done.21.two
  77.5 0.8 %collective-permute-done.20.one = f32[9,512]{1,0:T(8,128)S(1)} collective-permute-done((f32[9,512]{1,0:T(8,128)S(1)}, f32[9,512]{1,0:T(8,128)S(1)}, u32[]{:S(2)}, u32[]{:S(2)}) %collective-permute-start.20) | collective-permute-done | bytes 18464 | tf_op jit(solution)/shard_map/ppermute | solution.py:520
  78.3 0.0 collective-permute-done.16.got
  78.3 1.0 %shard_map.108 = (bf16[256,512]{1,0:T(8,128)(2,1)}, f32[9,512]{1,0:T(8,128)}) custom-call(f32[256,512]{1,0:T(8,128)S(1)} %get-tuple-element.82.n1o, f32[256,128]{1,0:T(8,128)S(1)} %get-tuple-element.83.rstd, f32[256,512]{1,0:T(8,128)S(1)} %get-tuple-element.97.keep, f32[256,128]{1,0:T(8,128)S(1)} %get-tuple-element.98.stat, ...), custom_call_target="tpu_custom_call" | custom-call | flops 10000000000 | bytes 10000000 | tf_op jit(solution)/shard_map/pallas_call | solution.py:425
  (17 shorter events, 0.1 us)
Async XLA Ops:
  0.6 12.9 %collective-permute-start = (bf16[256,512]{1,0:T(8,128)(2,1)}, bf16[256,512]{1,0:T(8,128)(2,1)S(1)}, u32[]{:S(2)}, u32[]{:S(2)}) collective-permute-start(bf16[256,512]{1,0:T(8,128)(2,1)} %refs_4_.1), channel_id=1, source_target_pairs={{0,1},{1,0},{2,3},{3,2},{4,5},{5,4},{6,7},{7,6},{8,9},{9,8},{10,11... | collective-permute-start | bytes 786440 | tf_op jit(solution)/shard_map/ppermute | solution.py:442
  2.8 17.3 %collective-permute-start.2 = (bf16[256,512]{1,0:T(8,128)(2,1)}, bf16[256,512]{1,0:T(8,128)(2,1)S(1)}, u32[]{:S(2)}, u32[]{:S(2)}) collective-permute-start(bf16[256,512]{1,0:T(8,128)(2,1)} %refs_4_.1), channel_id=1, source_target_pairs={{2,5},{3,4},{6,9},{7,8},{10,13},{11,12},{14,17},{15,16},{18,21},{1... | collective-permute-start | bytes 786440 | tf_op jit(solution)/shard_map/ppermute | solution.py:456
  6.2 13.9 %collective-permute-start.1 = (bf16[256,512]{1,0:T(8,128)(2,1)}, bf16[256,512]{1,0:T(8,128)(2,1)S(1)}, u32[]{:S(2)}, u32[]{:S(2)}) collective-permute-start(bf16[256,512]{1,0:T(8,128)(2,1)} %refs_4_.1), channel_id=1, source_target_pairs={{2,4},{6,8},{10,12},{14,16},{18,20},{22,24},{26,28},{30,32},{34,36... | collective-permute-start | bytes 786440 | tf_op jit(solution)/shard_map/ppermute | solution.py:449
  13.5 1.2 %copy-start.4 = (bf16[1024,512]{1,0:T(8,128)(2,1)}, bf16[1024,512]{1,0:T(8,128)(2,1)S(1)}, u32[]{:S(2)}) copy-start(bf16[1024,512]{1,0:T(8,128)(2,1)S(1)} %get-tuple-element.65.wq) | copy-start | bytes 3145732
  13.5 6.7 %copy-start = (bf16[1024,512]{1,0:T(8,128)(2,1)}, bf16[1024,512]{1,0:T(8,128)(2,1)S(1)}, u32[]{:S(2)}) copy-start(bf16[1024,512]{1,0:T(8,128)(2,1)S(1)} %get-tuple-element.62.wk) | copy-start | bytes 3145732
  13.5 6.7 %copy-start.2 = (bf16[1024,512]{1,0:T(8,128)(2,1)}, bf16[1024,512]{1,0:T(8,128)(2,1)S(1)}, u32[]{:S(2)}) copy-start(bf16[1024,512]{1,0:T(8,128)(2,1)S(1)} %get-tuple-element.63.wv) | copy-start | bytes 3145732
  14.7 10.7 %copy-start.6 = (bf16[256,512]{1,0:T(8,128)(2,1)}, bf16[256,512]{1,0:T(8,128)(2,1)S(1)}, u32[]{:S(2)}) copy-start(bf16[256,512]{1,0:T(8,128)(2,1)S(1)} %get-tuple-element.69.k) | copy-start | bytes 786436
  14.7 10.7 %copy-start.8 = (bf16[256,512]{1,0:T(8,128)(2,1)}, bf16[256,512]{1,0:T(8,128)(2,1)S(1)}, u32[]{:S(2)}) copy-start(bf16[256,512]{1,0:T(8,128)(2,1)S(1)} %get-tuple-element.70.v) | copy-start | bytes 786436
  14.7 5.5 %collective-permute-start.3 = (bf16[256,512]{1,0:T(8,128)(2,1)S(1)}, bf16[256,512]{1,0:T(8,128)(2,1)S(1)}, u32[]{:S(2)}, u32[]{:S(2)}) collective-permute-start(bf16[256,512]{1,0:T(8,128)(2,1)S(1)} %get-tuple-element.69.k), channel_id=1, source_target_pairs={{0,2},{2,0},{4,6},{6,4},{8,10},{10,8},{12,14},{14,12},{16,18},{18,... | collective-permute-start | bytes 786440 | tf_op jit(solution)/shard_map/ppermute | solution.py:445
  14.8 5.4 %collective-permute-start.4 = (bf16[256,512]{1,0:T(8,128)(2,1)S(1)}, bf16[256,512]{1,0:T(8,128)(2,1)S(1)}, u32[]{:S(2)}, u32[]{:S(2)}) collective-permute-start(bf16[256,512]{1,0:T(8,128)(2,1)S(1)} %get-tuple-element.70.v), channel_id=1, source_target_pairs={{0,2},{2,0},{4,6},{6,4},{8,10},{10,8},{12,14},{14,12},{16,18},{18,... | collective-permute-start | bytes 786440 | tf_op jit(solution)/shard_map/ppermute | solution.py:445
  15.3 13.5 %collective-permute-start.7 = (bf16[304,512]{1,0:T(8,128)(2,1)S(1)}, bf16[304,512]{1,0:T(8,128)(2,1)S(1)}, u32[]{:S(2)}, u32[]{:S(2)}) collective-permute-start(bf16[304,512]{1,0:T(8,128)(2,1)S(1)} %get-tuple-element.76), channel_id=1, source_target_pairs={{0,1},{1,0},{2,3},{3,2},{4,5},{5,4},{6,7},{7,6},{8,9},{9,8},{10,11... | collective-permute-start | bytes 933896 | tf_op jit(solution)/shard_map/ppermute | solution.py:442
  22.9 6.8 %collective-permute-start.5 = (bf16[64,1024]{1,0:T(8,128)(2,1)S(1)}, bf16[64,1024]{1,0:T(8,128)(2,1)S(1)}, u32[]{:S(2)}, u32[]{:S(2)}) collective-permute-start(bf16[64,1024]{1,0:T(8,128)(2,1)S(1)} %get-tuple-element.71.part.rim), channel_id=1, source_target_pairs={{0,1},{1,0},{2,3},{3,2},{4,5},{5,4},{6,7},{7,6},{8,9},{9,8},{10,11... | collective-permute-start | bytes 393224 | tf_op jit(solution)/shard_map/ppermute | solution.py:442
  27.6 12.8 %collective-permute-start.6 = (bf16[192,1024]{1,0:T(8,128)(2,1)S(1)}, bf16[192,1024]{1,0:T(8,128)(2,1)S(1)}, u32[]{:S(2)}, u32[]{:S(2)}) collective-permute-start(bf16[192,1024]{1,0:T(8,128)(2,1)S(1)} %get-tuple-element.74.mid), channel_id=1, source_target_pairs={{0,1},{1,0},{2,3},{3,2},{4,5},{5,4},{6,7},{7,6},{8,9},{9,8},{10,11... | collective-permute-start | bytes 1179656 | tf_op jit(solution)/shard_map/ppermute | solution.py:442
  29.7 3.3 %collective-permute-start.8 = (bf16[48,1024]{1,0:T(8,128)(2,1)S(1)}, bf16[48,1024]{1,0:T(8,128)(2,1)S(1)}, u32[]{:S(2)}, u32[]{:S(2)}) collective-permute-start(bf16[48,1024]{1,0:T(8,128)(2,1)S(1)} %get-tuple-element.77), channel_id=1, source_target_pairs={{0,2},{2,0},{4,6},{6,4},{8,10},{10,8},{12,14},{14,12},{16,18},{18,... | collective-permute-start | bytes 294920 | tf_op jit(solution)/shard_map/ppermute | solution.py:445
  29.8 10.6 %collective-permute-start.9 = (bf16[48,1024]{1,0:T(8,128)(2,1)S(1)}, bf16[48,1024]{1,0:T(8,128)(2,1)S(1)}, u32[]{:S(2)}, u32[]{:S(2)}) collective-permute-start(bf16[48,1024]{1,0:T(8,128)(2,1)S(1)} %get-tuple-element.78), channel_id=1, source_target_pairs={{2,4},{6,8},{10,12},{14,16},{18,20},{22,24},{26,28},{30,32},{34,36... | collective-permute-start | bytes 294920 | tf_op jit(solution)/shard_map/ppermute | solution.py:449
  44.4 4.0 %collective-permute-start.10 = (f32[9,512]{1,0:T(8,128)S(1)}, f32[9,512]{1,0:T(8,128)S(1)}, u32[]{:S(2)}, u32[]{:S(2)}) collective-permute-start(f32[9,512]{1,0:T(8,128)S(1)} %get-tuple-element.91.refs_0_), channel_id=1, source_target_pairs={{0,2},{2,0},{4,6},{6,4},{8,10},{10,8},{12,14},{14,12},{16,18},{18,... | collective-permute-start | bytes 55304 | tf_op jit(solution)/shard_map/ppermute | solution.py:520
  45.7 22.4 %collective-permute-start.12 = (bf16[2,256,512]{2,1,0:T(8,128)(2,1)S(1)}, bf16[2,256,512]{2,1,0:T(8,128)(2,1)S(1)}, u32[]{:S(2)}, u32[]{:S(2)}) collective-permute-start(bf16[2,256,512]{2,1,0:T(8,128)(2,1)S(1)} %get-tuple-element.95), channel_id=1, source_target_pairs={{2,4},{6,8},{10,12},{14,16},{18,20},{22,24},{26,28},{30,32},{34,36... | collective-permute-start | bytes 1572872 | tf_op jit(solution)/shard_map/ppermute | solution.py:449
  48.4 11.8 %collective-permute-start.15 = (f32[9,512]{1,0:T(8,128)S(1)}, f32[9,512]{1,0:T(8,128)S(1)}, u32[]{:S(2)}, u32[]{:S(2)}) collective-permute-start(f32[9,512]{1,0:T(8,128)S(1)} %shard_map.102.refs_1_.after.refs_0_), channel_id=1, source_target_pairs={{0,192},{2,194},{4,196},{6,198},{8,200},{10,202},{12,204},{14,206}... | collective-permute-start | bytes 55304 | tf_op jit(solution)/shard_map/ppermute | solution.py:520
  54.8 8.3 %collective-permute-start.14 = (f32[9,512]{1,0:T(8,128)S(1)}, f32[9,512]{1,0:T(8,128)S(1)}, u32[]{:S(2)}, u32[]{:S(2)}) collective-permute-start(f32[9,512]{1,0:T(8,128)S(1)} %shard_map.102.refs_1_.after.refs_0_), channel_id=1, source_target_pairs={{0,128},{2,130},{4,132},{6,134},{8,136},{10,138},{12,140},{14,142}... | collective-permute-start | bytes 55304 | tf_op jit(solution)/shard_map/ppermute | solution.py:520
  55.8 7.4 %collective-permute-start.13 = (f32[9,512]{1,0:T(8,128)S(1)}, f32[9,512]{1,0:T(8,128)S(1)}, u32[]{:S(2)}, u32[]{:S(2)}) collective-permute-start(f32[9,512]{1,0:T(8,128)S(1)} %shard_map.102.refs_1_.after.refs_0_), channel_id=1, source_target_pairs={{0,64},{2,66},{4,68},{6,70},{8,72},{10,74},{12,76},{14,78},{16,80}... | collective-permute-start | bytes 55304 | tf_op jit(solution)/shard_map/ppermute | solution.py:520
  57.2 1.2 %copy-start.5 = (bf16[1024,512]{1,0:T(8,128)(2,1)S(1)}, bf16[1024,512]{1,0:T(8,128)(2,1)}, u32[]{:S(2)}) copy-start(bf16[1024,512]{1,0:T(8,128)(2,1)} %copy-done.4) | copy-start | bytes 3145732
  57.2 1.3 %copy-start.7 = (bf16[256,512]{1,0:T(8,128)(2,1)S(1)}, bf16[256,512]{1,0:T(8,128)(2,1)}, u32[]{:S(2)}) copy-start(bf16[256,512]{1,0:T(8,128)(2,1)} %copy-done.6) | copy-start | bytes 786436
  57.3 1.3 %copy-start.9 = (bf16[256,512]{1,0:T(8,128)(2,1)S(1)}, bf16[256,512]{1,0:T(8,128)(2,1)}, u32[]{:S(2)}) copy-start(bf16[256,512]{1,0:T(8,128)(2,1)} %copy-done.8) | copy-start | bytes 786436
  60.1 8.1 %copy-start.1 = (bf16[1024,512]{1,0:T(8,128)(2,1)S(1)}, bf16[1024,512]{1,0:T(8,128)(2,1)}, u32[]{:S(2)}) copy-start(bf16[1024,512]{1,0:T(8,128)(2,1)} %copy-done) | copy-start | bytes 3145732
  60.1 8.1 %copy-start.3 = (bf16[1024,512]{1,0:T(8,128)(2,1)S(1)}, bf16[1024,512]{1,0:T(8,128)(2,1)}, u32[]{:S(2)}) copy-start(bf16[1024,512]{1,0:T(8,128)(2,1)} %copy-done.2) | copy-start | bytes 3145732
  60.1 8.1 %collective-permute-start.11 = (bf16[2,256,512]{2,1,0:T(8,128)(2,1)S(1)}, bf16[2,256,512]{2,1,0:T(8,128)(2,1)S(1)}, u32[]{:S(2)}, u32[]{:S(2)}) collective-permute-start(bf16[2,256,512]{2,1,0:T(8,128)(2,1)S(1)} %get-tuple-element.94), channel_id=1, source_target_pairs={{0,2},{2,0},{4,6},{6,4},{8,10},{10,8},{12,14},{14,12},{16,18},{18,... | collective-permute-start | bytes 1572872 | tf_op jit(solution)/shard_map/ppermute | solution.py:445
  63.2 6.8 %collective-permute-start.19 = (f32[9,512]{1,0:T(8,128)S(1)}, f32[9,512]{1,0:T(8,128)S(1)}, u32[]{:S(2)}, u32[]{:S(2)}) collective-permute-start(f32[9,512]{1,0:T(8,128)S(1)} %shard_map.105.after.refs_0_), channel_id=1, source_target_pairs={{0,48},{2,50},{4,52},{6,54},{8,56},{10,58},{12,60},{14,62},{16,32}... | collective-permute-start | bytes 55304 | tf_op jit(solution)/shard_map/ppermute | solution.py:520
  67.5 3.9 %collective-permute-start.18 = (f32[9,512]{1,0:T(8,128)S(1)}, f32[9,512]{1,0:T(8,128)S(1)}, u32[]{:S(2)}, u32[]{:S(2)}) collective-permute-start(f32[9,512]{1,0:T(8,128)S(1)} %shard_map.105.after.refs_0_), channel_id=1, source_target_pairs={{0,32},{2,34},{4,36},{6,38},{8,40},{10,42},{12,44},{14,46},{16,48}... | collective-permute-start | bytes 55304 | tf_op jit(solution)/shard_map/ppermute | solution.py:520
  67.5 4.3 %collective-permute-start.17 = (f32[9,512]{1,0:T(8,128)S(1)}, f32[9,512]{1,0:T(8,128)S(1)}, u32[]{:S(2)}, u32[]{:S(2)}) collective-permute-start(f32[9,512]{1,0:T(8,128)S(1)} %shard_map.105.after.refs_0_), channel_id=1, source_target_pairs={{0,16},{2,18},{4,20},{6,22},{8,24},{10,26},{12,28},{14,30},{16,0},... | collective-permute-start | bytes 55304 | tf_op jit(solution)/shard_map/ppermute | solution.py:520
  69.1 9.2 %collective-permute-start.16 = (bf16[256,640]{1,0:T(8,128)(2,1)S(1)}, bf16[256,640]{1,0:T(8,128)(2,1)S(1)}, u32[]{:S(2)}, u32[]{:S(2)}) collective-permute-start(bf16[256,640]{1,0:T(8,128)(2,1)S(1)} %get-tuple-element.99), channel_id=1, source_target_pairs={{0,1},{1,0},{2,3},{3,2},{4,5},{5,4},{6,7},{7,6},{8,9},{9,8},{10,11... | collective-permute-start | bytes 983048 | tf_op jit(solution)/shard_map/ppermute | solution.py:442
  71.8 5.2 %collective-permute-start.22 = (f32[9,512]{1,0:T(8,128)S(1)}, f32[9,512]{1,0:T(8,128)S(1)}, u32[]{:S(2)}, u32[]{:S(2)}) collective-permute-start(f32[9,512]{1,0:T(8,128)S(1)} %shard_map.107.row), channel_id=1, source_target_pairs={{0,12},{2,14},{4,8},{6,10},{8,4},{10,6},{12,0},{14,2},{16,28},{18,... | collective-permute-start | bytes 55304 | tf_op jit(solution)/shard_map/ppermute | solution.py:520
  71.9 5.5 %collective-permute-start.21 = (f32[9,512]{1,0:T(8,128)S(1)}, f32[9,512]{1,0:T(8,128)S(1)}, u32[]{:S(2)}, u32[]{:S(2)}) collective-permute-start(f32[9,512]{1,0:T(8,128)S(1)} %shard_map.107.row), channel_id=1, source_target_pairs={{0,8},{2,10},{4,12},{6,14},{8,0},{10,2},{12,4},{14,6},{16,24},{18,... | collective-permute-start | bytes 55304 | tf_op jit(solution)/shard_map/ppermute | solution.py:520
  72.0 6.2 %collective-permute-start.20 = (f32[9,512]{1,0:T(8,128)S(1)}, f32[9,512]{1,0:T(8,128)S(1)}, u32[]{:S(2)}, u32[]{:S(2)}) collective-permute-start(f32[9,512]{1,0:T(8,128)S(1)} %shard_map.107.row), channel_id=1, source_target_pairs={{0,4},{2,6},{4,0},{6,2},{8,12},{10,14},{12,8},{14,10},{16,20},{18,... | collective-permute-start | bytes 55304 | tf_op jit(solution)/shard_map/ppermute | solution.py:520

commit v6 on v5

--- a/solution.py
+++ b/solution.py
@@ -316,12 +316,19 @@
 
 
 def back_halo_kernel(q, k, v, datt, att, att_mid, p, p_mid, *refs, which):
-    dq, dkv = refs[-2:]
+    if which == 1:
+        dq, dkv = refs[-2:]
+    else:
+        dq, dkv, deltas = refs
     at = slice(which * ROWS, (which + 1) * ROWS)
     for head in range(HEADS):
         f = lanes_of(head)
         gh = datt[:, f]
-        delta = row_sum(gh.astype(F32) * in_order(att[:, f], att_mid[:, f]).astype(F32))
+        if which == 1:
+            delta = refs[1][head][:, :1]
+        else:
+            delta = row_sum(gh.astype(F32) * in_order(att[:, f], att_mid[:, f]).astype(F32))
+            deltas[head] = jnp.broadcast_to(delta, (ROWS, LANES))
         probs = in_order(p[head, :, at], p_mid[head, :, at])
         d_q, d_k, d_v = pair_grad(q[:, f], k[:, f], v[:, f], gh, probs, delta)
         dq[:, f] = d_q + refs[0][:, f] if which == 1 else d_q
@@ -329,12 +336,12 @@
         dkv[1, :, f] = d_v.astype(BF16)
 
 
-def back_own_kernel(q, k, v, datt, att, att_mid, p, p_mid, dq_ab, wq, after, dkv, pin):
+def back_own_kernel(q, k, v, datt, att, att_mid, p, p_mid, dq_ab, deltas, wq, after, dkv, pin):
     dq = []
     for head in range(HEADS):
         f = lanes_of(head)
         gh = datt[:, f]
-        delta = row_sum(gh.astype(F32) * in_order(att[:, f], att_mid[:, f]).astype(F32))
+        delta = deltas[head][:, :1]
         probs = in_order(p[head, :, :ROWS], p_mid[head, :, :ROWS])
         d_q, d_k, d_v = pair_grad(q[:, f], k[:, f], v[:, f], gh, probs, delta)
         dkv[0, :, f] = d_k
@@ -521,27 +528,27 @@
         ]
 
     chain = [gk]
-    for steps in ((1,), (32, 64, 96), (8, 16, 24)):
+    for steps in ((1,), (32, 96, 64), (8, 16, 24)):
         parts = (chain[-1], *swaps(chain[-1], steps))
         chain.extend(call(sum_kernel, parts, (tap_sums,), us=0.6, mib=1))
     pair = ((2, ROWS, SHARE), BF16)
-    dq_b, dkv_b = call(
+    dq_b, dkv_b, deltas = call(
         functools.partial(back_halo_kernel, which=2),
         (q, kb, vb, datt, *attended),
-        (((ROWS, SHARE), F32), pair),
+        (((ROWS, SHARE), F32), pair, ((HEADS, ROWS, LANES), F32)),
         us=1.5,
     )
     got_b = over_b(dkv_b)
     dq_ab, dkv_a = call(
         functools.partial(back_halo_kernel, which=1),
-        (q, ka, va, datt, *attended, dq_b, chain[1]),
+        (q, ka, va, datt, *attended, dq_b, deltas, chain[1]),
         (((ROWS, SHARE), F32), pair),
         us=1.5,
     )
     got_a = over_a(dkv_a)
     dkv, pin = call(
         back_own_kernel,
-        (q, k, v, datt, *attended, dq_ab, w_query, chain[1]),
+        (q, k, v, datt, *attended, dq_ab, deltas, w_query, chain[1]),
         (((2, ROWS, SHARE), F32), ((ROWS, D), F32)),
         us=2.0,
     )
@@ -554,7 +561,7 @@
     got = over_head(send)
     grad, grad_taps = call(
         final_kernel,
-        (n1o, rstd, keep, stat, got, dh, chain[3], *swaps(chain[3], (2, 4, 6))),
+        (n1o, rstd, keep, stat, got, dh, chain[3], *swaps(chain[3], (2, 6, 4))),
         (big, tap_sums),
         us=1.0,
     )

time: 79.8 us -> 79.5 us (level)
  waiting for transfers between devices: 19.2 us -> 18 us
    ppermute x10, waiting for transfers between devices: 7.05 us -> 5.53 us  [swaps(): lax.ppermute(value, 'tm', [(i, i ^ step) for i in range(count)])]
  transfers between devices with their start and end apart: 23 -> 23, of which waited for: 9 -> 8; matrix products, arithmetic and copies ran while one was open for 0% -> 0% of each run, Pallas kernels for 17% -> 18%
where the time goes in v6:
time: 79.5 us; the launch traced here: 78.3 us
  starting transfers between devices  40.6 us (51%)
  Pallas kernels  18.7 us (24%)
  waiting for transfers between devices  18 us (23%)
  between operations  0.92 us (1%)
    ppermute x10, starting transfers between devices, swaps(): lax.ppermute(value, 'tm', [(i, i ^ step) for i in range(count)])  18.4 us
    pallas_call x14, Pallas kernels, call(): pl.pallas_call(kernel, out_shape=[jax.ShapeDtypeStruct(shape, dtype) for...  16.3 us
    ppermute x3, starting transfers between devices, over_b(): return lax.ppermute(value, 'tm', pairs + [(j, i) for i, j in pairs])  10.3 us
    ppermute x5, starting transfers between devices, over_head(): return lax.ppermute(value, 'head', [(0, 1), (1, 0)])  7.72 us
    ppermute x3, waiting for transfers between devices, over_b(): return lax.ppermute(value, 'tm', pairs + [(j, i) for i, j in pairs])  7.35 us
    ppermute x10, waiting for transfers between devices, swaps(): lax.ppermute(value, 'tm', [(i, i ^ step) for i in range(count)])  5.53 us
    ppermute x1, waiting for transfers between devices, over_b_and_head(): return lax.ppermute(value, ('tm', 'head'), crossed)  3.97 us
    ppermute x1, starting transfers between devices, over_b_and_head(): return lax.ppermute(value, ('tm', 'head'), crossed)  3.38 us
  transfers between devices with their start and end apart: 23, of which 8 were waited for; matrix products, arithmetic and copies ran while one was open for 0% of the time, Pallas kernels for 18%

profile of v6, /device:TPU:2, one launch (start us, length us, event | category | flops | bytes accessed | tf_op | source)
XLA Modules:
  0.0 78.3 jit_solution(3112606215100200181)
XLA Ops:
  0.6 2.2 %collective-permute-start = (bf16[256,512]{1,0:T(8,128)(2,1)}, bf16[256,512]{1,0:T(8,128)(2,1)S(1)}, u32[]{:S(2)}, u32[]{:S(2)}) collective-permute-start(bf16[256,512]{1,0:T(8,128)(2,1)} %refs_4_.1), channel_id=1, source_target_pairs={{0,1},{1,0},{2,3},{3,2},{4,5},{5,4},{6,7},{7,6},{8,9},{9,8},{10,11... | collective-permute-start | bytes 786440 | tf_op jit(solution)/shard_map/ppermute | solution.py:449
  2.8 3.4 %collective-permute-start.2 = (bf16[256,512]{1,0:T(8,128)(2,1)}, bf16[256,512]{1,0:T(8,128)(2,1)S(1)}, u32[]{:S(2)}, u32[]{:S(2)}) collective-permute-start(bf16[256,512]{1,0:T(8,128)(2,1)} %refs_4_.1), channel_id=1, source_target_pairs={{2,5},{3,4},{6,9},{7,8},{10,13},{11,12},{14,17},{15,16},{18,21},{1... | collective-permute-start | bytes 786440 | tf_op jit(solution)/shard_map/ppermute | solution.py:463
  6.2 4.8 %collective-permute-start.1 = (bf16[256,512]{1,0:T(8,128)(2,1)}, bf16[256,512]{1,0:T(8,128)(2,1)S(1)}, u32[]{:S(2)}, u32[]{:S(2)}) collective-permute-start(bf16[256,512]{1,0:T(8,128)(2,1)} %refs_4_.1), channel_id=1, source_target_pairs={{2,4},{6,8},{10,12},{14,16},{18,20},{22,24},{26,28},{30,32},{34,36... | collective-permute-start | bytes 786440 | tf_op jit(solution)/shard_map/ppermute | solution.py:456
  11.1 2.4 %shard_map.94 = (bf16[1024,512]{1,0:T(8,128)(2,1)S(1)}, bf16[1024,512]{1,0:T(8,128)(2,1)S(1)}, bf16[1024,512]{1,0:T(8,128)(2,1)S(1)}, bf16[512,1024]{1,0:T(8,128...) custom-call(bf16[1024,512]{1,0:T(8,128)(2,1)} %refs_0_.1, ...), custom_call_target="tpu_custom_call" | custom-call | bytes 67108864 | tf_op jit(solution)/shard_map/pallas_call | solution.py:419
  13.5 0.0 copy-start.4
  13.5 0.0 copy-start
  13.5 0.0 copy-start.2
  13.5 0.0 collective-permute-done.xp
  13.5 1.1 %shard_map.95 = (bf16[256,512]{1,0:T(8,128)(2,1)S(1)}, bf16[256,512]{1,0:T(8,128)(2,1)S(1)}, bf16[256,512]{1,0:T(8,128)(2,1)S(1)}) custom-call(bf16[256,512]{1,0:T(8,128)(2,1)S(1)} %get-tuple-element.61.xo, bf16[256,512]{1,0:T(8,128)(2,1)S(1)} %collective-permute-done.xp, bf16[1024,512]{1,0:T(8,128)(2,1)S(1)} %get-tuple-element.66.wq, ...), custom_call_target="tpu_custom_call" | custom-call | tf_op jit(solution)/shard_map/pallas_call | solution.py:432
  14.7 0.0 copy-start.6
  14.7 0.1 collective-permute-start.3
  14.8 0.5 collective-permute-start.4
  15.3 0.9 %collective-permute-start.7 = (bf16[304,512]{1,0:T(8,128)(2,1)S(1)}, bf16[304,512]{1,0:T(8,128)(2,1)S(1)}, u32[]{:S(2)}, u32[]{:S(2)}) collective-permute-start(bf16[304,512]{1,0:T(8,128)(2,1)S(1)} %get-tuple-element.77), channel_id=1, source_target_pairs={{0,1},{1,0},{2,3},{3,2},{4,5},{5,4},{6,7},{7,6},{8,9},{9,8},{10,11... | collective-permute-start | bytes 933896 | tf_op jit(solution)/shard_map/ppermute | solution.py:449
  16.2 4.0 %collective-permute-done.2.b1 = bf16[256,512]{1,0:T(8,128)(2,1)S(1)} collective-permute-done((bf16[256,512]{1,0:T(8,128)(2,1)}, bf16[256,512]{1,0:T(8,128)(2,1)S(1)}, u32[]{:S(2)}, u32[]{:S(2)}) %collective-permute-start.2) | collective-permute-done | bytes 262176 | tf_op jit(solution)/shard_map/ppermute | solution.py:463
  20.2 0.0 collective-permute-done.1.b0
  20.2 0.0 collective-permute-done.3.ka.k
  20.2 0.0 collective-permute-done.4.va.v
  20.2 2.7 %shard_map.96 = (bf16[256,512]{1,0:T(8,128)(2,1)S(1)}, bf16[256,512]{1,0:T(8,128)(2,1)S(1)}, bf16[4,64,768]{2,1,0:T(8,128)(2,1)S(1)}, bf16[64,512]{1,0:T(8,128)(2,1)S(1)}, bf16[64,1024]{1,0:T(8,128)(2,1)S(1)}) custom-call(bf16[256,512]{1,0:T(8,128)(2,1)S(1)} %collective-permute-done.1.b0, bf16[256,512]{1,0:T(8,128)(2,1)S(1)} %collective-permute-done.2.b1, ...), custom_call_target="tpu_custom_call" | custom-call | flops 20000000000 | bytes 20000000 | tf_op jit(solution)/shard_map/pallas_call | solution.py:432
  22.9 2.5 %collective-permute-start.5 = (bf16[64,1024]{1,0:T(8,128)(2,1)S(1)}, bf16[64,1024]{1,0:T(8,128)(2,1)S(1)}, u32[]{:S(2)}, u32[]{:S(2)}) collective-permute-start(bf16[64,1024]{1,0:T(8,128)(2,1)S(1)} %get-tuple-element.72.part.rim), channel_id=1, source_target_pairs={{0,1},{1,0},{2,3},{3,2},{4,5},{5,4},{6,7},{7,6},{8,9},{9,8},{10,11... | collective-permute-start | bytes 393224 | tf_op jit(solution)/shard_map/ppermute | solution.py:449
  25.4 2.2 %shard_map.97 = (bf16[4,192,768]{2,1,0:T(8,128)(2,1)S(1)}, bf16[192,512]{1,0:T(8,128)(2,1)S(1)}, bf16[192,1024]{1,0:T(8,128)(2,1)S(1)}) custom-call(bf16[512,1024]{1,0:T(8,128)(2,1)S(1)} %get-tuple-element.65.wo, bf16[256,512]{1,0:T(8,128)(2,1)S(1)} %get-tuple-element.69.q, bf16[256,512]{1,0:T(8,128)(2,1)S(1)} %get-tuple-element.70.k, ...), custom_call_target="tpu_custom_call" | custom-call | flops 20000000000 | bytes 20000000 | tf_op jit(solution)/shard_map/pallas_call | solution.py:432
  27.6 1.2 %collective-permute-start.6 = (bf16[192,1024]{1,0:T(8,128)(2,1)S(1)}, bf16[192,1024]{1,0:T(8,128)(2,1)S(1)}, u32[]{:S(2)}, u32[]{:S(2)}) collective-permute-start(bf16[192,1024]{1,0:T(8,128)(2,1)S(1)} %get-tuple-element.75.mid), channel_id=1, source_target_pairs={{0,1},{1,0},{2,3},{3,2},{4,5},{5,4},{6,7},{7,6},{8,9},{9,8},{10,11... | collective-permute-start | bytes 1179656 | tf_op jit(solution)/shard_map/ppermute | solution.py:449
  28.8 0.0 collective-permute-done.7.cp
  28.8 0.9 %collective-permute-done.5.part_p.rim_p = bf16[64,1024]{1,0:T(8,128)(2,1)S(1)} collective-permute-done((bf16[64,1024]{1,0:T(8,128)(2,1)S(1)}, bf16[64,1024]{1,0:T(8,128)(2,1)S(1)}, u32[]{:S(2)}, u32[]{:S(2)}) %collective-permute-start.5) | collective-permute-done | bytes 131104 | tf_op jit(solution)/shard_map/ppermute | solution.py:449
  29.7 0.1 collective-permute-start.8
  29.8 2.8 %collective-permute-start.9 = (bf16[48,1024]{1,0:T(8,128)(2,1)S(1)}, bf16[48,1024]{1,0:T(8,128)(2,1)S(1)}, u32[]{:S(2)}, u32[]{:S(2)}) collective-permute-start(bf16[48,1024]{1,0:T(8,128)(2,1)S(1)} %get-tuple-element.79), channel_id=1, source_target_pairs={{2,4},{6,8},{10,12},{14,16},{18,20},{22,24},{26,28},{30,32},{34,36... | collective-permute-start | bytes 294920 | tf_op jit(solution)/shard_map/ppermute | solution.py:456
  32.6 0.4 shard_map.99
  33.0 0.0 collective-permute-done.8.ea
  33.0 7.3 %collective-permute-done.9.eb = bf16[48,1024]{1,0:T(8,128)(2,1)S(1)} collective-permute-done((bf16[48,1024]{1,0:T(8,128)(2,1)S(1)}, bf16[48,1024]{1,0:T(8,128)(2,1)S(1)}, u32[]{:S(2)}, u32[]{:S(2)}) %collective-permute-start.9) | collective-permute-done | bytes 98336 | tf_op jit(solution)/shard_map/ppermute | solution.py:456
  40.4 0.0 collective-permute-done.6.mid_p
  40.4 4.0 %shard_map.100 = (bf16[256,512]{1,0:T(8,128)(2,1)}, f32[256,512]{1,0:T(8,128)S(1)}, bf16[256,512]{1,0:T(8,128)(2,1)S(1)}, f32[9,512]{1,0:T(8,128)S(1)}) custom-call(bf16[256,512]{1,0:T(8,128)(2,1)S(1)} %get-tuple-element.61.xo, bf16[256,512]{1,0:T(8,128)(2,1)S(1)} %collective-permute-done.xp, bf16[64,1024]{1,0:T(8,128)(2,1)S(1)} %get-tuple-element.72.part.rim, ...), custom_call_target="tpu_custom_call" | custom-call | flops 49999998976 | bytes 50000000 | tf_op jit(solution)/shard_map/pallas_call | solution.py:432
  44.4 0.0 collective-permute-start.10
  44.4 1.4 %shard_map.101 = (f32[256,512]{1,0:T(8,128)S(1)}, bf16[2,256,512]{2,1,0:T(8,128)(2,1)S(1)}, f32[4,256,128]{2,1,0:T(8,128)S(1)}) custom-call(bf16[256,512]{1,0:T(8,128)(2,1)S(1)} %get-tuple-element.69.q, bf16[256,512]{1,0:T(8,128)(2,1)S(1)} %get-tuple-element.73.kb.k, bf16[256,512]{1,0:T(8,128)(2,1)S(1)} %get-tuple-element.74.vb.v, ...), custom_call_target="tpu_custom_call" | custom-call | flops 15000000512 | bytes 15000000 | tf_op jit(solution)/shard_map/pallas_call | solution.py:432
  45.7 2.6 %collective-permute-start.12 = (bf16[2,256,512]{2,1,0:T(8,128)(2,1)S(1)}, bf16[2,256,512]{2,1,0:T(8,128)(2,1)S(1)}, u32[]{:S(2)}, u32[]{:S(2)}) collective-permute-start(bf16[2,256,512]{2,1,0:T(8,128)(2,1)S(1)} %get-tuple-element.97), channel_id=1, source_target_pairs={{2,4},{6,8},{10,12},{14,16},{18,20},{22,24},{26,28},{30,32},{34,36... | collective-permute-start | bytes 1572872 | tf_op jit(solution)/shard_map/ppermute | solution.py:456
  48.4 0.0 collective-permute-done.10.refs_1_
  48.4 7.3 %collective-permute-start.15 = (f32[9,512]{1,0:T(8,128)S(1)}, f32[9,512]{1,0:T(8,128)S(1)}, u32[]{:S(2)}, u32[]{:S(2)}) collective-permute-start(f32[9,512]{1,0:T(8,128)S(1)} %shard_map.102.refs_2_.after.refs_0_), channel_id=1, source_target_pairs={{0,128},{2,130},{4,132},{6,134},{8,136},{10,138},{12,140},{14,142}... | collective-permute-start | bytes 55304 | tf_op jit(solution)/shard_map/ppermute | solution.py:527
  55.7 0.0 collective-permute-start.14
  55.7 1.5 %collective-permute-start.13 = (f32[9,512]{1,0:T(8,128)S(1)}, f32[9,512]{1,0:T(8,128)S(1)}, u32[]{:S(2)}, u32[]{:S(2)}) collective-permute-start(f32[9,512]{1,0:T(8,128)S(1)} %shard_map.102.refs_2_.after.refs_0_), channel_id=1, source_target_pairs={{0,64},{2,66},{4,68},{6,70},{8,72},{10,74},{12,76},{14,78},{16,80}... | collective-permute-start | bytes 55304 | tf_op jit(solution)/shard_map/ppermute | solution.py:527
  57.2 1.2 %shard_map.103 = (f32[256,512]{1,0:T(8,128)S(1)}, bf16[2,256,512]{2,1,0:T(8,128)(2,1)S(1)}) custom-call(bf16[256,512]{1,0:T(8,128)(2,1)S(1)} %get-tuple-element.69.q, bf16[256,512]{1,0:T(8,128)(2,1)S(1)} %collective-permute-done.3.ka.k, bf16[256,512]{1,0:T(8,128)(2,1)S(1)} %collective-permute-done.4.va.v, bf16[256,512]{1,0:T(8,128)(2,1)S(1)} %get-tuple-element.86.datt, ...), custom_call_target="tpu_custom_call" | custom-call | flops 15000000512 | bytes 15000000 | tf_op jit(solution)/shard_map/pallas_call | solution.py:432
  58.3 0.0 copy-done.5
  58.4 0.0 copy-done.7
  58.4 0.1 copy-done.9
  58.5 1.5 %shard_map.104 = (f32[2,256,512]{2,1,0:T(8,128)S(1)}, f32[256,1024]{1,0:T(8,128)S(1)}) custom-call(bf16[256,512]{1,0:T(8,128)(2,1)S(1)} %get-tuple-element.69.q, bf16[256,512]{1,0:T(8,128)(2,1)S(1)} %copy-done.7, bf16[256,512]{1,0:T(8,128)(2,1)S(1)} %copy-done.9, bf16[256,512]{1,0:T(8,128)(2,1)S(1)} %get-tuple-element.86.datt, ...), custom_call_target="tpu_custom_call" | custom-call | flops 20000000000 | bytes 20000000 | tf_op jit(solution)/shard_map/pallas_call | solution.py:432
  60.0 0.1 collective-permute-start.11
  60.1 0.0 collective-permute-done.15.refs_3_
  60.1 1.6 %collective-permute-done.14.refs_2_ = f32[9,512]{1,0:T(8,128)S(1)} collective-permute-done((f32[9,512]{1,0:T(8,128)S(1)}, f32[9,512]{1,0:T(8,128)S(1)}, u32[]{:S(2)}, u32[]{:S(2)}) %collective-permute-start.14) | collective-permute-done | bytes 18464 | tf_op jit(solution)/shard_map/ppermute | solution.py:527
  61.7 0.0 collective-permute-done.13.refs_1_
  61.7 5.4 %collective-permute-start.19 = (f32[9,512]{1,0:T(8,128)S(1)}, f32[9,512]{1,0:T(8,128)S(1)}, u32[]{:S(2)}, u32[]{:S(2)}) collective-permute-start(f32[9,512]{1,0:T(8,128)S(1)} %shard_map.105.after.refs_0_), channel_id=1, source_target_pairs={{0,48},{2,50},{4,52},{6,54},{8,56},{10,58},{12,60},{14,62},{16,32}... | collective-permute-start | bytes 55304 | tf_op jit(solution)/shard_map/ppermute | solution.py:527
  67.2 0.0 collective-permute-start.18
  67.2 0.7 collective-permute-start.17
  67.8 0.0 collective-permute-done.12.got_b
  67.8 0.0 collective-permute-done.11.got_a
  67.8 0.9 %shard_map.106 = (bf16[256,640]{1,0:T(8,128)(2,1)S(1)}, f32[256,512]{1,0:T(8,128)S(1)}, f32[256,128]{1,0:T(8,128)S(1)}) custom-call(f32[256,512]{1,0:T(8,128)S(1)} %get-tuple-element.83.n1o, f32[256,512]{1,0:T(8,128)S(1)} %get-tuple-element.85.n1p, f32[2,256,512]{2,1,0:T(8,128)S(1)} %get-tuple-element.95.dkv, ...), custom_call_target="tpu_custom_call" | custom-call | flops 15000000512 | bytes 15000000 | tf_op jit(solution)/shard_map/pallas_call | solution.py:432
  68.7 0.9 %collective-permute-start.16 = (bf16[256,640]{1,0:T(8,128)(2,1)S(1)}, bf16[256,640]{1,0:T(8,128)(2,1)S(1)}, u32[]{:S(2)}, u32[]{:S(2)}) collective-permute-start(bf16[256,640]{1,0:T(8,128)(2,1)S(1)} %get-tuple-element.101), channel_id=1, source_target_pairs={{0,1},{1,0},{2,3},{3,2},{4,5},{5,4},{6,7},{7,6},{8,9},{9,8},{10,11... | collective-permute-start | bytes 983048 | tf_op jit(solution)/shard_map/ppermute | solution.py:449
  69.6 0.0 collective-permute-done.19.refs_3_
  69.6 1.5 %collective-permute-done.18.refs_2_ = f32[9,512]{1,0:T(8,128)S(1)} collective-permute-done((f32[9,512]{1,0:T(8,128)S(1)}, f32[9,512]{1,0:T(8,128)S(1)}, u32[]{:S(2)}, u32[]{:S(2)}) %collective-permute-start.18) | collective-permute-done | bytes 18464 | tf_op jit(solution)/shard_map/ppermute | solution.py:527
  71.1 0.3 collective-permute-done.17.refs_1_
  71.4 0.1 collective-permute-start.22
  71.5 1.7 %collective-permute-start.21 = (f32[9,512]{1,0:T(8,128)S(1)}, f32[9,512]{1,0:T(8,128)S(1)}, u32[]{:S(2)}, u32[]{:S(2)}) collective-permute-start(f32[9,512]{1,0:T(8,128)S(1)} %shard_map.107.row), channel_id=1, source_target_pairs={{0,12},{2,14},{4,8},{6,10},{8,4},{10,6},{12,0},{14,2},{16,28},{18,... | collective-permute-start | bytes 55304 | tf_op jit(solution)/shard_map/ppermute | solution.py:527
  73.2 1.8 %collective-permute-start.20 = (f32[9,512]{1,0:T(8,128)S(1)}, f32[9,512]{1,0:T(8,128)S(1)}, u32[]{:S(2)}, u32[]{:S(2)}) collective-permute-start(f32[9,512]{1,0:T(8,128)S(1)} %shard_map.107.row), channel_id=1, source_target_pairs={{0,4},{2,6},{4,0},{6,2},{8,12},{10,14},{12,8},{14,10},{16,20},{18,... | collective-permute-start | bytes 55304 | tf_op jit(solution)/shard_map/ppermute | solution.py:527
  75.0 2.0 %collective-permute-done.22.three = f32[9,512]{1,0:T(8,128)S(1)} collective-permute-done((f32[9,512]{1,0:T(8,128)S(1)}, f32[9,512]{1,0:T(8,128)S(1)}, u32[]{:S(2)}, u32[]{:S(2)}) %collective-permute-start.22) | collective-permute-done | bytes 18464 | tf_op jit(solution)/shard_map/ppermute | solution.py:527
  77.0 0.0 collective-permute-done.21.two
  77.1 0.0 collective-permute-done.20.one
  77.1 0.3 collective-permute-done.16.got
  77.4 1.0 %shard_map.108 = (bf16[256,512]{1,0:T(8,128)(2,1)}, f32[9,512]{1,0:T(8,128)}) custom-call(f32[256,512]{1,0:T(8,128)S(1)} %get-tuple-element.83.n1o, f32[256,128]{1,0:T(8,128)S(1)} %get-tuple-element.84.rstd, f32[256,512]{1,0:T(8,128)S(1)} %get-tuple-element.99.keep, f32[256,128]{1,0:T(8,128)S(1)} %get-tuple-element.100.stat, ...), custom_call_target="tpu_custom_call" | custom-call | flops 10000000000 | bytes 10000000 | tf_op jit(solution)/shard_map/pallas_call | solution.py:432
  (17 shorter events, 0.1 us)
Async XLA Ops:
  0.6 12.9 %collective-permute-start = (bf16[256,512]{1,0:T(8,128)(2,1)}, bf16[256,512]{1,0:T(8,128)(2,1)S(1)}, u32[]{:S(2)}, u32[]{:S(2)}) collective-permute-start(bf16[256,512]{1,0:T(8,128)(2,1)} %refs_4_.1), channel_id=1, source_target_pairs={{0,1},{1,0},{2,3},{3,2},{4,5},{5,4},{6,7},{7,6},{8,9},{9,8},{10,11... | collective-permute-start | bytes 786440 | tf_op jit(solution)/shard_map/ppermute | solution.py:449
  2.8 17.3 %collective-permute-start.2 = (bf16[256,512]{1,0:T(8,128)(2,1)}, bf16[256,512]{1,0:T(8,128)(2,1)S(1)}, u32[]{:S(2)}, u32[]{:S(2)}) collective-permute-start(bf16[256,512]{1,0:T(8,128)(2,1)} %refs_4_.1), channel_id=1, source_target_pairs={{2,5},{3,4},{6,9},{7,8},{10,13},{11,12},{14,17},{15,16},{18,21},{1... | collective-permute-start | bytes 786440 | tf_op jit(solution)/shard_map/ppermute | solution.py:463
  6.2 13.9 %collective-permute-start.1 = (bf16[256,512]{1,0:T(8,128)(2,1)}, bf16[256,512]{1,0:T(8,128)(2,1)S(1)}, u32[]{:S(2)}, u32[]{:S(2)}) collective-permute-start(bf16[256,512]{1,0:T(8,128)(2,1)} %refs_4_.1), channel_id=1, source_target_pairs={{2,4},{6,8},{10,12},{14,16},{18,20},{22,24},{26,28},{30,32},{34,36... | collective-permute-start | bytes 786440 | tf_op jit(solution)/shard_map/ppermute | solution.py:456
  13.5 1.2 %copy-start.4 = (bf16[1024,512]{1,0:T(8,128)(2,1)}, bf16[1024,512]{1,0:T(8,128)(2,1)S(1)}, u32[]{:S(2)}) copy-start(bf16[1024,512]{1,0:T(8,128)(2,1)S(1)} %get-tuple-element.66.wq) | copy-start | bytes 3145732
  13.5 6.7 %copy-start = (bf16[1024,512]{1,0:T(8,128)(2,1)}, bf16[1024,512]{1,0:T(8,128)(2,1)S(1)}, u32[]{:S(2)}) copy-start(bf16[1024,512]{1,0:T(8,128)(2,1)S(1)} %get-tuple-element.63.wk) | copy-start | bytes 3145732
  13.5 6.7 %copy-start.2 = (bf16[1024,512]{1,0:T(8,128)(2,1)}, bf16[1024,512]{1,0:T(8,128)(2,1)S(1)}, u32[]{:S(2)}) copy-start(bf16[1024,512]{1,0:T(8,128)(2,1)S(1)} %get-tuple-element.64.wv) | copy-start | bytes 3145732
  14.7 10.7 %copy-start.6 = (bf16[256,512]{1,0:T(8,128)(2,1)}, bf16[256,512]{1,0:T(8,128)(2,1)S(1)}, u32[]{:S(2)}) copy-start(bf16[256,512]{1,0:T(8,128)(2,1)S(1)} %get-tuple-element.70.k) | copy-start | bytes 786436
  14.7 10.7 %copy-start.8 = (bf16[256,512]{1,0:T(8,128)(2,1)}, bf16[256,512]{1,0:T(8,128)(2,1)S(1)}, u32[]{:S(2)}) copy-start(bf16[256,512]{1,0:T(8,128)(2,1)S(1)} %get-tuple-element.71.v) | copy-start | bytes 786436
  14.7 5.5 %collective-permute-start.3 = (bf16[256,512]{1,0:T(8,128)(2,1)S(1)}, bf16[256,512]{1,0:T(8,128)(2,1)S(1)}, u32[]{:S(2)}, u32[]{:S(2)}) collective-permute-start(bf16[256,512]{1,0:T(8,128)(2,1)S(1)} %get-tuple-element.70.k), channel_id=1, source_target_pairs={{0,2},{2,0},{4,6},{6,4},{8,10},{10,8},{12,14},{14,12},{16,18},{18,... | collective-permute-start | bytes 786440 | tf_op jit(solution)/shard_map/ppermute | solution.py:452
  14.8 5.4 %collective-permute-start.4 = (bf16[256,512]{1,0:T(8,128)(2,1)S(1)}, bf16[256,512]{1,0:T(8,128)(2,1)S(1)}, u32[]{:S(2)}, u32[]{:S(2)}) collective-permute-start(bf16[256,512]{1,0:T(8,128)(2,1)S(1)} %get-tuple-element.71.v), channel_id=1, source_target_pairs={{0,2},{2,0},{4,6},{6,4},{8,10},{10,8},{12,14},{14,12},{16,18},{18,... | collective-permute-start | bytes 786440 | tf_op jit(solution)/shard_map/ppermute | solution.py:452
  15.3 13.5 %collective-permute-start.7 = (bf16[304,512]{1,0:T(8,128)(2,1)S(1)}, bf16[304,512]{1,0:T(8,128)(2,1)S(1)}, u32[]{:S(2)}, u32[]{:S(2)}) collective-permute-start(bf16[304,512]{1,0:T(8,128)(2,1)S(1)} %get-tuple-element.77), channel_id=1, source_target_pairs={{0,1},{1,0},{2,3},{3,2},{4,5},{5,4},{6,7},{7,6},{8,9},{9,8},{10,11... | collective-permute-start | bytes 933896 | tf_op jit(solution)/shard_map/ppermute | solution.py:449
  22.9 6.8 %collective-permute-start.5 = (bf16[64,1024]{1,0:T(8,128)(2,1)S(1)}, bf16[64,1024]{1,0:T(8,128)(2,1)S(1)}, u32[]{:S(2)}, u32[]{:S(2)}) collective-permute-start(bf16[64,1024]{1,0:T(8,128)(2,1)S(1)} %get-tuple-element.72.part.rim), channel_id=1, source_target_pairs={{0,1},{1,0},{2,3},{3,2},{4,5},{5,4},{6,7},{7,6},{8,9},{9,8},{10,11... | collective-permute-start | bytes 393224 | tf_op jit(solution)/shard_map/ppermute | solution.py:449
  27.6 12.8 %collective-permute-start.6 = (bf16[192,1024]{1,0:T(8,128)(2,1)S(1)}, bf16[192,1024]{1,0:T(8,128)(2,1)S(1)}, u32[]{:S(2)}, u32[]{:S(2)}) collective-permute-start(bf16[192,1024]{1,0:T(8,128)(2,1)S(1)} %get-tuple-element.75.mid), channel_id=1, source_target_pairs={{0,1},{1,0},{2,3},{3,2},{4,5},{5,4},{6,7},{7,6},{8,9},{9,8},{10,11... | collective-permute-start | bytes 1179656 | tf_op jit(solution)/shard_map/ppermute | solution.py:449
  29.7 3.3 %collective-permute-start.8 = (bf16[48,1024]{1,0:T(8,128)(2,1)S(1)}, bf16[48,1024]{1,0:T(8,128)(2,1)S(1)}, u32[]{:S(2)}, u32[]{:S(2)}) collective-permute-start(bf16[48,1024]{1,0:T(8,128)(2,1)S(1)} %get-tuple-element.78), channel_id=1, source_target_pairs={{0,2},{2,0},{4,6},{6,4},{8,10},{10,8},{12,14},{14,12},{16,18},{18,... | collective-permute-start | bytes 294920 | tf_op jit(solution)/shard_map/ppermute | solution.py:452
  29.8 10.6 %collective-permute-start.9 = (bf16[48,1024]{1,0:T(8,128)(2,1)S(1)}, bf16[48,1024]{1,0:T(8,128)(2,1)S(1)}, u32[]{:S(2)}, u32[]{:S(2)}) collective-permute-start(bf16[48,1024]{1,0:T(8,128)(2,1)S(1)} %get-tuple-element.79), channel_id=1, source_target_pairs={{2,4},{6,8},{10,12},{14,16},{18,20},{22,24},{26,28},{30,32},{34,36... | collective-permute-start | bytes 294920 | tf_op jit(solution)/shard_map/ppermute | solution.py:456
  44.4 4.0 %collective-permute-start.10 = (f32[9,512]{1,0:T(8,128)S(1)}, f32[9,512]{1,0:T(8,128)S(1)}, u32[]{:S(2)}, u32[]{:S(2)}) collective-permute-start(f32[9,512]{1,0:T(8,128)S(1)} %get-tuple-element.93.refs_0_), channel_id=1, source_target_pairs={{0,2},{2,0},{4,6},{6,4},{8,10},{10,8},{12,14},{14,12},{16,18},{18,... | collective-permute-start | bytes 55304 | tf_op jit(solution)/shard_map/ppermute | solution.py:527
  45.7 22.1 %collective-permute-start.12 = (bf16[2,256,512]{2,1,0:T(8,128)(2,1)S(1)}, bf16[2,256,512]{2,1,0:T(8,128)(2,1)S(1)}, u32[]{:S(2)}, u32[]{:S(2)}) collective-permute-start(bf16[2,256,512]{2,1,0:T(8,128)(2,1)S(1)} %get-tuple-element.97), channel_id=1, source_target_pairs={{2,4},{6,8},{10,12},{14,16},{18,20},{22,24},{26,28},{30,32},{34,36... | collective-permute-start | bytes 1572872 | tf_op jit(solution)/shard_map/ppermute | solution.py:456
  48.4 11.7 %collective-permute-start.15 = (f32[9,512]{1,0:T(8,128)S(1)}, f32[9,512]{1,0:T(8,128)S(1)}, u32[]{:S(2)}, u32[]{:S(2)}) collective-permute-start(f32[9,512]{1,0:T(8,128)S(1)} %shard_map.102.refs_2_.after.refs_0_), channel_id=1, source_target_pairs={{0,128},{2,130},{4,132},{6,134},{8,136},{10,138},{12,140},{14,142}... | collective-permute-start | bytes 55304 | tf_op jit(solution)/shard_map/ppermute | solution.py:527
  55.7 6.0 %collective-permute-start.14 = (f32[9,512]{1,0:T(8,128)S(1)}, f32[9,512]{1,0:T(8,128)S(1)}, u32[]{:S(2)}, u32[]{:S(2)}) collective-permute-start(f32[9,512]{1,0:T(8,128)S(1)} %shard_map.102.refs_2_.after.refs_0_), channel_id=1, source_target_pairs={{0,192},{2,194},{4,196},{6,198},{8,200},{10,202},{12,204},{14,206}... | collective-permute-start | bytes 55304 | tf_op jit(solution)/shard_map/ppermute | solution.py:527
  55.7 6.0 %collective-permute-start.13 = (f32[9,512]{1,0:T(8,128)S(1)}, f32[9,512]{1,0:T(8,128)S(1)}, u32[]{:S(2)}, u32[]{:S(2)}) collective-permute-start(f32[9,512]{1,0:T(8,128)S(1)} %shard_map.102.refs_2_.after.refs_0_), channel_id=1, source_target_pairs={{0,64},{2,66},{4,68},{6,70},{8,72},{10,74},{12,76},{14,78},{16,80}... | collective-permute-start | bytes 55304 | tf_op jit(solution)/shard_map/ppermute | solution.py:527
  57.1 1.2 %copy-start.5 = (bf16[1024,512]{1,0:T(8,128)(2,1)S(1)}, bf16[1024,512]{1,0:T(8,128)(2,1)}, u32[]{:S(2)}) copy-start(bf16[1024,512]{1,0:T(8,128)(2,1)} %copy-done.4) | copy-start | bytes 3145732
  57.2 1.3 %copy-start.7 = (bf16[256,512]{1,0:T(8,128)(2,1)S(1)}, bf16[256,512]{1,0:T(8,128)(2,1)}, u32[]{:S(2)}) copy-start(bf16[256,512]{1,0:T(8,128)(2,1)} %copy-done.6) | copy-start | bytes 786436
  57.2 1.3 %copy-start.9 = (bf16[256,512]{1,0:T(8,128)(2,1)S(1)}, bf16[256,512]{1,0:T(8,128)(2,1)}, u32[]{:S(2)}) copy-start(bf16[256,512]{1,0:T(8,128)(2,1)} %copy-done.8) | copy-start | bytes 786436
  60.0 7.9 %copy-start.1 = (bf16[1024,512]{1,0:T(8,128)(2,1)S(1)}, bf16[1024,512]{1,0:T(8,128)(2,1)}, u32[]{:S(2)}) copy-start(bf16[1024,512]{1,0:T(8,128)(2,1)} %copy-done) | copy-start | bytes 3145732
  60.0 7.9 %copy-start.3 = (bf16[1024,512]{1,0:T(8,128)(2,1)S(1)}, bf16[1024,512]{1,0:T(8,128)(2,1)}, u32[]{:S(2)}) copy-start(bf16[1024,512]{1,0:T(8,128)(2,1)} %copy-done.2) | copy-start | bytes 3145732
  60.0 7.8 %collective-permute-start.11 = (bf16[2,256,512]{2,1,0:T(8,128)(2,1)S(1)}, bf16[2,256,512]{2,1,0:T(8,128)(2,1)S(1)}, u32[]{:S(2)}, u32[]{:S(2)}) collective-permute-start(bf16[2,256,512]{2,1,0:T(8,128)(2,1)S(1)} %get-tuple-element.96), channel_id=1, source_target_pairs={{0,2},{2,0},{4,6},{6,4},{8,10},{10,8},{12,14},{14,12},{16,18},{18,... | collective-permute-start | bytes 1572872 | tf_op jit(solution)/shard_map/ppermute | solution.py:452
  61.7 7.9 %collective-permute-start.19 = (f32[9,512]{1,0:T(8,128)S(1)}, f32[9,512]{1,0:T(8,128)S(1)}, u32[]{:S(2)}, u32[]{:S(2)}) collective-permute-start(f32[9,512]{1,0:T(8,128)S(1)} %shard_map.105.after.refs_0_), channel_id=1, source_target_pairs={{0,48},{2,50},{4,52},{6,54},{8,56},{10,58},{12,60},{14,62},{16,32}... | collective-permute-start | bytes 55304 | tf_op jit(solution)/shard_map/ppermute | solution.py:527
  67.2 3.9 %collective-permute-start.18 = (f32[9,512]{1,0:T(8,128)S(1)}, f32[9,512]{1,0:T(8,128)S(1)}, u32[]{:S(2)}, u32[]{:S(2)}) collective-permute-start(f32[9,512]{1,0:T(8,128)S(1)} %shard_map.105.after.refs_0_), channel_id=1, source_target_pairs={{0,32},{2,34},{4,36},{6,38},{8,40},{10,42},{12,44},{14,46},{16,48}... | collective-permute-start | bytes 55304 | tf_op jit(solution)/shard_map/ppermute | solution.py:527
  67.2 4.3 %collective-permute-start.17 = (f32[9,512]{1,0:T(8,128)S(1)}, f32[9,512]{1,0:T(8,128)S(1)}, u32[]{:S(2)}, u32[]{:S(2)}) collective-permute-start(f32[9,512]{1,0:T(8,128)S(1)} %shard_map.105.after.refs_0_), channel_id=1, source_target_pairs={{0,16},{2,18},{4,20},{6,22},{8,24},{10,26},{12,28},{14,30},{16,0},... | collective-permute-start | bytes 55304 | tf_op jit(solution)/shard_map/ppermute | solution.py:527
  68.7 8.7 %collective-permute-start.16 = (bf16[256,640]{1,0:T(8,128)(2,1)S(1)}, bf16[256,640]{1,0:T(8,128)(2,1)S(1)}, u32[]{:S(2)}, u32[]{:S(2)}) collective-permute-start(bf16[256,640]{1,0:T(8,128)(2,1)S(1)} %get-tuple-element.101), channel_id=1, source_target_pairs={{0,1},{1,0},{2,3},{3,2},{4,5},{5,4},{6,7},{7,6},{8,9},{9,8},{10,11... | collective-permute-start | bytes 983048 | tf_op jit(solution)/shard_map/ppermute | solution.py:449
  71.4 5.6 %collective-permute-start.22 = (f32[9,512]{1,0:T(8,128)S(1)}, f32[9,512]{1,0:T(8,128)S(1)}, u32[]{:S(2)}, u32[]{:S(2)}) collective-permute-start(f32[9,512]{1,0:T(8,128)S(1)} %shard_map.107.row), channel_id=1, source_target_pairs={{0,8},{2,10},{4,12},{6,14},{8,0},{10,2},{12,4},{14,6},{16,24},{18,... | collective-permute-start | bytes 55304 | tf_op jit(solution)/shard_map/ppermute | solution.py:527
  71.5 5.6 %collective-permute-start.21 = (f32[9,512]{1,0:T(8,128)S(1)}, f32[9,512]{1,0:T(8,128)S(1)}, u32[]{:S(2)}, u32[]{:S(2)}) collective-permute-start(f32[9,512]{1,0:T(8,128)S(1)} %shard_map.107.row), channel_id=1, source_target_pairs={{0,12},{2,14},{4,8},{6,10},{8,4},{10,6},{12,0},{14,2},{16,28},{18,... | collective-permute-start | bytes 55304 | tf_op jit(solution)/shard_map/ppermute | solution.py:527
  73.2 3.9 %collective-permute-start.20 = (f32[9,512]{1,0:T(8,128)S(1)}, f32[9,512]{1,0:T(8,128)S(1)}, u32[]{:S(2)}, u32[]{:S(2)}) collective-permute-start(f32[9,512]{1,0:T(8,128)S(1)} %shard_map.107.row), channel_id=1, source_target_pairs={{0,4},{2,6},{4,0},{6,2},{8,12},{10,14},{12,8},{14,10},{16,20},{18,... | collective-permute-start | bytes 55304 | tf_op jit(solution)/shard_map/ppermute | solution.py:527
